TPU v7x, 256 devices: a whole 4x4x8 slice. The times are simulated.
256 devices in a mesh: date: 16 (over z, core), strip: 16 (over y, x).
Axes of the slice: x: 4, y: 4, z: 8, core: 2. Of those that a mesh axis runs over, the one named last changes fastest.
Arguments:
- images: bfloat16 [2, 64, 1280, 5120], P(None, 'date', 'strip'), as said below
- date_pairs: int32 [128, 2], replicated, may hold values from 0 to 63, as said below
- assignment: int32 [128], replicated, may hold values from 0 to 255, as said below
Outputs:
- coherence: float32 [2, 256, 65536], P(None, 'date', 'strip')
- date_sums: float32 [2, 64, 65536], P(None, 'date', 'strip')
Inputs may be any that keep to these rules, and one draw needn't show every extreme that they name: `date_pairs`: each row holds two different dates at most 4 apart, and no ordered pair of dates is listed twice. Rows whose first date lies in one aligned block of 4 dates number at most 16, and exactly that many in some block. `assignment`: rows are distinct. The rows r with r // 16 equal to o belong to owner o; within them, consecutive groups of 1 row hold, in order, only pairs whose first date lies in the 0th, 1st, ... aligned block of 4 dates. In some owner's rows every group is full. `images`: values stay finite and of moderate size; every pixel is nonzero with probability one.
All inputs are finite; a program needn't handle non-finite values.
Results may differ from a plain program's by a relative error of at most 0.00084.
Values may be sent and summed in bfloat16 or wider, within the bound.
No kernel may reach another device: no remote copies, remote signals or barrier semaphores. Data moves between devices by JAX's collectives and lax.ppermute only.
A program may use at most 256 MiB of HBM per device.

v0:
```python
import jax
import jax.numpy as jnp
from jax import lax
from jax.sharding import PartitionSpec as P

PAIR_DEV = 8
BASE = 4
ALOOK = 5
RLOOK = 20


eps_power = 1e-06


def extended_2(block, sides, width):
    for axis, dim in sides:
        count = lax.axis_size(axis)
        forward = [(i, i + 1) for i in range(count - 1)]
        backward = [(target, source) for source, target in forward]
        low = lax.ppermute(
            lax.slice_in_dim(block, block.shape[dim] - width, None, axis=dim), axis, forward
        )
        high = lax.ppermute(lax.slice_in_dim(block, 0, width, axis=dim), axis, backward)
        block = jnp.concatenate([low, block, high], axis=dim)
    return block


def passed_along(value, axis, steps):
    count = lax.axis_size(axis)
    first, last = (max(0, -steps), min(count, count - steps))
    return lax.ppermute(value, axis, [(source, source + steps) for source in range(first, last)])


def range_looks(pixels, look_matrix):
    summed = jnp.einsum("...ar,rl->...al", pixels, look_matrix, preferred_element_type=jnp.float32)
    shaped = summed.reshape(
        summed.shape[:-2] + (summed.shape[-2] // ALOOK, ALOOK, summed.shape[-1])
    )
    return jnp.sum(shaped, axis=-2)


def on_device(images, date_pairs, assignment):
    owners = lax.axis_size("date")
    myself = lax.axis_index("date")
    local_dates = images.shape[1]
    columns = images.shape[3]
    per_owner = 2 * PAIR_DEV // owners
    slot_count = 2 * PAIR_DEV
    span = local_dates + 2 * BASE
    extended = extended_2(images, (("date", 1),), BASE)
    look_matrix = (
        jnp.arange(columns)[:, None] // RLOOK == jnp.arange(columns // RLOOK)[None, :]
    ).astype(jnp.bfloat16)
    power = (
        jnp.square(extended[0].astype(jnp.float32)) + jnp.square(extended[1].astype(jnp.float32))
    ).astype(jnp.bfloat16)
    power_looked = range_looks(power, look_matrix)
    look_az = power_looked.shape[1]
    look_rg = power_looked.shape[2]
    first_date = date_pairs[:, 0]
    second_date = date_pairs[:, 1]
    mine = first_date // local_dates == myself
    send_slot = assignment // slot_count * per_owner + assignment % per_owner
    matches = (send_slot[None, :] == jnp.arange(slot_count)[:, None]) & mine[None, :]
    present = jnp.any(matches, axis=1)
    anchor = myself * local_dates - BASE
    first_local = jnp.where(
        present, jnp.sum(jnp.where(matches, first_date[None, :], 0), axis=1) - anchor, BASE
    )
    second_local = jnp.where(
        present, jnp.sum(jnp.where(matches, second_date[None, :], 0), axis=1) - anchor, BASE
    )
    block_size = 8
    first_groups = first_local.reshape(slot_count // block_size, block_size)
    second_groups = second_local.reshape(slot_count // block_size, block_size)

    def form(indices):
        lead_index, trail_index = indices
        front_images = jnp.take(extended, lead_index, axis=1).astype(jnp.float32)
        back_images = jnp.take(extended, trail_index, axis=1).astype(jnp.float32)
        cross_real = front_images[0] * back_images[0] + front_images[1] * back_images[1]
        cross_imag = front_images[1] * back_images[0] - front_images[0] * back_images[1]
        cross = jnp.stack([cross_real, cross_imag]).astype(jnp.bfloat16)
        return range_looks(cross, look_matrix)

    looked = lax.map(form, (first_groups, second_groups))
    cross_looked = jnp.moveaxis(looked, 0, 1).reshape(2 * slot_count, look_az, look_rg)
    stacked = jnp.concatenate([cross_looked, power_looked], axis=0)
    padded = extended_2(stacked, (("strip", 1),), 1)
    smoothed = padded[:, :-2] + 2.0 * padded[:, 1:-1] + padded[:, 2:]
    cross_smooth = smoothed[: 2 * slot_count].reshape(2, slot_count, look_az, look_rg)
    power_smooth = smoothed[2 * slot_count :]
    power_first = jnp.take(power_smooth, first_local, axis=0)
    power_second = jnp.take(power_smooth, second_local, axis=0)
    scale = lax.rsqrt(power_first * power_second + eps_power) * present[:, None, None].astype(
        jnp.float32
    )
    coherent = cross_smooth * scale[None]
    cell_count = look_az * look_rg
    outgoing = coherent.reshape(2, owners, per_owner, cell_count)
    arrived = lax.all_to_all(outgoing, "date", split_axis=1, concat_axis=1, tiled=True)
    coherence = arrived.reshape(2, owners * per_owner, cell_count)
    flat = coherent.reshape(2, slot_count, cell_count)
    positions = jnp.arange(span)
    lead_hot = ((first_local[:, None] == positions[None, :]) & present[:, None]).astype(jnp.float32)
    trail_hot = ((second_local[:, None] == positions[None, :]) & present[:, None]).astype(
        jnp.float32
    )
    accum_real = jnp.einsum(
        "se,sx->ex", lead_hot + trail_hot, flat[0], precision=lax.Precision.HIGHEST
    )
    accum_imag = jnp.einsum(
        "se,sx->ex", lead_hot - trail_hot, flat[1], precision=lax.Precision.HIGHEST
    )
    accum = jnp.stack([accum_real, accum_imag])
    from_below = passed_along(accum[:, span - BASE :], "date", 1)
    from_above = passed_along(accum[:, :BASE], "date", -1)
    totals = accum[:, BASE : BASE + local_dates]
    totals = totals.at[:, :BASE].add(from_below)
    totals = totals.at[:, local_dates - BASE :].add(from_above)
    return (coherence, totals)


def solution(mesh):
    return jax.shard_map(
        on_device,
        mesh=mesh,
        in_specs=(P(None, "date", "strip", None), P(), P()),
        out_specs=(P(None, "date", "strip"), P(None, "date", "strip")),
        check_vma=False,
    )
```

profile of v0, /device:TPU:9, one launch (start us, length us, event | category | flops | bytes accessed | tf_op | source)
XLA Modules:
  0.0 322.3 jit_solution(13346363931780721209)
XLA Ops:
  0.6 4.2 %collective-permute-start = (bf16[2,4,80,5120]{3,2,1,0:T(8,128)(2,1)}, bf16[2,4,80,5120]{3,2,1,0:T(8,128)(2,1)}, u32[]{:S(2)}, u32[]{:S(2)}) collective-permute-start(bf16[2,4,80,5120]{3,2,1,0:T(8,128)(2,1)} %param.17), channel_id=1, source_target_pairs={{0,16},{16,32},{32,48},{48,64},{64,80},{80,96},{96,112},{112,128},... | collective-permute-start | bytes 19660808 | tf_op jit(solution)/shard_map/ppermute | solution.py:20
  4.9 3.0 collective-permute-start.1
  7.9 0.7 and_select_fusion.1
  8.5 0.7 fusion.46
  9.4 0.8 slice_bitcast_fusion.1
  10.2 0.6 compare_and_fusion.2
  11.0 0.6 compare_select_fusion.2
  11.6 0.6 pad_clamp_fusion.3
  12.2 63.7 %collective-permute-done = bf16[2,4,80,5120]{3,2,1,0:T(8,128)(2,1)} collective-permute-done((bf16[2,4,80,5120]{3,2,1,0:T(8,128)(2,1)}, bf16[2,4,80,5120]{3,2,1,0:T(8,128)(2,1)}, u32[]{:S(2)}, u32[]{:S(2)}) %collective-permute-start) | collective-permute-done | bytes 6553632 | tf_op jit(solution)/shard_map/ppermute | solution.py:20
  75.9 6.0 %constant_dynamic-update-slice_fusion.2 = bf16[2,12,80,5120]{3,2,1,0:T(8,128)(2,1)} fusion(bf16[2,4,80,5120]{3,2,1,0:T(8,128)(2,1)} %collective-permute-done), kind=kLoop, calls=%fused_computation.83 | loop fusion | bytes 13107200
  82.0 3.4 %constant_dynamic-update-slice_fusion.1 = bf16[2,12,80,5120]{3,2,1,0:T(8,128)(2,1)} fusion(bf16[2,12,80,5120]{3,2,1,0:T(8,128)(2,1)} %constant_dynamic-update-slice_fusion.2, bf16[2,4,80,5120]{3,2,1,0:T(8,128)(2,1)S(1)} %bitcast.69), kind=kLoop, calls=%fused_computation.82 | loop fusion | bytes 13107200
  85.4 6.0 %constant_dynamic-update-slice_fusion = bf16[2,12,80,5120]{3,2,1,0:T(8,128)(2,1)} fusion(bf16[2,12,80,5120]{3,2,1,0:T(8,128)(2,1)} %constant_dynamic-update-slice_fusion.1, bf16[2,4,80,5120]{3,2,1,0:T(8,128)(2,1)} %collective-permute-done.1), kind=kLoop, calls=%fused_computation.81 | loop fusion | bytes 13107200 | tf_op jit(solution)/shard_map/concatenate | solution.py:24
  91.4 12.9 %add_convert_fusion.1 = bf16[1,12,80,5120]{3,2,1,0:T(8,128)(2,1)} fusion(bf16[2,12,80,5120]{3,2,1,0:T(8,128)(2,1)} %constant_dynamic-update-slice_fusion), kind=kLoop, calls=%fused_computation.31 | loop fusion | flops 29491200 | bytes 29491200 | tf_op jit(solution)/shard_map/convert_element_type | solution.py:56
  104.3 154.9 %while.15 = (s32[]{:T(128)}, f32[2,2,8,16,256]{4,3,2,0,1:T(8,128)S(1)}, s32[2,8]{1,0:T(2,128)S(1)}, bf16[2,12,80,5120]{3,2,1,0:T(8,128)(2,1)}, s32[2,8]{1,0:T(2,...) while((s32[]{:T(128)}, f32[2,2,8,16,256]{4,3,2,0,1:T(8,128)S(1)}, s32[2,8]{1,0:T(2,128)S(1)}, ...), condition=%wide.region_5.7_spmd.clone, body=%wide.region_3.6_spmd.clone.sunk | while | flops 3417311232 | bytes 215773568 | solution.py:86
  104.4 12.8 %gather_fusion.1 = bf16[8,2,80,5120]{3,2,1,0:T(8,128)(2,1)} fusion(bf16[2,12,80,5120]{3,2,1,0:T(8,128)(2,1)} %get-tuple-element.205, s32[1024]{0:T(1024)S(1)} %pad_clamp_fusion.7), kind=kCustom, calls=%fused_computation.clone.clone.1 | custom fusion | bytes 26214432 | tf_op jit(solution)/shard_map/while/body/eval_jaxpr/jit(_take)/gather | solution.py:79
  117.1 14.6 %bitcast_convert_fusion.5 = f32[2,8,80,5120]{3,2,1,0:T(8,128)} fusion(bf16[8,2,80,5120]{3,2,1,0:T(8,128)(2,1)} %gather_fusion.1, pred[8]{0:T(512)(128)(4,1)S(1)} %get-tuple-element.183), kind=kLoop, calls=%fused_computation.10.clone.1 | loop fusion | flops 13107200 | bytes 39321608 | tf_op jit(solution)/shard_map/while/body/eval_jaxpr/convert_element_type | solution.py:79
  131.7 13.1 %gather_fusion = bf16[8,2,80,5120]{3,2,1,0:T(8,128)(2,1)} fusion(bf16[2,12,80,5120]{3,2,1,0:T(8,128)(2,1)} %get-tuple-element.205, s32[1024]{0:T(1024)S(1)} %pad_clamp_fusion.6), kind=kCustom, calls=%fused_computation.2.clone.clone.1 | custom fusion | bytes 26214432 | tf_op jit(solution)/shard_map/while/body/eval_jaxpr/jit(_take)/gather | solution.py:80
  144.8 14.5 %bitcast_convert_fusion.4 = f32[2,8,80,5120]{3,2,1,0:T(8,128)} fusion(bf16[8,2,80,5120]{3,2,1,0:T(8,128)(2,1)} %gather_fusion, pred[8]{0:T(512)(128)(4,1)S(1)} %get-tuple-element.181), kind=kLoop, calls=%fused_computation.9.clone.1 | loop fusion | flops 13107200 | bytes 39321608 | tf_op jit(solution)/shard_map/while/body/eval_jaxpr/convert_element_type | solution.py:80
  159.3 17.7 %add_convert_fusion.3 = (bf16[1,8,80,5120]{3,2,1,0:T(8,128)(2,1)S(1)}, bf16[1,8,80,5120]{3,2,1,0:T(8,128)(2,1)S(1)}) fusion(f32[2,8,80,5120]{3,2,1,0:T(8,128)} %bitcast_convert_fusion.4, f32[2,8,80,5120]{3,2,1,0:T(8,128)} %bitcast_convert_fusion.5), kind=kLoop, calls=%fused_computation.14.clone.1 | loop fusion | flops 26214400 | bytes 65536000 | tf_op jit(solution)/shard_map/convert
  177.0 3.8 %fusion.56 = f32[2,8,80,256]{3,2,1,0:T(8,128)S(1)} fusion(bf16[1,8,80,5120]{3,2,1,0:T(8,128)(2,1)S(1)} %get-tuple-element.184, bf16[1,8,80,5120]{3,2,1,0:T(8,128)(2,1)S(1)} %get-tuple-element.185, s32[5120]{0:T(1024)S(1)} %get-tuple-element.207), kind=kOutput, calls=%fused_computation.5.clone.1 | convolution fusion | flops 3364618240 | bytes 14438400 | tf_op jit(solution)/shard_map/while/body/eval_jaxpr/...ar,rl->...al/dot_general | solution.py:35
  180.8 0.8 copy.58
  181.8 12.9 %gather_fusion.1 = bf16[8,2,80,5120]{3,2,1,0:T(8,128)(2,1)} fusion(bf16[2,12,80,5120]{3,2,1,0:T(8,128)(2,1)} %get-tuple-element.205, s32[1024]{0:T(1024)S(1)} %pad_clamp_fusion.7), kind=kCustom, calls=%fused_computation.clone.clone.1 | custom fusion | bytes 26214432 | tf_op jit(solution)/shard_map/while/body/eval_jaxpr/jit(_take)/gather | solution.py:79
  194.7 14.6 %bitcast_convert_fusion.5 = f32[2,8,80,5120]{3,2,1,0:T(8,128)} fusion(bf16[8,2,80,5120]{3,2,1,0:T(8,128)(2,1)} %gather_fusion.1, pred[8]{0:T(512)(128)(4,1)S(1)} %get-tuple-element.183), kind=kLoop, calls=%fused_computation.10.clone.1 | loop fusion | flops 13107200 | bytes 39321608 | tf_op jit(solution)/shard_map/while/body/eval_jaxpr/convert_element_type | solution.py:79
  209.2 13.0 %gather_fusion = bf16[8,2,80,5120]{3,2,1,0:T(8,128)(2,1)} fusion(bf16[2,12,80,5120]{3,2,1,0:T(8,128)(2,1)} %get-tuple-element.205, s32[1024]{0:T(1024)S(1)} %pad_clamp_fusion.6), kind=kCustom, calls=%fused_computation.2.clone.clone.1 | custom fusion | bytes 26214432 | tf_op jit(solution)/shard_map/while/body/eval_jaxpr/jit(_take)/gather | solution.py:80
  222.2 14.5 %bitcast_convert_fusion.4 = f32[2,8,80,5120]{3,2,1,0:T(8,128)} fusion(bf16[8,2,80,5120]{3,2,1,0:T(8,128)(2,1)} %gather_fusion, pred[8]{0:T(512)(128)(4,1)S(1)} %get-tuple-element.181), kind=kLoop, calls=%fused_computation.9.clone.1 | loop fusion | flops 13107200 | bytes 39321608 | tf_op jit(solution)/shard_map/while/body/eval_jaxpr/convert_element_type | solution.py:80
  236.7 17.7 %add_convert_fusion.3 = (bf16[1,8,80,5120]{3,2,1,0:T(8,128)(2,1)S(1)}, bf16[1,8,80,5120]{3,2,1,0:T(8,128)(2,1)S(1)}) fusion(f32[2,8,80,5120]{3,2,1,0:T(8,128)} %bitcast_convert_fusion.4, f32[2,8,80,5120]{3,2,1,0:T(8,128)} %bitcast_convert_fusion.5), kind=kLoop, calls=%fused_computation.14.clone.1 | loop fusion | flops 26214400 | bytes 65536000 | tf_op jit(solution)/shard_map/convert
  254.5 3.8 %fusion.56 = f32[2,8,80,256]{3,2,1,0:T(8,128)S(1)} fusion(bf16[1,8,80,5120]{3,2,1,0:T(8,128)(2,1)S(1)} %get-tuple-element.184, bf16[1,8,80,5120]{3,2,1,0:T(8,128)(2,1)S(1)} %get-tuple-element.185, s32[5120]{0:T(1024)S(1)} %get-tuple-element.207), kind=kOutput, calls=%fused_computation.5.clone.1 | convolution fusion | flops 3364618240 | bytes 14438400 | tf_op jit(solution)/shard_map/while/body/eval_jaxpr/...ar,rl->...al/dot_general | solution.py:35
  258.2 0.8 copy.58
  259.2 8.6 %copy.31 = bf16[1,12,80,5120]{3,1,2,0:T(8,128)(2,1)S(1)} copy(bf16[1,12,80,5120]{3,2,1,0:T(8,128)(2,1)} %add_convert_fusion.1) | data formatting | bytes 19660800 | tf_op jit(solution)/shard_map/convert_element_type | solution.py:56
  267.9 3.8 %fusion.17 = f32[12,16,256]{2,0,1:T(8,128)S(1)} fusion(bf16[12,16,5,5120]{3,0,2,1:T(8,128)(2,1)S(1)} %bitcast.67, s32[5120]{0:T(1024)S(1)} %get-tuple-element.221), kind=kOutput, calls=%fused_computation.38 | convolution fusion | flops 2518089728 | bytes 10047488 | tf_op jit(solution)/shard_map/...ar,rl->...al/dot_general | solution.py:35
  271.9 3.1 collective-permute-start.2
  275.0 4.3 %collective-permute-start.3 = (f32[44,1,256]{2,1,0:T(1,128)S(1)}, f32[44,1,256]{2,1,0:T(1,128)S(1)}, u32[]{:S(2)}, u32[]{:S(2)}) collective-permute-start(f32[44,1,256]{2,1,0:T(1,128)S(1)} %get-tuple-element.125), channel_id=1, source_target_pairs={{1,0},{2,1},{3,2},{4,3},{5,4},{6,5},{7,6},{8,7},{9,8},{10,9},{11,1... | collective-permute-start | bytes 135176 | tf_op jit(solution)/shard_map/ppermute | solution.py:23
  279.4 1.1 collective-permute-done.3
  280.4 0.3 fusion.22
  280.8 0.7 gather_fusion.2
  281.5 0.6 gather_fusion.3
  282.4 0.2 copy.41
  282.6 0.5 convolution_bitcast_fusion.1
  283.1 0.2 copy.42
  283.3 0.5 convolution_bitcast_fusion
  283.8 6.4 %collective-permute-start.4 = (f32[2,4,4096]{2,1,0:T(4,128)S(1)}, f32[2,4,4096]{2,1,0:T(4,128)S(1)}, u32[]{:S(2)}, u32[]{:S(2)}) collective-permute-start(f32[2,4,4096]{2,1,0:T(4,128)S(1)} %get-tuple-element.126), channel_id=1, source_target_pairs={{0,16},{16,32},{32,48},{48,64},{64,80},{80,96},{96,112},{112,128},... | collective-permute-start | bytes 393224 | tf_op jit(solution)/shard_map/ppermute | solution.py:31
  290.2 1.9 collective-permute-start.5
  292.1 0.2 copy.40
  292.3 1.3 copy_multiply_fusion
  293.6 10.3 %all-to-all-start = ((f32[2,16,1,4096]{3,0,2,1:T(2,128)}), f32[2,16,1,4096]{3,0,2,1:T(2,128)S(1)}, u32[]{:S(2)}, u32[]{:S(2)}) async-start(f32[2,16,1,4096]{3,0,2,1:T(2,128)} %copy_multiply_fusion), calls=%async_computation | async-start | bytes 1048576 | tf_op jit(solution)/shard_map/all_to_all | solution.py:101
  303.9 0.7 fusion.26
  304.6 16.6 %all-to-all-done = f32[2,16,1,4096]{3,0,2,1:T(2,128)S(1)} async-done(((f32[2,16,1,4096]{3,0,2,1:T(2,128)}), f32[2,16,1,4096]{3,0,2,1:T(2,128)S(1)}, u32[]{:S(2)}, u32[]{:S(2)}) %all-to-all-start) | async-done | bytes 524320 | tf_op jit(solution)/shard_map/all_to_all | solution.py:101
  321.2 1.1 copy.34
  (55 shorter events, 1.5 us)
Async XLA Ops:
  0.6 81.3 %slice-start = ((s8[6553600]{0:T(1024)(128)(4,1)}), s8[2359296]{0:T(1024)(128)(4,1)S(1)}, s32[]{:S(2)}) async-start(s8[6553600]{0:T(1024)(128)(4,1)} %bitcast.68), calls=%async_computation.1 | async-start | bytes 4718592
  0.6 75.3 %collective-permute-start = (bf16[2,4,80,5120]{3,2,1,0:T(8,128)(2,1)}, bf16[2,4,80,5120]{3,2,1,0:T(8,128)(2,1)}, u32[]{:S(2)}, u32[]{:S(2)}) collective-permute-start(bf16[2,4,80,5120]{3,2,1,0:T(8,128)(2,1)} %param.17), channel_id=1, source_target_pairs={{0,16},{16,32},{32,48},{48,64},{64,80},{80,96},{96,112},{112,128},... | collective-permute-start | bytes 19660808 | tf_op jit(solution)/shard_map/ppermute | solution.py:20
  4.9 80.5 %collective-permute-start.1 = (bf16[2,4,80,5120]{3,2,1,0:T(8,128)(2,1)}, bf16[2,4,80,5120]{3,2,1,0:T(8,128)(2,1)}, u32[]{:S(2)}, u32[]{:S(2)}) collective-permute-start(bf16[2,4,80,5120]{3,2,1,0:T(8,128)(2,1)} %param.17), channel_id=1, source_target_pairs={{16,0},{32,16},{48,32},{64,48},{80,64},{96,80},{112,96},{128,112},... | collective-permute-start | bytes 19660808 | tf_op jit(solution)/shard_map/ppermute | solution.py:23
  9.4 1.5 copy-start.4
  10.8 0.7 copy-start
  10.8 0.7 copy-start.2
  12.2 69.8 %slice-start.1 = ((s8[6553600]{0:T(1024)(128)(4,1)}), s8[4194304]{0:T(1024)(128)(4,1)S(1)}, s32[]{:S(2)}) async-start(s8[6553600]{0:T(1024)(128)(4,1)} %bitcast.68), calls=%async_computation.2 | async-start | bytes 8388608
  267.8 11.5 %copy-start.6 = (s32[16]{0:T(128)S(1)}, s32[16]{0:T(128)}, u32[]{:S(2)}) copy-start(s32[16]{0:T(128)} %get-tuple-element.135) | copy-start | bytes 196
  267.8 14.3 %copy-start.7 = (pred[16]{0:T(512)(128)(4,1)S(1)}, pred[16]{0:T(512)(128)(4,1)}, u32[]{:S(2)}) copy-start(pred[16]{0:T(512)(128)(4,1)} %get-tuple-element.118) | copy-start | bytes 52
  267.8 14.3 %copy-start.8 = (f32[16]{0:T(128)S(1)}, f32[16]{0:T(128)}, u32[]{:S(2)}) copy-start(f32[16]{0:T(128)} %get-tuple-element.132) | copy-start | bytes 196
  267.8 14.3 %copy-start.9 = (pred[16]{0:T(512)(128)(4,1)S(1)}, pred[16]{0:T(512)(128)(4,1)}, u32[]{:S(2)}) copy-start(pred[16]{0:T(512)(128)(4,1)} %get-tuple-element.133) | copy-start | bytes 52
  267.8 14.8 %copy-start.1 = (s32[16]{0:T(128)S(1)}, s32[16]{0:T(128)}, u32[]{:S(2)}) copy-start(s32[16]{0:T(128)} %copy-done) | copy-start | bytes 196
  267.8 14.8 %copy-start.3 = (s32[16]{0:T(128)S(1)}, s32[16]{0:T(128)}, u32[]{:S(2)}) copy-start(s32[16]{0:T(128)} %copy-done.2) | copy-start | bytes 196
  267.8 14.8 %copy-start.5 = (pred[16]{0:T(512)(128)(4,1)S(1)}, pred[16]{0:T(512)(128)(4,1)}, u32[]{:S(2)}) copy-start(pred[16]{0:T(512)(128)(4,1)} %copy-done.4) | copy-start | bytes 52
  271.9 7.4 %collective-permute-start.2 = (f32[44,1,256]{2,1,0:T(1,128)S(1)}, f32[44,1,256]{2,1,0:T(1,128)S(1)}, u32[]{:S(2)}, u32[]{:S(2)}) collective-permute-start(f32[44,1,256]{2,1,0:T(1,128)S(1)} %get-tuple-element.124), channel_id=1, source_target_pairs={{0,1},{1,2},{2,3},{3,4},{4,5},{5,6},{6,7},{7,8},{8,9},{9,10},{10,1... | collective-permute-start | bytes 135176 | tf_op jit(solution)/shard_map/ppermute | solution.py:20
  275.0 5.4 %collective-permute-start.3 = (f32[44,1,256]{2,1,0:T(1,128)S(1)}, f32[44,1,256]{2,1,0:T(1,128)S(1)}, u32[]{:S(2)}, u32[]{:S(2)}) collective-permute-start(f32[44,1,256]{2,1,0:T(1,128)S(1)} %get-tuple-element.125), channel_id=1, source_target_pairs={{1,0},{2,1},{3,2},{4,3},{5,4},{6,5},{7,6},{8,7},{9,8},{10,9},{11,1... | collective-permute-start | bytes 135176 | tf_op jit(solution)/shard_map/ppermute | solution.py:23
  283.8 20.1 %collective-permute-start.4 = (f32[2,4,4096]{2,1,0:T(4,128)S(1)}, f32[2,4,4096]{2,1,0:T(4,128)S(1)}, u32[]{:S(2)}, u32[]{:S(2)}) collective-permute-start(f32[2,4,4096]{2,1,0:T(4,128)S(1)} %get-tuple-element.126), channel_id=1, source_target_pairs={{0,16},{16,32},{32,48},{48,64},{64,80},{80,96},{96,112},{112,128},... | collective-permute-start | bytes 393224 | tf_op jit(solution)/shard_map/ppermute | solution.py:31
  290.2 13.7 %collective-permute-start.5 = (f32[2,4,4096]{2,1,0:T(4,128)S(1)}, f32[2,4,4096]{2,1,0:T(4,128)S(1)}, u32[]{:S(2)}, u32[]{:S(2)}) collective-permute-start(f32[2,4,4096]{2,1,0:T(4,128)S(1)} %get-tuple-element.127), channel_id=1, source_target_pairs={{16,0},{32,16},{48,32},{64,48},{80,64},{96,80},{112,96},{128,112},... | collective-permute-start | bytes 393224 | tf_op jit(solution)/shard_map/ppermute | solution.py:31
  293.6 27.6 %all-to-all-start = ((f32[2,16,1,4096]{3,0,2,1:T(2,128)}), f32[2,16,1,4096]{3,0,2,1:T(2,128)S(1)}, u32[]{:S(2)}, u32[]{:S(2)}) async-start(f32[2,16,1,4096]{3,0,2,1:T(2,128)} %copy_multiply_fusion), calls=%async_computation | async-start | bytes 1048576 | tf_op jit(solution)/shard_map/all_to_all | solution.py:101
where the time goes:
time: 325 us; the launch traced here: 322 us
  other arithmetic  113 us (35%)
  local copies, waits for them, and re-layouts  81.6 us (25%)
  waiting for transfers between devices  81.4 us (25%)
  starting transfers between devices  33.1 us (10%)
  matrix products  12.3 us (4%)
    ppermute x2, waiting for transfers between devices, extended_2(): lax.ppermute(lax.slice_in_dim(block, block.shape[dim] - width, None, axis...  63.7 us
    another operation x2, other arithmetic  35.4 us
    convert_element_type x2, other arithmetic, form(): front_images = jnp.take(extended, lead_index, axis=1).astype(jnp.float32)  29.1 us
    convert_element_type x2, other arithmetic, form(): back_images = jnp.take(extended, trail_index, axis=1).astype(jnp.float32)  29.1 us
    gather x2, local copies, waits for them, and re-layouts, form(): back_images = jnp.take(extended, trail_index, axis=1).astype(jnp.float32)  26 us
    gather x2, local copies, waits for them, and re-layouts, form(): front_images = jnp.take(extended, lead_index, axis=1).astype(jnp.float32)  25.6 us
    all_to_all x1, waiting for transfers between devices, on_device(): lax.all_to_all(outgoing, 'date', split_axis=1, concat_axis=1, tiled=True)  16.6 us
    convert_element_type x1, other arithmetic, on_device(): power = (jnp.square(extended[0].astype(jnp.float32)) + jnp.square(extende...  12.9 us
  transfers between devices with their start and end apart: 7, of which 3 were waited for; matrix products, arithmetic and copies ran while one was open for 5% of the time, Pallas kernels for 0%

commit v1 on v0

v1 whole, which is shorter than its diff:
```python
import functools

import jax
import jax.numpy as jnp
from jax import lax
from jax.experimental import pallas as pl
from jax.experimental.pallas import tpu as pltpu
from jax.sharding import PartitionSpec as P

ALOOK = 5
RLOOK = 20
LANES = 128
EPS_POWER = 1e-06

INNER = ((2, 3), (2, 4), (2, 5), (3, 4), (3, 5), (4, 5))
LOWER = ((0, 4), (1, 4), (1, 5), (1, 2), (1, 3))
UPPER = ((2, 6), (3, 6), (3, 7), (4, 6), (4, 7))
FORMED = INNER + LOWER + UPPER
FROM_BELOW = tuple((i - 4, j - 4) for i, j in UPPER)
FROM_ABOVE = tuple((i + 4, j + 4) for i, j in LOWER)
KNOWN = FORMED + FROM_BELOW + FROM_ABOVE
COLUMNS = 1280


def products_kernel(edges, powers, counts, *refs):
    sources = refs[: len(counts)]
    look_ref, out_ref, planes_ref, acc_ref = refs[len(counts) :]
    rows, width = sources[0].shape[2], sources[0].shape[3]
    total = 2 * len(edges) + len(powers)
    step = pl.program_id(0)
    places = {}
    for source, start in zip(sources, counts):
        for n in range(source.shape[1]):
            places[start + n] = (source, n)
    used = sorted({k for e in edges for k in e} | set(powers))
    tiles = rows // 16

    def form(index, _):
        row = pl.multiple_of(index % tiles * 16, 16)
        lane = pl.multiple_of(index // tiles * LANES, LANES)
        pixel = {}
        for k in used:
            source, n = places[k]
            pixel[k] = tuple(
                source[c, n, pl.ds(row, 16), pl.ds(lane, LANES)].astype(jnp.float32) for c in (0, 1)
            )
        results = []
        for i, j in edges:
            results.append(pixel[i][0] * pixel[j][0] + pixel[i][1] * pixel[j][1])
        for i, j in edges:
            results.append(pixel[i][1] * pixel[j][0] - pixel[i][0] * pixel[j][1])
        for k in powers:
            results.append(pixel[k][0] * pixel[k][0] + pixel[k][1] * pixel[k][1])
        for p, value in enumerate(results):
            planes_ref[pl.ds(p * rows + row, 16), pl.ds(lane, LANES)] = value.astype(jnp.bfloat16)
        return 0

    lax.fori_loop(0, tiles * (width // LANES), form, 0)
    group = 4 if total % 4 == 0 else 2
    for g in range(total // group):
        span = pl.ds(g * group * rows, group * rows)
        part = jnp.dot(planes_ref[span, :], look_ref[...], preferred_element_type=jnp.float32)

        @pl.when(step % 2 == 0)
        def _():
            acc_ref[span, :] = part

        @pl.when(step % 2 == 1)
        def _():
            acc_ref[span, :] += part

    @pl.when(step % 2 == 1)
    def _():
        for m in range(rows // ALOOK):
            for p in range(0, total, 8):
                size = min(8, total - p)
                value = acc_ref[pl.ds(p * rows + m * ALOOK, size, stride=rows), :]
                for k in range(1, ALOOK):
                    value += acc_ref[pl.ds(p * rows + m * ALOOK + k, size, stride=rows), :]
                out_ref[m, p : p + size, :] = value


def looked_products(edges, powers, sources, counts, look_matrix):
    rows, columns = sources[0].shape[2], sources[0].shape[3]
    total = 2 * len(edges) + len(powers)
    cells = rows // ALOOK
    return pl.pallas_call(
        functools.partial(products_kernel, edges, powers, counts),
        out_shape=jax.ShapeDtypeStruct((cells, total, columns // RLOOK), jnp.float32),
        grid=(columns // COLUMNS,),
        in_specs=[
            pl.BlockSpec((2, s.shape[1], rows, COLUMNS), lambda i: (0, 0, 0, i)) for s in sources
        ]
        + [pl.BlockSpec((COLUMNS, LANES), lambda i: (i % 2, 0))],
        out_specs=pl.BlockSpec((cells, total, LANES), lambda i: (0, 0, i // 2)),
        scratch_shapes=[
            pltpu.VMEM((total * rows, COLUMNS), jnp.bfloat16),
            pltpu.VMEM((total * rows, LANES), jnp.float32),
        ],
        compiler_params=pltpu.CompilerParams(vmem_limit_bytes=48 * 2**20),
    )(*sources, look_matrix)


def coherence_kernel(inner_ref, outer_ref, inner_before, outer_before, inner_after, outer_after, own_ref, low_ref, up_ref):
    cells = inner_ref.shape[0]
    n_in, n_out = len(INNER), len(LOWER) + len(UPPER)
    n_low = len(LOWER)

    def at(ref, before, after, m):
        if m < 0:
            return before[0]
        if m >= cells:
            return after[0]
        return ref[m]

    for m in range(cells):
        smooth = []
        for ref, before, after in (
            (inner_ref, inner_before, inner_after),
            (outer_ref, outer_before, outer_after),
        ):
            smooth.append(
                at(ref, before, after, m - 1) + 2.0 * ref[m] + at(ref, before, after, m + 1)
            )
        inner, outer = smooth
        power = {2 + k: inner[2 * n_in + k : 2 * n_in + k + 1] for k in range(4)}
        for k, place in enumerate((0, 1, 6, 7)):
            power[place] = outer[2 * n_out + k : 2 * n_out + k + 1]

        def scaled(values, edges, start, count):
            first = jnp.concatenate([power[i] for i, _ in edges], axis=0)
            second = jnp.concatenate([power[j] for _, j in edges], axis=0)
            scale = lax.rsqrt(first * second + EPS_POWER)
            return values[start : start + len(edges)] * scale, values[
                start + count : start + count + len(edges)
            ] * scale

        re, im = scaled(inner, INNER, 0, n_in)
        own_ref[m, 0:n_in, :] = re
        own_ref[m, n_in : 2 * n_in, :] = im
        re, im = scaled(outer, LOWER, 0, n_out)
        low_ref[m, 0:n_low, :] = re
        low_ref[m, n_low : 2 * n_low, :] = im
        re, im = scaled(outer, UPPER, n_low, n_out)
        up_ref[m, 0:n_low, :] = re
        up_ref[m, n_low : 2 * n_low, :] = im


def coherences(inner, outer, inner_halo, outer_halo):
    cells, _, width = inner.shape
    shapes = [2 * len(INNER), 2 * len(LOWER), 2 * len(UPPER)]
    full = lambda a: pl.BlockSpec(a.shape, lambda: (0,) * len(a.shape))
    args = (inner, outer, inner_halo[0], outer_halo[0], inner_halo[1], outer_halo[1])
    return pl.pallas_call(
        coherence_kernel,
        out_shape=[jax.ShapeDtypeStruct((cells, n, width), jnp.float32) for n in shapes],
        in_specs=[full(a) for a in args],
        out_specs=[
            pl.BlockSpec((cells, n, width), lambda: (0, 0, 0)) for n in shapes
        ],
        compiler_params=pltpu.CompilerParams(vmem_limit_bytes=32 * 2**20),
    )(*args)


def select_kernel(slot_ref, sign_ref, count_ref, own, low, up, below, above, slots_ref, sums_ref):
    cells, _, width = own.shape
    tables = (own, low, up, below, above)
    lengths = (len(INNER), len(LOWER), len(UPPER), len(UPPER), len(LOWER))
    pick_index = []

    owners = slots_ref.shape[0] // (2 * cells * width // LANES)
    known = len(KNOWN)
    one_hot = []
    hot_im = []
    lanes = lax.broadcasted_iota(jnp.int32, (1, known), 1)
    for o in range(owners):
        hit = (lanes == slot_ref[o]).astype(jnp.float32)
        one_hot.append(hit)
        hot_im.append(hit * sign_ref[o])
    weight_re, weight_im = [], []
    for k in range(2, 6):
        row_re = jnp.zeros((1, known), jnp.float32)
        row_im = jnp.zeros((1, known), jnp.float32)
        for e, (i, j) in enumerate(KNOWN):
            if k in (i, j):
                row_re = jnp.where(lanes == e, count_ref[e], row_re)
                row_im = jnp.where(lanes == e, count_ref[e] if k == i else -count_ref[e], row_im)
        weight_re.append(row_re)
        weight_im.append(row_im)
    re_matrix = jnp.concatenate(one_hot + weight_re, axis=0)
    im_matrix = jnp.concatenate(hot_im + weight_im, axis=0)
    per_owner = 2 * cells * width // LANES
    for m in range(cells):
        for part, matrix in ((0, re_matrix), (1, im_matrix)):
            values = jnp.concatenate(
                [t[m, part * n : (part + 1) * n, :] for t, n in zip(tables, lengths)], axis=0
            )
            made = jnp.dot(
                matrix, values, precision=lax.Precision.HIGHEST, preferred_element_type=jnp.float32
            )
            sums_ref[part * 4 : part * 4 + 4, m * width : (m + 1) * width] = made[owners:]
            for t in range(width // LANES):
                piece = made[:owners, t * LANES : (t + 1) * LANES]
                start = (part * cells + m) * (width // LANES) + t
                slots_ref[pl.ds(start, owners, stride=per_owner), :] = piece


def selected(slot, sign, count, tables, owners):
    cells, _, width = tables[0].shape
    full = lambda a: pl.BlockSpec(a.shape, lambda: (0,) * len(a.shape))
    smem = pl.BlockSpec(memory_space=pltpu.SMEM)
    shape = (owners * 2 * cells * width // LANES, LANES)
    return pl.pallas_call(
        select_kernel,
        out_shape=[
            jax.ShapeDtypeStruct(shape, jnp.float32),
            jax.ShapeDtypeStruct((8, cells * width), jnp.float32),
        ],
        in_specs=[smem, smem, smem] + [full(a) for a in tables],
        out_specs=[pl.BlockSpec(shape, lambda: (0, 0)), pl.BlockSpec((8, cells * width), lambda: (0, 0))],
        compiler_params=pltpu.CompilerParams(vmem_limit_bytes=32 * 2**20),
    )(slot, sign, count, *tables)


def table_kernel(arrived_ref, out_ref):
    _, owners, cell_count = out_ref.shape
    tiles = cell_count // LANES
    for part in range(2):
        for t in range(tiles):
            out_ref[part, :, t * LANES : (t + 1) * LANES] = arrived_ref[
                pl.ds(part * tiles + t, owners, stride=2 * tiles), :
            ]


def as_table(arrived, owners, cell_count):
    return pl.pallas_call(
        table_kernel,
        out_shape=jax.ShapeDtypeStruct((2, owners, cell_count), jnp.float32),
        compiler_params=pltpu.CompilerParams(vmem_limit_bytes=32 * 2**20),
    )(arrived)


def shifted(value, axis, steps):
    count = lax.axis_size(axis)
    first, last = (max(0, -steps), min(count, count - steps))
    return lax.ppermute(value, axis, [(source, source + steps) for source in range(first, last)])


def on_device(images, date_pairs, assignment):
    owners = lax.axis_size("date")
    myself = lax.axis_index("date")
    local_dates = images.shape[1]
    columns = images.shape[3]
    below = shifted(images[:, local_dates - 2 :], "date", 1)
    above = shifted(images[:, :2], "date", -1)
    look_matrix = (
        jnp.arange(2 * COLUMNS)[:, None] // RLOOK == jnp.arange(LANES)[None, :]
    ).astype(jnp.bfloat16)

    anchor = myself * local_dates - 2
    first = date_pairs[:, 0] - anchor
    second = date_pairs[:, 1] - anchor
    low_date = jnp.minimum(first, second)
    high_date = jnp.maximum(first, second)
    known = jnp.array(KNOWN, jnp.int32)
    is_edge = (low_date[:, None] == known[None, :, 0]) & (high_date[:, None] == known[None, :, 1])
    count = jnp.sum(is_edge, axis=0).astype(jnp.float32)
    edge = jnp.sum(jnp.where(is_edge, jnp.arange(len(KNOWN))[None, :], 0), axis=1)
    mine = date_pairs[:, 0] // local_dates == myself
    matches = (assignment[None, :] // owners == jnp.arange(owners)[:, None]) & mine[None, :]
    present = jnp.any(matches, axis=1)
    slot = jnp.where(present, jnp.sum(jnp.where(matches, edge[None, :], 0), axis=1), -1)
    sign = jnp.sum(jnp.where(matches, jnp.where(first < second, 1.0, -1.0)[None, :], 0.0), axis=1)

    inner = looked_products(INNER, (2, 3, 4, 5), (images,), (2,), look_matrix)
    outer = looked_products(
        LOWER + UPPER, (0, 1, 6, 7), (below, images, above), (0, 2, 6), look_matrix
    )
    cells = inner.shape[0]
    inner_halo = (shifted(inner[cells - 1 :], "strip", 1), shifted(inner[:1], "strip", -1))
    outer_halo = (shifted(outer[cells - 1 :], "strip", 1), shifted(outer[:1], "strip", -1))
    own, low, up = coherences(inner, outer, inner_halo, outer_halo)
    from_below = shifted(up, "date", 1)
    from_above = shifted(low, "date", -1)
    slots, sums = selected(slot, sign, count, (own, low, up, from_below, from_above), owners)
    outgoing = slots.reshape(owners, slots.shape[0] // owners, LANES)
    arrived = lax.all_to_all(outgoing, "date", split_axis=0, concat_axis=0, tiled=True)
    cell_count = cells * (columns // RLOOK)
    coherence = as_table(arrived.reshape(slots.shape), owners, cell_count)
    return (coherence, sums.reshape(2, local_dates, cell_count))


def solution(mesh):
    return jax.shard_map(
        on_device,
        mesh=mesh,
        in_specs=(P(None, "date", "strip", None), P(), P()),
        out_specs=(P(None, "date", "strip"), P(None, "date", "strip")),
        check_vma=False,
    )
```

time: 325 us -> 130 us (0.40)
  other arithmetic: 113 us -> 1.78 us
  local copies, waits for them, and re-layouts: 81.6 us -> 6.83 us
  Pallas kernels: 0 us -> 49.8 us
  waiting for transfers between devices: 81.4 us -> 33.2 us
  matrix products: 12.3 us -> 0 us
    convert_element_type x5 -> x2, other arithmetic: 71.1 us -> 1.19 us  [the longest x1 1.19 us: on_device(): look_matrix = (jnp.arange(2 * COLUMNS)[:, None] // RLOOK == jnp.arange(LA...]
    gather x6 -> x0, local copies, waits for them, and re-layouts: 52.9 us -> none  [the longest x2 26 us: form(): back_images = jnp.take(extended, trail_index, axis=1).astype(jnp.float32)]
    pallas_call x0 -> x5, Pallas kernels: none -> 49.8 us  [the longest x2 46 us: looked_products(): pl.pallas_call(functools.partial(products_kernel, edges, powers, counts),...]
    ppermute x6 -> x8, waiting for transfers between devices: 64.8 us -> 16.5 us  [shifted(): lax.ppermute(value, axis, [(source, source + steps) for source in range(f...]
    another operation x2 -> x0, other arithmetic: 35.4 us -> none
    dot_general x5 -> x0, matrix products: 12.3 us -> none  [the longest x3 11.4 us: range_looks(): jnp.einsum('...ar,rl->...al', pixels, look_matrix, preferred_element_type...]
    unnamed x30 -> x8, local copies, waits for them, and re-layouts: 11.1 us -> 0.03 us
    convert_element_type x1 -> x0, local copies, waits for them, and re-layouts: 8.57 us -> none  [on_device(): power = (jnp.square(extended[0].astype(jnp.float32)) + jnp.square(extende...]
  transfers between devices with their start and end apart: 7 -> 9, of which waited for: 3 -> 6; matrix products, arithmetic and copies ran while one was open for 5% -> 2% of each run, Pallas kernels for 0% -> 36%
where the time goes in v1:
time: 130 us; the launch traced here: 128 us
  Pallas kernels  49.8 us (38%)
  starting transfers between devices  35.3 us (27%)
  waiting for transfers between devices  33.2 us (26%)
  local copies, waits for them, and re-layouts  6.83 us (5%)
  other arithmetic  1.78 us (1%)
    pallas_call x2, Pallas kernels, looked_products(): pl.pallas_call(functools.partial(products_kernel, edges, powers, counts),...  46 us
    ppermute x8, starting transfers between devices, shifted(): lax.ppermute(value, axis, [(source, source + steps) for source in range(f...  25.6 us
    all_to_all x1, waiting for transfers between devices, on_device(): lax.all_to_all(outgoing, 'date', split_axis=0, concat_axis=0, tiled=True)  16.6 us
    ppermute x8, waiting for transfers between devices, shifted(): lax.ppermute(value, axis, [(source, source + steps) for source in range(f...  16.5 us
    all_to_all x1, starting transfers between devices, on_device(): lax.all_to_all(outgoing, 'date', split_axis=0, concat_axis=0, tiled=True)  9.66 us
    slice x1, local copies, waits for them, and re-layouts, on_device(): above = shifted(images[:, :2], 'date', -1)  6.1 us
  transfers between devices with their start and end apart: 9, of which 6 were waited for; matrix products, arithmetic and copies ran while one was open for 2% of the time, Pallas kernels for 36%

profile of v1, /device:TPU:9, one launch (start us, length us, event | category | flops | bytes accessed | tf_op | source)
XLA Modules:
  0.0 127.7 jit_solution(8660908146833078955)
XLA Ops:
  0.6 6.1 %fusion.7 = (bf16[2,2,80,5120]{3,2,1,0:T(8,128)(2,1)}, bf16[2,2,80,5120]{3,2,1,0:T(8,128)(2,1)}) fusion(bf16[2,4,80,5120]{3,2,1,0:T(8,128)(2,1)} %refs_1_.1), kind=kLoop, calls=%fused_computation.33 | loop fusion | bytes 13107200 | tf_op jit(solution)/shard_map/slice | solution.py:255
  6.7 4.1 %collective-permute-start = (bf16[2,2,80,5120]{3,2,1,0:T(8,128)(2,1)}, bf16[2,2,80,5120]{3,2,1,0:T(8,128)(2,1)}, u32[]{:S(2)}, u32[]{:S(2)}) collective-permute-start(bf16[2,2,80,5120]{3,2,1,0:T(8,128)(2,1)} %get-tuple-element.15), channel_id=1, source_target_pairs={{0,16},{16,32},{32,48},{48,64},{64,80},{80,96},{96,112},{112,128},... | collective-permute-start | bytes 9830408 | tf_op jit(solution)/shard_map/ppermute | solution.py:246
  10.8 2.0 %collective-permute-start.1 = (bf16[2,2,80,5120]{3,2,1,0:T(8,128)(2,1)}, bf16[2,2,80,5120]{3,2,1,0:T(8,128)(2,1)}, u32[]{:S(2)}, u32[]{:S(2)}) collective-permute-start(bf16[2,2,80,5120]{3,2,1,0:T(8,128)(2,1)} %get-tuple-element.14), channel_id=1, source_target_pairs={{16,0},{32,16},{48,32},{64,48},{80,64},{96,80},{112,96},{128,112},... | collective-permute-start | bytes 9830408 | tf_op jit(solution)/shard_map/ppermute | solution.py:246
  12.8 1.2 fusion.refs_1_.refs_3_
  14.0 0.0 copy-start
  14.0 0.0 copy-start.1
  14.0 0.0 copy-start.2
  14.0 0.0 copy-start.3
  14.1 19.1 %shard_map.59.inner_ref = f32[16,16,256]{2,1,0:T(8,128)S(1)} custom-call(bf16[2,4,80,5120]{3,2,1,0:T(8,128)(2,1)} %refs_1_.1, bf16[2560,128]{1,0:T(8,128)(2,1)S(1)} %fusion.refs_1_.refs_3_), custom_call_target="tpu_custom_call" | custom-call | tf_op jit(solution)/shard_map/pallas_call | solution.py:87
  33.2 3.1 %collective-permute-start.2 = (f32[1,16,256]{2,1,0:T(8,128)S(1)}, f32[1,16,256]{2,1,0:T(8,128)S(1)}, u32[]{:S(2)}, u32[]{:S(2)}) collective-permute-start(f32[1,16,256]{2,1,0:T(8,128)S(1)} %get-tuple-element.19), channel_id=1, source_target_pairs={{0,1},{1,2},{2,3},{3,4},{4,5},{5,6},{6,7},{7,8},{8,9},{9,10},{10,1... | collective-permute-start | bytes 49160 | tf_op jit(solution)/shard_map/ppermute | solution.py:246
  36.3 4.3 %collective-permute-start.4 = (f32[1,16,256]{2,1,0:T(8,128)S(1)}, f32[1,16,256]{2,1,0:T(8,128)S(1)}, u32[]{:S(2)}, u32[]{:S(2)}) collective-permute-start(f32[1,16,256]{2,1,0:T(8,128)S(1)} %get-tuple-element.18), channel_id=1, source_target_pairs={{1,0},{2,1},{3,2},{4,3},{5,4},{6,5},{7,6},{8,7},{9,8},{10,9},{11,1... | collective-permute-start | bytes 49160 | tf_op jit(solution)/shard_map/ppermute | solution.py:246
  40.6 0.0 copy-done
  40.6 0.0 copy-done.1
  40.6 0.0 copy-done.2
  40.6 0.2 convert_reduce_fusion
  40.8 0.0 copy-done.3
  40.9 0.1 select_reduce_fusion.2
  41.0 5.7 %collective-permute-done.refs_0_ = bf16[2,2,80,5120]{3,2,1,0:T(8,128)(2,1)} collective-permute-done((bf16[2,2,80,5120]{3,2,1,0:T(8,128)(2,1)}, bf16[2,2,80,5120]{3,2,1,0:T(8,128)(2,1)}, u32[]{:S(2)}, u32[]{:S(2)}) %collective-permute-start) | collective-permute-done | bytes 3276832 | tf_op jit(solution)/shard_map/ppermute | solution.py:246
  46.7 4.4 %collective-permute-done.1.refs_2_ = bf16[2,2,80,5120]{3,2,1,0:T(8,128)(2,1)} collective-permute-done((bf16[2,2,80,5120]{3,2,1,0:T(8,128)(2,1)}, bf16[2,2,80,5120]{3,2,1,0:T(8,128)(2,1)}, u32[]{:S(2)}, u32[]{:S(2)}) %collective-permute-start.1) | collective-permute-done | bytes 3276832 | tf_op jit(solution)/shard_map/ppermute | solution.py:246
  51.1 26.9 %shard_map.60.outer_ref = f32[16,24,256]{2,1,0:T(8,128)S(1)} custom-call(bf16[2,2,80,5120]{3,2,1,0:T(8,128)(2,1)} %collective-permute-done.refs_0_, bf16[2,4,80,5120]{3,2,1,0:T(8,128)(2,1)} %refs_1_.1, bf16[2,2,80,5120]{3,2,1,0:T(8,128)(2,1)} %collective-permute-done.1.refs_2_, bf16[2560,128]{1,0:T(8,128)(2,1)S(1)} %fusion.refs_1_.refs_3_), custom_call_target="tpu_custom_call" | custom-call | tf_op jit(solution)/shard_map/pallas_call | solution.py:87
  78.1 3.1 %collective-permute-start.3 = (f32[1,24,256]{2,1,0:T(8,128)S(1)}, f32[1,24,256]{2,1,0:T(8,128)S(1)}, u32[]{:S(2)}, u32[]{:S(2)}) collective-permute-start(f32[1,24,256]{2,1,0:T(8,128)S(1)} %get-tuple-element.17), channel_id=1, source_target_pairs={{0,1},{1,2},{2,3},{3,4},{4,5},{5,6},{6,7},{7,8},{8,9},{9,10},{10,1... | collective-permute-start | bytes 73736 | tf_op jit(solution)/shard_map/ppermute | solution.py:246
  81.2 4.3 %collective-permute-start.5 = (f32[1,24,256]{2,1,0:T(8,128)S(1)}, f32[1,24,256]{2,1,0:T(8,128)S(1)}, u32[]{:S(2)}, u32[]{:S(2)}) collective-permute-start(f32[1,24,256]{2,1,0:T(8,128)S(1)} %get-tuple-element.16), channel_id=1, source_target_pairs={{1,0},{2,1},{3,2},{4,3},{5,4},{6,5},{7,6},{8,7},{9,8},{10,9},{11,1... | collective-permute-start | bytes 73736 | tf_op jit(solution)/shard_map/ppermute | solution.py:246
  85.5 0.1 fusion.5
  85.6 0.0 collective-permute-done.2.inner_before
  85.6 0.0 collective-permute-done.4.inner_after
  85.6 0.0 collective-permute-done.3.outer_before
  85.6 0.8 collective-permute-done.5.outer_after
  86.4 0.3 shard_map.61
  86.7 2.9 %collective-permute-start.6 = (f32[16,10,256]{2,1,0:T(8,128)S(1)}, f32[16,10,256]{2,1,0:T(8,128)S(1)}, u32[]{:S(2)}, u32[]{:S(2)}) collective-permute-start(f32[16,10,256]{2,1,0:T(8,128)S(1)} %get-tuple-element.9.up), channel_id=1, source_target_pairs={{0,16},{16,32},{32,48},{48,64},{64,80},{80,96},{96,112},{112,128},... | collective-permute-start | bytes 491528 | tf_op jit(solution)/shard_map/ppermute | solution.py:246
  89.6 1.9 %collective-permute-start.7 = (f32[16,10,256]{2,1,0:T(8,128)S(1)}, f32[16,10,256]{2,1,0:T(8,128)S(1)}, u32[]{:S(2)}, u32[]{:S(2)}) collective-permute-start(f32[16,10,256]{2,1,0:T(8,128)S(1)} %get-tuple-element.8.low), channel_id=1, source_target_pairs={{16,0},{32,16},{48,32},{64,48},{80,64},{96,80},{112,96},{128,112},... | collective-permute-start | bytes 491528 | tf_op jit(solution)/shard_map/ppermute | solution.py:246
  91.6 0.1 select_reduce_fusion.1.sign_ref
  91.7 1.2 collective-permute-done.6.below
  92.9 4.4 %collective-permute-done.7.above = f32[16,10,256]{2,1,0:T(8,128)S(1)} collective-permute-done((f32[16,10,256]{2,1,0:T(8,128)S(1)}, f32[16,10,256]{2,1,0:T(8,128)S(1)}, u32[]{:S(2)}, u32[]{:S(2)}) %collective-permute-start.7) | collective-permute-done | bytes 163872 | tf_op jit(solution)/shard_map/ppermute | solution.py:246
  97.3 2.3 %shard_map.62 = (f32[1024,128]{1,0:T(8,128)}, f32[8,4096]{1,0:T(8,128)S(1)}) custom-call(s32[16]{0:T(128)S(1)} %broadcast_select_fusion.slot_ref, f32[16]{0:T(128)S(1)} %select_reduce_fusion.1.sign_ref, f32[26]{0:T(128)S(1)} %convert_element_type.12.count_ref, f32[16,12,256]{2,1,0:T(8,128)S(1)} %get-tuple-element.7.own, ...), custom_call_target="tpu_custom_call" | custom-call | tf_op jit(solution)/shard_map/pallas_call | solution.py:213
  99.6 9.7 %all-to-all-start = ((f32[16,64,128]{2,1,0:T(8,128)}), f32[16,64,128]{2,1,0:T(8,128)S(1)}, u32[]{:S(2)}, u32[]{:S(2)}) async-start(f32[16,64,128]{2,1,0:T(8,128)} %bitcast.4), calls=%async_computation | async-start | bytes 1048576 | tf_op jit(solution)/shard_map/all_to_all | solution.py:287
  109.3 0.7 reshape.103
  110.0 16.6 %all-to-all-done = f32[16,64,128]{2,1,0:T(8,128)S(1)} async-done(((f32[16,64,128]{2,1,0:T(8,128)}), f32[16,64,128]{2,1,0:T(8,128)S(1)}, u32[]{:S(2)}, u32[]{:S(2)}) %all-to-all-start) | async-done | bytes 524320 | tf_op jit(solution)/shard_map/all_to_all | solution.py:287
  126.6 1.1 shard_map.63
  (9 shorter events, 0.1 us)
Async XLA Ops:
  6.7 40.0 %collective-permute-start = (bf16[2,2,80,5120]{3,2,1,0:T(8,128)(2,1)}, bf16[2,2,80,5120]{3,2,1,0:T(8,128)(2,1)}, u32[]{:S(2)}, u32[]{:S(2)}) collective-permute-start(bf16[2,2,80,5120]{3,2,1,0:T(8,128)(2,1)} %get-tuple-element.15), channel_id=1, source_target_pairs={{0,16},{16,32},{32,48},{48,64},{64,80},{80,96},{96,112},{112,128},... | collective-permute-start | bytes 9830408 | tf_op jit(solution)/shard_map/ppermute | solution.py:246
  10.8 40.3 %collective-permute-start.1 = (bf16[2,2,80,5120]{3,2,1,0:T(8,128)(2,1)}, bf16[2,2,80,5120]{3,2,1,0:T(8,128)(2,1)}, u32[]{:S(2)}, u32[]{:S(2)}) collective-permute-start(bf16[2,2,80,5120]{3,2,1,0:T(8,128)(2,1)} %get-tuple-element.14), channel_id=1, source_target_pairs={{16,0},{32,16},{48,32},{64,48},{80,64},{96,80},{112,96},{128,112},... | collective-permute-start | bytes 9830408 | tf_op jit(solution)/shard_map/ppermute | solution.py:246
  14.0 26.6 %copy-start = (s32[128,2]{0,1:T(2,128)S(1)}, s32[128,2]{0,1:T(2,128)}, u32[]{:S(2)}) copy-start(s32[128,2]{0,1:T(2,128)} %param.5) | copy-start | bytes 3076
  14.0 26.6 %copy-start.1 = (s32[26]{0:T(128)S(1)}, s32[26]{0:T(128)}, u32[]{:S(2)}) copy-start(s32[26]{0:T(128)} %constant.60) | copy-start | bytes 316
  14.0 26.6 %copy-start.2 = (s32[26]{0:T(128)S(1)}, s32[26]{0:T(128)}, u32[]{:S(2)}) copy-start(s32[26]{0:T(128)} %constant.62) | copy-start | bytes 316
  14.0 26.8 %copy-start.3 = (s32[128]{0:T(128)S(1)}, s32[128]{0:T(128)}, u32[]{:S(2)}) copy-start(s32[128]{0:T(128)} %param.6) | copy-start | bytes 1540
  33.2 52.4 %collective-permute-start.2 = (f32[1,16,256]{2,1,0:T(8,128)S(1)}, f32[1,16,256]{2,1,0:T(8,128)S(1)}, u32[]{:S(2)}, u32[]{:S(2)}) collective-permute-start(f32[1,16,256]{2,1,0:T(8,128)S(1)} %get-tuple-element.19), channel_id=1, source_target_pairs={{0,1},{1,2},{2,3},{3,4},{4,5},{5,6},{6,7},{7,8},{8,9},{9,10},{10,1... | collective-permute-start | bytes 49160 | tf_op jit(solution)/shard_map/ppermute | solution.py:246
  36.3 49.3 %collective-permute-start.4 = (f32[1,16,256]{2,1,0:T(8,128)S(1)}, f32[1,16,256]{2,1,0:T(8,128)S(1)}, u32[]{:S(2)}, u32[]{:S(2)}) collective-permute-start(f32[1,16,256]{2,1,0:T(8,128)S(1)} %get-tuple-element.18), channel_id=1, source_target_pairs={{1,0},{2,1},{3,2},{4,3},{5,4},{6,5},{7,6},{8,7},{9,8},{10,9},{11,1... | collective-permute-start | bytes 49160 | tf_op jit(solution)/shard_map/ppermute | solution.py:246
  78.1 7.5 %collective-permute-start.3 = (f32[1,24,256]{2,1,0:T(8,128)S(1)}, f32[1,24,256]{2,1,0:T(8,128)S(1)}, u32[]{:S(2)}, u32[]{:S(2)}) collective-permute-start(f32[1,24,256]{2,1,0:T(8,128)S(1)} %get-tuple-element.17), channel_id=1, source_target_pairs={{0,1},{1,2},{2,3},{3,4},{4,5},{5,6},{6,7},{7,8},{8,9},{9,10},{10,1... | collective-permute-start | bytes 73736 | tf_op jit(solution)/shard_map/ppermute | solution.py:246
  81.2 5.2 %collective-permute-start.5 = (f32[1,24,256]{2,1,0:T(8,128)S(1)}, f32[1,24,256]{2,1,0:T(8,128)S(1)}, u32[]{:S(2)}, u32[]{:S(2)}) collective-permute-start(f32[1,24,256]{2,1,0:T(8,128)S(1)} %get-tuple-element.16), channel_id=1, source_target_pairs={{1,0},{2,1},{3,2},{4,3},{5,4},{6,5},{7,6},{8,7},{9,8},{10,9},{11,1... | collective-permute-start | bytes 73736 | tf_op jit(solution)/shard_map/ppermute | solution.py:246
  86.7 6.2 %collective-permute-start.6 = (f32[16,10,256]{2,1,0:T(8,128)S(1)}, f32[16,10,256]{2,1,0:T(8,128)S(1)}, u32[]{:S(2)}, u32[]{:S(2)}) collective-permute-start(f32[16,10,256]{2,1,0:T(8,128)S(1)} %get-tuple-element.9.up), channel_id=1, source_target_pairs={{0,16},{16,32},{32,48},{48,64},{64,80},{80,96},{96,112},{112,128},... | collective-permute-start | bytes 491528 | tf_op jit(solution)/shard_map/ppermute | solution.py:246
  89.6 7.7 %collective-permute-start.7 = (f32[16,10,256]{2,1,0:T(8,128)S(1)}, f32[16,10,256]{2,1,0:T(8,128)S(1)}, u32[]{:S(2)}, u32[]{:S(2)}) collective-permute-start(f32[16,10,256]{2,1,0:T(8,128)S(1)} %get-tuple-element.8.low), channel_id=1, source_target_pairs={{16,0},{32,16},{48,32},{64,48},{80,64},{96,80},{112,96},{128,112},... | collective-permute-start | bytes 491528 | tf_op jit(solution)/shard_map/ppermute | solution.py:246
  99.6 27.0 %all-to-all-start = ((f32[16,64,128]{2,1,0:T(8,128)}), f32[16,64,128]{2,1,0:T(8,128)S(1)}, u32[]{:S(2)}, u32[]{:S(2)}) async-start(f32[16,64,128]{2,1,0:T(8,128)} %bitcast.4), calls=%async_computation | async-start | bytes 1048576 | tf_op jit(solution)/shard_map/all_to_all | solution.py:287

commit v2 on v0

v2 whole, which is shorter than its diff:
```python
import functools

import jax
import jax.numpy as jnp
from jax import lax
from jax.experimental import pallas as pl
from jax.experimental.pallas import tpu as pltpu
from jax.sharding import PartitionSpec as P

ALOOK = 5
RLOOK = 20
LANES = 128
TILE = 16
COLUMNS = 1280
FIXED = 32000.0
EPS_POWER = 1e-06
MIB = 2**20

INNER = ((2, 3), (2, 4), (2, 5), (3, 4), (3, 5), (4, 5))
LOWER = ((0, 4), (1, 4), (1, 5), (1, 2), (1, 3))
UPPER = ((2, 6), (3, 6), (3, 7), (4, 6), (4, 7))
OUTER = LOWER + UPPER
FROM_BELOW = tuple((i - 4, j - 4) for i, j in UPPER)
FROM_ABOVE = tuple((i + 4, j + 4) for i, j in LOWER)
KNOWN = INNER + OUTER + FROM_BELOW + FROM_ABOVE
INNER_POWERS = (2, 3, 4, 5)
OUTER_POWERS = (0, 1, 6, 7)


def products_kernel(edges, powers, places, groups, *refs):
    look_ref, out_ref, planes_ref, acc_ref = refs[-4:]
    width = planes_ref.shape[1]
    total = 2 * len(edges) + len(powers)
    rows = planes_ref.shape[0] // total
    step = pl.program_id(0)
    used = sorted({k for e in edges for k in e} | set(powers))

    def form(index, _):
        lane = pl.ds(pl.multiple_of(index * LANES, LANES), LANES)
        for tile in range(rows // TILE):
            pixel = {}
            for k in used:
                source, date, row = places[k][tile]
                pixel[k] = tuple(
                    refs[source][c, date, row : row + TILE, lane].astype(jnp.float32)
                    for c in (0, 1)
                )
            results = []
            for i, j in edges:
                results.append(pixel[i][0] * pixel[j][0] + pixel[i][1] * pixel[j][1])
            for i, j in edges:
                results.append(pixel[i][1] * pixel[j][0] - pixel[i][0] * pixel[j][1])
            for k in powers:
                results.append(pixel[k][0] * pixel[k][0] + pixel[k][1] * pixel[k][1])
            for p, value in enumerate(results):
                first = p * rows + tile * TILE
                planes_ref[first : first + TILE, lane] = value.astype(jnp.bfloat16)
        return 0

    lax.fori_loop(0, width // LANES, form, 0)
    part = jnp.dot(planes_ref[...], look_ref[...], preferred_element_type=jnp.float32)

    @pl.when(step % 2 == 0)
    def _():
        acc_ref[...] = part

    @pl.when(step % 2 == 1)
    def _():
        acc_ref[...] += part
        for m, (first, last) in enumerate(groups):
            for p in range(0, total, 8):
                size = min(8, total - p)
                value = acc_ref[pl.ds(p * rows + first, size, stride=rows), :]
                for row in range(first + 1, last):
                    value += acc_ref[pl.ds(p * rows + row, size, stride=rows), :]
                out_ref[m, p : p + size, :] = value


def looked_products(edges, powers, sources, places, groups, rows, columns, look_matrix):
    total = 2 * len(edges) + len(powers)

    def spec(block, index, offset):
        return pl.BlockSpec(block + (COLUMNS,), lambda i: index + (i + offset // COLUMNS,))

    return pl.pallas_call(
        functools.partial(products_kernel, edges, powers, places, groups),
        out_shape=jax.ShapeDtypeStruct((len(groups), total, columns // RLOOK), jnp.float32),
        grid=(columns // COLUMNS,),
        in_specs=[spec(*s[1:]) for s in sources]
        + [pl.BlockSpec((COLUMNS, LANES), lambda i: (i % 2, 0))],
        out_specs=pl.BlockSpec((len(groups), total, LANES), lambda i: (0, 0, i // 2)),
        scratch_shapes=[
            pltpu.VMEM((total * rows, COLUMNS), jnp.bfloat16),
            pltpu.VMEM((total * rows, LANES), jnp.float32),
        ],
        compiler_params=pltpu.CompilerParams(vmem_limit_bytes=48 * MIB),
    )(*[s[0] for s in sources], look_matrix)


def pack_kernel(parts, *refs):
    outs = refs[-2:]
    for n, (out, _, row) in enumerate(parts):
        outs[out][:, :, row : row + TILE, :] = refs[n][...]


def packed_rows(images, tiles):
    _, local_dates, _, columns = images.shape
    last = local_dates // 2 - 1
    parts = [(out, t, n * TILE) for out in range(2) for n, t in enumerate(tiles)]
    return pl.pallas_call(
        functools.partial(pack_kernel, parts),
        out_shape=[jax.ShapeDtypeStruct((2, 2, len(tiles) * TILE, columns), images.dtype)] * 2,
        grid=(columns // COLUMNS,),
        in_specs=[
            pl.BlockSpec((2, 2, TILE, COLUMNS), lambda i, d=last * (1 - out), t=t: (0, d, t, i))
            for out, t, _ in parts
        ],
        out_specs=[pl.BlockSpec((2, 2, len(tiles) * TILE, COLUMNS), lambda i: (0, 0, 0, i))] * 2,
        compiler_params=pltpu.CompilerParams(vmem_limit_bytes=32 * MIB),
    )(*[images] * len(parts))


def coherence_kernel(layout, *refs):
    inner_ref, first_ref, second_ref, before_ref, after_ref = refs[:5]
    outs = refs[5:]
    cells, n_first, width = inner_ref.shape
    n_in, n_out = len(INNER), len(OUTER)
    halves = width // LANES
    block = 2 * cells * halves

    def inner_at(m):
        if m < 0:
            return before_ref[0, :n_first]
        if m >= cells:
            return after_ref[0, :n_first]
        return inner_ref[m]

    def outer_at(m):
        if m < 0:
            return before_ref[0, n_first:]
        if m >= cells:
            return after_ref[0, n_first:]
        return sum(ref[n] for ref, n in zip((first_ref, second_ref), layout[m]) if n is not None)

    inners = [inner_at(m) for m in range(-1, cells + 1)]
    outers = [outer_at(m) for m in range(-1, cells + 1)]
    for m in range(cells):
        inner = inners[m] + 2.0 * inners[m + 1] + inners[m + 2]
        outer = outers[m] + 2.0 * outers[m + 1] + outers[m + 2]
        power = {}
        for n, k in enumerate(INNER_POWERS):
            power[k] = inner[2 * n_in + n : 2 * n_in + n + 1]
        for n, k in enumerate(OUTER_POWERS):
            power[k] = outer[2 * n_out + n : 2 * n_out + n + 1]
        for out, values, edges, start, count in (
            (outs[0], inner, INNER, 0, n_in),
            (outs[1], outer, LOWER, 0, n_out),
            (outs[2], outer, UPPER, len(LOWER), n_out),
        ):
            size = len(edges)
            first = jnp.concatenate([power[i] for i, _ in edges], axis=0)
            second = jnp.concatenate([power[j] for _, j in edges], axis=0)
            scale = lax.rsqrt(first * second + EPS_POWER)
            for part in range(2):
                begin = start + part * count
                value = values[begin : begin + size] * scale
                for h in range(halves):
                    row = (part * cells + m) * halves + h
                    out[pl.ds(row, size, stride=block), :] = value[:, h * LANES : (h + 1) * LANES]


def coherences(layout, inner, first, second, before, after):
    cells, _, width = inner.shape
    block = 2 * cells * (width // LANES)
    return pl.pallas_call(
        functools.partial(coherence_kernel, layout),
        out_shape=[
            jax.ShapeDtypeStruct((len(e) * block, LANES), jnp.float32)
            for e in (INNER, LOWER, UPPER)
        ],
        compiler_params=pltpu.CompilerParams(vmem_limit_bytes=32 * MIB),
    )(inner, first, second, before, after)


def slots_kernel(slot_ref, sign_ref, *refs):
    out_ref, known_ref = refs[-2:]
    owners, block, _ = out_ref.shape
    start = 0
    for table in refs[:-2]:
        known_ref[start : start + table.shape[0], :] = table[...]
        start += table.shape[0]
    for o in range(owners):
        row = pl.multiple_of(slot_ref[o] * block, block)
        value = known_ref[pl.ds(row, block), :]
        half = block // 2
        scales = (jnp.abs(sign_ref[o]) * FIXED, sign_ref[o] * FIXED)
        for part in range(2):
            fixed = jnp.round(value[part * half : (part + 1) * half] * scales[part])
            out_ref[o, part * half : (part + 1) * half, :] = fixed.astype(jnp.int32).astype(jnp.int16)


def slots_of(slot, sign, tables, owners, block):
    smem = pl.BlockSpec(memory_space=pltpu.SMEM)
    vmem = pl.BlockSpec(memory_space=pltpu.VMEM)
    return pl.pallas_call(
        slots_kernel,
        out_shape=jax.ShapeDtypeStruct((owners, block, LANES), jnp.int16),
        in_specs=[smem, smem] + [vmem] * len(tables),
        scratch_shapes=[pltpu.VMEM((len(KNOWN) * block, LANES), jnp.float32)],
        compiler_params=pltpu.CompilerParams(vmem_limit_bytes=32 * MIB),
    )(slot, sign, *tables)


def sums_kernel(count_ref, *refs):
    out_ref, rows_ref = refs[-2:]
    parts, dates, cell_count = out_ref.shape
    tiles = cell_count // LANES
    tables = []
    for table in refs[:-2]:
        tables += [(table, n * parts * tiles) for n in range(table.shape[0] // (parts * tiles))]
    for part in range(parts):
        totals = [jnp.zeros((tiles, LANES), jnp.float32) for _ in range(dates)]
        for e, (table, row) in enumerate(tables):
            value = table[row + part * tiles : row + (part + 1) * tiles, :] * count_ref[e]
            for d, k in enumerate(INNER_POWERS):
                if k == KNOWN[e][0] or (k == KNOWN[e][1] and part == 0):
                    totals[d] = totals[d] + value
                elif k == KNOWN[e][1]:
                    totals[d] = totals[d] - value
        for d in range(dates):
            first = (part * dates + d) * tiles
            rows_ref[first : first + tiles, :] = totals[d]
    for part in range(parts):
        for t in range(tiles):
            out_ref[part, :, t * LANES : (t + 1) * LANES] = rows_ref[
                pl.ds(part * dates * tiles + t, dates, stride=tiles), :
            ]


def sums_of(count, tables, local_dates, cell_count):
    smem = pl.BlockSpec(memory_space=pltpu.SMEM)
    vmem = pl.BlockSpec(memory_space=pltpu.VMEM)
    return pl.pallas_call(
        sums_kernel,
        out_shape=jax.ShapeDtypeStruct((2, local_dates, cell_count), jnp.float32),
        in_specs=[smem] + [vmem] * len(tables),
        scratch_shapes=[pltpu.VMEM((2 * local_dates * cell_count // LANES, LANES), jnp.float32)],
        compiler_params=pltpu.CompilerParams(vmem_limit_bytes=32 * MIB),
    )(count, *tables)


def table_kernel(arrived_ref, out_ref, rows_ref):
    parts, owners, cell_count = out_ref.shape
    tiles = cell_count // LANES
    for o in range(owners):
        rows_ref[o * parts * tiles : (o + 1) * parts * tiles, :] = arrived_ref[o].astype(
            jnp.int32
        ).astype(jnp.float32) * (1.0 / FIXED)
    for part in range(parts):
        for t in range(tiles):
            out_ref[part, :, t * LANES : (t + 1) * LANES] = rows_ref[
                pl.ds(part * tiles + t, owners, stride=parts * tiles), :
            ]


def as_table(arrived, cell_count):
    owners, block, _ = arrived.shape
    return pl.pallas_call(
        table_kernel,
        out_shape=jax.ShapeDtypeStruct((2, owners, cell_count), jnp.float32),
        scratch_shapes=[pltpu.VMEM((owners * block, LANES), jnp.float32)],
        compiler_params=pltpu.CompilerParams(vmem_limit_bytes=32 * MIB),
    )(arrived)


def shifted(value, axis, steps):
    count = lax.axis_size(axis)
    first, last = (max(0, -steps), min(count, count - steps))
    return lax.ppermute(value, axis, [(source, source + steps) for source in range(first, last)])


def pair_tables(date_pairs, assignment, myself, owners, local_dates):
    anchor = myself * local_dates - 2
    first = date_pairs[:, 0] - anchor
    second = date_pairs[:, 1] - anchor
    low_date = jnp.minimum(first, second)
    high_date = jnp.maximum(first, second)
    known = jnp.array(KNOWN, jnp.int32)
    is_edge = (low_date[:, None] == known[None, :, 0]) & (high_date[:, None] == known[None, :, 1])
    count = jnp.sum(is_edge, axis=0).astype(jnp.float32)
    edge = jnp.sum(jnp.where(is_edge, jnp.arange(len(KNOWN))[None, :], 0), axis=1)
    mine = date_pairs[:, 0] // local_dates == myself
    matches = (assignment[None, :] // owners == jnp.arange(owners)[:, None]) & mine[None, :]
    slot = jnp.sum(jnp.where(matches, edge[None, :], 0), axis=1)
    sign = jnp.sum(jnp.where(matches, jnp.where(first < second, 1.0, -1.0)[None, :], 0.0), axis=1)
    return slot, sign, count


def row_groups(tiles, cells):
    held = [t * TILE + r for t in tiles for r in range(TILE)]
    groups, owners = [], []
    for m in range(cells):
        local = [n for n, row in enumerate(held) if row // ALOOK == m]
        if local:
            groups.append((local[0], local[-1] + 1))
            owners.append(m)
    return groups, owners


def on_device(images, date_pairs, assignment):
    owners = lax.axis_size("date")
    myself = lax.axis_index("date")
    _, local_dates, rows, columns = images.shape
    cells = rows // ALOOK
    cell_count = cells * (columns // RLOOK)
    block = 2 * cell_count // LANES
    pieces = ((0,) + tuple(range(3, rows // TILE)), (1, 2))

    arrived = []
    for tiles in pieces:
        to_above, to_below = packed_rows(images, tiles)
        arrived.append((shifted(to_above, "date", 1), shifted(to_below, "date", -1)))

    look_matrix = (
        jnp.arange(2 * COLUMNS)[:, None] // RLOOK == jnp.arange(LANES)[None, :]
    ).astype(jnp.bfloat16)
    slot, sign, count = pair_tables(date_pairs, assignment, myself, owners, local_dates)

    own_places = {
        2 + d: [(0, d, t * TILE) for t in range(rows // TILE)] for d in range(local_dates)
    }
    inner = looked_products(
        INNER,
        INNER_POWERS,
        [(images, (2, local_dates, rows), (0, 0, 0), 0)],
        own_places,
        row_groups(range(rows // TILE), cells)[0],
        rows,
        columns,
        look_matrix,
    )
    layout = [[None, None] for _ in range(cells)]
    outer = []
    for piece, (tiles, (below, above)) in enumerate(zip(pieces, arrived)):
        size = len(tiles)
        sources = [
            (below, (2, 2, size * TILE), (0, 0, 0), 0),
            (above, (2, 2, size * TILE), (0, 0, 0), 0),
        ] + [(images, (2, local_dates, TILE), (0, 0, t), 0) for t in tiles]
        places = {d: [(0, d, t * TILE) for t in range(size)] for d in range(2)}
        places |= {6 + d: [(1, d, t * TILE) for t in range(size)] for d in range(2)}
        places |= {2 + d: [(2 + t, d, 0) for t in range(size)] for d in range(local_dates)}
        groups, where = row_groups(tiles, cells)
        for n, m in enumerate(where):
            layout[m][piece] = n
        outer.append(
            looked_products(
                OUTER, OUTER_POWERS, sources, places, groups, size * TILE, columns, look_matrix
            )
        )
    before = shifted(jnp.concatenate([inner[cells - 1 :], outer[0][-1:]], axis=1), "strip", 1)
    after = shifted(jnp.concatenate([inner[:1], outer[0][:1]], axis=1), "strip", -1)
    own, low, up = coherences(layout, inner, *outer, before, after)
    tables = (own, low, up, shifted(up, "date", 1), shifted(low, "date", -1))
    outgoing = slots_of(slot, sign, tables, owners, block)
    table = lax.all_to_all(outgoing, "date", split_axis=0, concat_axis=0, tiled=True)
    sums = sums_of(count, tables, local_dates, cell_count)
    return (as_table(table, cell_count), sums)


def solution(mesh):
    return jax.shard_map(
        on_device,
        mesh=mesh,
        in_specs=(P(None, "date", "strip", None), P(), P()),
        out_specs=(P(None, "date", "strip"), P(None, "date", "strip")),
        check_vma=False,
    )
```

time: 325 us -> 95.2 us (0.29)
  other arithmetic: 113 us -> 1.67 us
  local copies, waits for them, and re-layouts: 81.6 us -> 2.89 us
  waiting for transfers between devices: 81.4 us -> 19.8 us
  Pallas kernels: 0 us -> 36.6 us
  matrix products: 12.3 us -> 0 us
    convert_element_type x5 -> x2, other arithmetic: 71.1 us -> 1.19 us  [the longest x1 1.19 us: on_device(): look_matrix = (jnp.arange(2 * COLUMNS)[:, None] // RLOOK == jnp.arange(LA...]
    ppermute x6 -> x8, waiting for transfers between devices: 64.8 us -> 9.48 us  [shifted(): lax.ppermute(value, axis, [(source, source + steps) for source in range(f...]
    gather x6 -> x0, local copies, waits for them, and re-layouts: 52.9 us -> none  [the longest x2 26 us: form(): back_images = jnp.take(extended, trail_index, axis=1).astype(jnp.float32)]
    pallas_call x0 -> x9, Pallas kernels: none -> 36.6 us  [the longest x3 27.2 us: looked_products(): pl.pallas_call(functools.partial(products_kernel, edges, powers, places,...]
    another operation x2 -> x0, other arithmetic: 35.4 us -> none
    dot_general x5 -> x0, matrix products: 12.3 us -> none  [the longest x3 11.4 us: range_looks(): jnp.einsum('...ar,rl->...al', pixels, look_matrix, preferred_element_type...]
    convert_element_type x1 -> x0, local copies, waits for them, and re-layouts: 8.57 us -> none  [on_device(): power = (jnp.square(extended[0].astype(jnp.float32)) + jnp.square(extende...]
    unnamed x30 -> x10, local copies, waits for them, and re-layouts: 11.1 us -> 2.88 us
  transfers between devices with their start and end apart: 7 -> 9, of which waited for: 3 -> 4; matrix products, arithmetic and copies ran while one was open for 5% -> 2% of each run, Pallas kernels for 0% -> 33%
where the time goes in v2:
time: 95.2 us; the launch traced here: 94.7 us
  Pallas kernels  36.6 us (38%)
  starting transfers between devices  32.8 us (34%)
  waiting for transfers between devices  19.8 us (21%)
  local copies, waits for them, and re-layouts  2.89 us (3%)
  other arithmetic  1.67 us (2%)
    pallas_call x3, Pallas kernels, looked_products(): pl.pallas_call(functools.partial(products_kernel, edges, powers, places,...  27.2 us
    ppermute x8, starting transfers between devices, shifted(): lax.ppermute(value, axis, [(source, source + steps) for source in range(f...  23.3 us
    all_to_all x1, waiting for transfers between devices, on_device(): lax.all_to_all(outgoing, 'date', split_axis=0, concat_axis=0, tiled=True)  10.4 us
    all_to_all x1, starting transfers between devices, on_device(): lax.all_to_all(outgoing, 'date', split_axis=0, concat_axis=0, tiled=True)  9.48 us
    ppermute x8, waiting for transfers between devices, shifted(): lax.ppermute(value, axis, [(source, source + steps) for source in range(f...  9.48 us
    pallas_call x2, Pallas kernels, packed_rows(): pl.pallas_call(functools.partial(pack_kernel, parts), out_shape=[jax.Shap...  4.99 us
    unnamed x10, local copies, waits for them, and re-layouts  2.88 us
  transfers between devices with their start and end apart: 9, of which 4 were waited for; matrix products, arithmetic and copies ran while one was open for 2% of the time, Pallas kernels for 33%

profile of v2, /device:TPU:9, one launch (start us, length us, event | category | flops | bytes accessed | tf_op | source)
XLA Modules:
  0.0 94.7 jit_solution(8442638505237195867)
XLA Ops:
  0.6 0.0 copy-start
  0.6 2.9 %copy-done = bf16[2,4,80,5120]{3,2,1,0:T(8,128)(2,1)S(1)} copy-done((bf16[2,4,80,5120]{3,2,1,0:T(8,128)(2,1)S(1)}, bf16[2,4,80,5120]{3,2,1,0:T(8,128)(2,1)}, u32[]{:S(2)}) %copy-start) | copy-done | bytes 6553624
  3.5 2.7 %shard_map.60 = (bf16[2,2,48,5120]{3,2,1,0:T(8,128)(2,1)}, bf16[2,2,48,5120]{3,2,1,0:T(8,128)(2,1)}) custom-call(bf16[2,4,80,5120]{3,2,1,0:T(8,128)(2,1)S(1)} %copy-done, bf16[2,4,80,5120]{3,2,1,0:T(8,128)(2,1)S(1)} %copy-done, bf16[2,4,80,5120]{3,2,1,0:T(8,128)(2,1)S(1)} %copy-done, bf16[2,4,80,5120]{3,2,1,0:T(8,128)(2,1)S(1)} %copy-done, ...), custom_call_target="tpu_custom_call" | custom-call | tf_op jit(solution)/shard_map/pallas_call | solution.py:110
  6.2 4.1 %collective-permute-start = (bf16[2,2,48,5120]{3,2,1,0:T(8,128)(2,1)}, bf16[2,2,48,5120]{3,2,1,0:T(8,128)(2,1)S(1)}, u32[]{:S(2)}, u32[]{:S(2)}) collective-permute-start(bf16[2,2,48,5120]{3,2,1,0:T(8,128)(2,1)} %get-tuple-element.9), channel_id=1, source_target_pairs={{0,16},{16,32},{32,48},{48,64},{64,80},{80,96},{96,112},{112,128},... | collective-permute-start | bytes 5898248 | tf_op jit(solution)/shard_map/ppermute | solution.py:279
  10.3 0.0 copy-start.1
  10.3 0.0 copy-start.4
  10.3 1.9 %collective-permute-start.1 = (bf16[2,2,48,5120]{3,2,1,0:T(8,128)(2,1)}, bf16[2,2,48,5120]{3,2,1,0:T(8,128)(2,1)}, u32[]{:S(2)}, u32[]{:S(2)}) collective-permute-start(bf16[2,2,48,5120]{3,2,1,0:T(8,128)(2,1)} %get-tuple-element.10), channel_id=1, source_target_pairs={{16,0},{32,16},{48,32},{64,48},{80,64},{96,80},{112,96},{128,112},... | collective-permute-start | bytes 5898248 | tf_op jit(solution)/shard_map/ppermute | solution.py:279
  12.2 2.3 %shard_map.62 = (bf16[2,2,32,5120]{3,2,1,0:T(8,128)(2,1)}, bf16[2,2,32,5120]{3,2,1,0:T(8,128)(2,1)}) custom-call(bf16[2,4,80,5120]{3,2,1,0:T(8,128)(2,1)S(1)} %copy-done, bf16[2,4,80,5120]{3,2,1,0:T(8,128)(2,1)S(1)} %copy-done, bf16[2,4,80,5120]{3,2,1,0:T(8,128)(2,1)S(1)} %copy-done, bf16[2,4,80,5120]{3,2,1,0:T(8,128)(2,1)S(1)} %copy-done), custom_call_target="tpu_custom_call" | custom-call | tf_op jit(solution)/shard_map/pallas_call | solution.py:110
  14.5 3.6 %collective-permute-start.2 = (bf16[2,2,32,5120]{3,2,1,0:T(8,128)(2,1)}, bf16[2,2,32,5120]{3,2,1,0:T(8,128)(2,1)}, u32[]{:S(2)}, u32[]{:S(2)}) collective-permute-start(bf16[2,2,32,5120]{3,2,1,0:T(8,128)(2,1)} %get-tuple-element.11), channel_id=1, source_target_pairs={{0,16},{16,32},{32,48},{48,64},{64,80},{80,96},{96,112},{112,128},... | collective-permute-start | bytes 3932168 | tf_op jit(solution)/shard_map/ppermute | solution.py:279
  18.2 1.9 %collective-permute-start.3 = (bf16[2,2,32,5120]{3,2,1,0:T(8,128)(2,1)}, bf16[2,2,32,5120]{3,2,1,0:T(8,128)(2,1)}, u32[]{:S(2)}, u32[]{:S(2)}) collective-permute-start(bf16[2,2,32,5120]{3,2,1,0:T(8,128)(2,1)} %get-tuple-element.12), channel_id=1, source_target_pairs={{16,0},{32,16},{48,32},{64,48},{80,64},{96,80},{112,96},{128,112},... | collective-permute-start | bytes 3932168 | tf_op jit(solution)/shard_map/ppermute | solution.py:279
  20.1 0.0 copy-done.1
  20.2 1.2 %fusion.refs_1_.refs_5_.refs_4_ = bf16[2560,128]{1,0:T(8,128)(2,1)S(1)} fusion(s32[2560]{0:T(1024)S(1)} %add_select_fusion), kind=kLoop, calls=%fused_computation.1 | loop fusion | flops 655360 | bytes 665600 | tf_op jit(solution)/shard_map/convert_element_type | solution.py:326
  21.4 0.0 copy-done.4
  21.4 10.2 %shard_map.59.refs_0_ = f32[16,16,256]{2,1,0:T(8,128)S(1)} custom-call(bf16[2,4,80,5120]{3,2,1,0:T(8,128)(2,1)} %refs_3_.7, bf16[2560,128]{1,0:T(8,128)(2,1)S(1)} %fusion.refs_1_.refs_5_.refs_4_), custom_call_target="tpu_custom_call" | custom-call | tf_op jit(solution)/shard_map/pallas_call | solution.py:85
  31.6 0.0 copy-start.2
  31.6 0.0 copy-start.3
  31.7 0.5 collective-permute-done.refs_0_
  32.1 4.4 %collective-permute-done.1.refs_1_ = bf16[2,2,48,5120]{3,2,1,0:T(8,128)(2,1)} collective-permute-done((bf16[2,2,48,5120]{3,2,1,0:T(8,128)(2,1)}, bf16[2,2,48,5120]{3,2,1,0:T(8,128)(2,1)}, u32[]{:S(2)}, u32[]{:S(2)}) %collective-permute-start.1) | collective-permute-done | bytes 1966112 | tf_op jit(solution)/shard_map/ppermute | solution.py:279
  36.6 9.7 %shard_map.61.refs_1_ = f32[11,24,256]{2,1,0:T(8,128)S(1)} custom-call(bf16[2,2,48,5120]{3,2,1,0:T(8,128)(2,1)S(1)} %collective-permute-done.refs_0_, bf16[2,2,48,5120]{3,2,1,0:T(8,128)(2,1)} %collective-permute-done.1.refs_1_, bf16[2,4,80,5120]{3,2,1,0:T(8,128)(2,1)} %refs_3_.7, bf16[2,4,80,5120]{3,2,1,0:T(8,128)(2,1)} %refs_3_.7, ...), custom_call_target="tpu_custom_call" | custom-call | tf_op jit(solution)/shard_map/pallas_call | solution.py:85
  46.3 3.1 %collective-permute-start.4 = (f32[1,40,256]{2,1,0:T(8,128)S(1)}, f32[1,40,256]{2,1,0:T(8,128)S(1)}, u32[]{:S(2)}, u32[]{:S(2)}) collective-permute-start(f32[1,40,256]{2,1,0:T(8,128)S(1)} %pad_maximum_fusion), channel_id=1, source_target_pairs={{0,1},{1,2},{2,3},{3,4},{4,5},{5,6},{6,7},{7,8},{8,9},{9,10},{10,1... | collective-permute-start | bytes 122888 | tf_op jit(solution)/shard_map/ppermute | solution.py:279
  49.4 4.3 %collective-permute-start.5 = (f32[1,40,256]{2,1,0:T(8,128)S(1)}, f32[1,40,256]{2,1,0:T(8,128)S(1)}, u32[]{:S(2)}, u32[]{:S(2)}) collective-permute-start(f32[1,40,256]{2,1,0:T(8,128)S(1)} %pad_maximum_fusion.1), channel_id=1, source_target_pairs={{1,0},{2,1},{3,2},{4,3},{5,4},{6,5},{7,6},{8,7},{9,8},{10,9},{11,1... | collective-permute-start | bytes 122888 | tf_op jit(solution)/shard_map/ppermute | solution.py:279
  53.7 0.0 copy-done.2
  53.7 0.0 copy-done.3
  53.7 0.2 convert_reduce_fusion
  53.9 0.0 collective-permute-done.2.refs_0_
  53.9 0.0 collective-permute-done.3.refs_1_
  53.9 7.3 %shard_map.63.refs_2_ = f32[7,24,256]{2,1,0:T(8,128)S(1)} custom-call(bf16[2,2,32,5120]{3,2,1,0:T(8,128)(2,1)} %collective-permute-done.2.refs_0_, bf16[2,2,32,5120]{3,2,1,0:T(8,128)(2,1)} %collective-permute-done.3.refs_1_, bf16[2,4,80,5120]{3,2,1,0:T(8,128)(2,1)} %refs_3_.7, bf16[2,4,80,5120]{3,2,1,0:T(8,128)(2,1)} %refs_3_.7, ...), custom_call_target="tpu_custom_call" | custom-call | tf_op jit(solution)/shard_map/pallas_call | solution.py:85
  61.3 0.0 collective-permute-done.4.refs_3_
  61.3 0.0 collective-permute-done.5.refs_4_
  61.3 0.5 shard_map.64
  61.8 2.3 %collective-permute-start.6 = (f32[320,128]{1,0:T(8,128)S(1)}, f32[320,128]{1,0:T(8,128)S(1)}, u32[]{:S(2)}, u32[]{:S(2)}) collective-permute-start(f32[320,128]{1,0:T(8,128)S(1)} %get-tuple-element.15.refs_2_), channel_id=1, source_target_pairs={{0,16},{16,32},{32,48},{48,64},{64,80},{80,96},{96,112},{112,128},... | collective-permute-start | bytes 491528 | tf_op jit(solution)/shard_map/ppermute | solution.py:279
  64.2 2.0 %collective-permute-start.7 = (f32[320,128]{1,0:T(8,128)S(1)}, f32[320,128]{1,0:T(8,128)S(1)}, u32[]{:S(2)}, u32[]{:S(2)}) collective-permute-start(f32[320,128]{1,0:T(8,128)S(1)} %get-tuple-element.14.refs_1_), channel_id=1, source_target_pairs={{16,0},{32,16},{48,32},{64,48},{80,64},{96,80},{112,96},{128,112},... | collective-permute-start | bytes 491528 | tf_op jit(solution)/shard_map/ppermute | solution.py:279
  66.2 0.1 select_reduce_fusion.2.slot_ref
  66.3 0.1 select_reduce_fusion.1.sign_ref
  66.4 0.0 collective-permute-done.6.refs_3_
  66.4 4.6 %collective-permute-done.7.refs_4_ = f32[320,128]{1,0:T(8,128)S(1)} collective-permute-done((f32[320,128]{1,0:T(8,128)S(1)}, f32[320,128]{1,0:T(8,128)S(1)}, u32[]{:S(2)}, u32[]{:S(2)}) %collective-permute-start.7) | collective-permute-done | bytes 163872 | tf_op jit(solution)/shard_map/ppermute | solution.py:279
  71.0 1.4 %shard_map.65 = s16[16,64,128]{2,1,0:T(8,128)(2,1)} custom-call(s32[16]{0:T(128)S(1)} %select_reduce_fusion.2.slot_ref, f32[16]{0:T(128)S(1)} %select_reduce_fusion.1.sign_ref, f32[384,128]{1,0:T(8,128)S(1)} %get-tuple-element.13.refs_0_, f32[320,128]{1,0:T(8,128)S(1)} %get-tuple-element.14.refs_1_, f32[320,128]{1,0:T(8,128)S(1)} %get-tuple-element.15.refs_2_, ...), custom_call_target="tpu_custom_call" | custom-call | tf_op jit(solution)/shard_map/pallas_call | solution.py:205
  72.3 9.5 %all-to-all-start = ((s16[16,64,128]{2,1,0:T(8,128)(2,1)}), s16[16,64,128]{2,1,0:T(8,128)(2,1)S(1)}, u32[]{:S(2)}, u32[]{:S(2)}) async-start(s16[16,64,128]{2,1,0:T(8,128)(2,1)} %shard_map.65), calls=%async_computation | async-start | bytes 524288 | tf_op jit(solution)/shard_map/all_to_all | solution.py:366
  81.8 1.3 %shard_map.67 = f32[2,4,4096]{2,1,0:T(4,128)} custom-call(f32[26]{0:T(128)S(1)} %convert_element_type.15.count_ref, f32[384,128]{1,0:T(8,128)S(1)} %get-tuple-element.13.refs_0_, f32[320,128]{1,0:T(8,128)S(1)} %get-tuple-element.14.refs_1_, f32[320,128]{1,0:T(8,128)S(1)} %get-tuple-element.15.refs_2_, f32[320,128]{1,0:T(8,128)S(1)} %collective-permute-done.6.refs_3_, ...), custom_call_target="tpu_custom_call" | custom-call | tf_op jit(solution)/shard_map/pallas_call | solution.py:243
  83.2 10.4 %all-to-all-done.arrived_ref = s16[16,64,128]{2,1,0:T(8,128)(2,1)S(1)} async-done(((s16[16,64,128]{2,1,0:T(8,128)(2,1)}), s16[16,64,128]{2,1,0:T(8,128)(2,1)S(1)}, u32[]{:S(2)}, u32[]{:S(2)}) %all-to-all-start) | async-done | bytes 262176 | tf_op jit(solution)/shard_map/all_to_all | solution.py:366
  93.5 1.1 %shard_map.66 = f32[2,16,4096]{2,1,0:T(8,128)} custom-call(s16[16,64,128]{2,1,0:T(8,128)(2,1)S(1)} %all-to-all-done.arrived_ref), custom_call_target="tpu_custom_call" | custom-call | tf_op jit(solution)/shard_map/pallas_call | solution.py:268
  (10 shorter events, 0.1 us)
Async XLA Ops:
  0.6 2.9 %copy-start = (bf16[2,4,80,5120]{3,2,1,0:T(8,128)(2,1)S(1)}, bf16[2,4,80,5120]{3,2,1,0:T(8,128)(2,1)}, u32[]{:S(2)}) copy-start(bf16[2,4,80,5120]{3,2,1,0:T(8,128)(2,1)} %refs_3_.7) | copy-start | bytes 19660804
  6.2 26.0 %collective-permute-start = (bf16[2,2,48,5120]{3,2,1,0:T(8,128)(2,1)}, bf16[2,2,48,5120]{3,2,1,0:T(8,128)(2,1)S(1)}, u32[]{:S(2)}, u32[]{:S(2)}) collective-permute-start(bf16[2,2,48,5120]{3,2,1,0:T(8,128)(2,1)} %get-tuple-element.9), channel_id=1, source_target_pairs={{0,16},{16,32},{32,48},{48,64},{64,80},{80,96},{96,112},{112,128},... | collective-permute-start | bytes 5898248 | tf_op jit(solution)/shard_map/ppermute | solution.py:279
  10.3 9.9 %copy-start.1 = (s32[128,2]{0,1:T(2,128)S(1)}, s32[128,2]{0,1:T(2,128)}, u32[]{:S(2)}) copy-start(s32[128,2]{0,1:T(2,128)} %param.5) | copy-start | bytes 3076
  10.3 11.1 %copy-start.4 = (s32[128]{0:T(128)S(1)}, s32[128]{0:T(128)}, u32[]{:S(2)}) copy-start(s32[128]{0:T(128)} %param.6) | copy-start | bytes 1540
  10.3 26.3 %collective-permute-start.1 = (bf16[2,2,48,5120]{3,2,1,0:T(8,128)(2,1)}, bf16[2,2,48,5120]{3,2,1,0:T(8,128)(2,1)}, u32[]{:S(2)}, u32[]{:S(2)}) collective-permute-start(bf16[2,2,48,5120]{3,2,1,0:T(8,128)(2,1)} %get-tuple-element.10), channel_id=1, source_target_pairs={{16,0},{32,16},{48,32},{64,48},{80,64},{96,80},{112,96},{128,112},... | collective-permute-start | bytes 5898248 | tf_op jit(solution)/shard_map/ppermute | solution.py:279
  14.5 39.4 %collective-permute-start.2 = (bf16[2,2,32,5120]{3,2,1,0:T(8,128)(2,1)}, bf16[2,2,32,5120]{3,2,1,0:T(8,128)(2,1)}, u32[]{:S(2)}, u32[]{:S(2)}) collective-permute-start(bf16[2,2,32,5120]{3,2,1,0:T(8,128)(2,1)} %get-tuple-element.11), channel_id=1, source_target_pairs={{0,16},{16,32},{32,48},{48,64},{64,80},{80,96},{96,112},{112,128},... | collective-permute-start | bytes 3932168 | tf_op jit(solution)/shard_map/ppermute | solution.py:279
  18.2 35.7 %collective-permute-start.3 = (bf16[2,2,32,5120]{3,2,1,0:T(8,128)(2,1)}, bf16[2,2,32,5120]{3,2,1,0:T(8,128)(2,1)}, u32[]{:S(2)}, u32[]{:S(2)}) collective-permute-start(bf16[2,2,32,5120]{3,2,1,0:T(8,128)(2,1)} %get-tuple-element.12), channel_id=1, source_target_pairs={{16,0},{32,16},{48,32},{64,48},{80,64},{96,80},{112,96},{128,112},... | collective-permute-start | bytes 3932168 | tf_op jit(solution)/shard_map/ppermute | solution.py:279
  31.6 22.1 %copy-start.2 = (s32[26]{0:T(128)S(1)}, s32[26]{0:T(128)}, u32[]{:S(2)}) copy-start(s32[26]{0:T(128)} %constant.57) | copy-start | bytes 316
  31.6 22.1 %copy-start.3 = (s32[26]{0:T(128)S(1)}, s32[26]{0:T(128)}, u32[]{:S(2)}) copy-start(s32[26]{0:T(128)} %constant.59) | copy-start | bytes 316
  46.3 15.0 %collective-permute-start.4 = (f32[1,40,256]{2,1,0:T(8,128)S(1)}, f32[1,40,256]{2,1,0:T(8,128)S(1)}, u32[]{:S(2)}, u32[]{:S(2)}) collective-permute-start(f32[1,40,256]{2,1,0:T(8,128)S(1)} %pad_maximum_fusion), channel_id=1, source_target_pairs={{0,1},{1,2},{2,3},{3,4},{4,5},{5,6},{6,7},{7,8},{8,9},{9,10},{10,1... | collective-permute-start | bytes 122888 | tf_op jit(solution)/shard_map/ppermute | solution.py:279
  49.4 11.9 %collective-permute-start.5 = (f32[1,40,256]{2,1,0:T(8,128)S(1)}, f32[1,40,256]{2,1,0:T(8,128)S(1)}, u32[]{:S(2)}, u32[]{:S(2)}) collective-permute-start(f32[1,40,256]{2,1,0:T(8,128)S(1)} %pad_maximum_fusion.1), channel_id=1, source_target_pairs={{1,0},{2,1},{3,2},{4,3},{5,4},{6,5},{7,6},{8,7},{9,8},{10,9},{11,1... | collective-permute-start | bytes 122888 | tf_op jit(solution)/shard_map/ppermute | solution.py:279
  61.8 4.6 %collective-permute-start.6 = (f32[320,128]{1,0:T(8,128)S(1)}, f32[320,128]{1,0:T(8,128)S(1)}, u32[]{:S(2)}, u32[]{:S(2)}) collective-permute-start(f32[320,128]{1,0:T(8,128)S(1)} %get-tuple-element.15.refs_2_), channel_id=1, source_target_pairs={{0,16},{16,32},{32,48},{48,64},{64,80},{80,96},{96,112},{112,128},... | collective-permute-start | bytes 491528 | tf_op jit(solution)/shard_map/ppermute | solution.py:279
  64.2 6.8 %collective-permute-start.7 = (f32[320,128]{1,0:T(8,128)S(1)}, f32[320,128]{1,0:T(8,128)S(1)}, u32[]{:S(2)}, u32[]{:S(2)}) collective-permute-start(f32[320,128]{1,0:T(8,128)S(1)} %get-tuple-element.14.refs_1_), channel_id=1, source_target_pairs={{16,0},{32,16},{48,32},{64,48},{80,64},{96,80},{112,96},{128,112},... | collective-permute-start | bytes 491528 | tf_op jit(solution)/shard_map/ppermute | solution.py:279
  72.3 21.2 %all-to-all-start = ((s16[16,64,128]{2,1,0:T(8,128)(2,1)}), s16[16,64,128]{2,1,0:T(8,128)(2,1)S(1)}, u32[]{:S(2)}, u32[]{:S(2)}) async-start(s16[16,64,128]{2,1,0:T(8,128)(2,1)} %shard_map.65), calls=%async_computation | async-start | bytes 524288 | tf_op jit(solution)/shard_map/all_to_all | solution.py:366

commit v3 on v2

v3 whole, which is shorter than its diff:
```python
import functools

import jax
import jax.numpy as jnp
from jax import lax
from jax.experimental import pallas as pl
from jax.experimental.pallas import tpu as pltpu
from jax.sharding import PartitionSpec as P

ALOOK = 5
RLOOK = 20
LANES = 128
TILE = 16
COLUMNS = 1280
CHUNK = 256
FIXED = 32000.0
EPS_POWER = 1e-06
MIB = 2**20

INNER = ((2, 3), (2, 4), (2, 5), (3, 4), (3, 5), (4, 5))
LOWER = ((0, 4), (1, 4), (1, 5), (1, 2), (1, 3))
UPPER = ((2, 6), (3, 6), (3, 7), (4, 6), (4, 7))
OUTER = LOWER + UPPER
FROM_BELOW = tuple((i - 4, j - 4) for i, j in UPPER)
FROM_ABOVE = tuple((i + 4, j + 4) for i, j in LOWER)
KNOWN = INNER + OUTER + FROM_BELOW + FROM_ABOVE
INNER_POWERS = (2, 3, 4, 5)
OUTER_POWERS = (0, 1, 6, 7)


def products_kernel(edges, powers, places, groups, *refs):
    odd_device = refs[0][0] == 1
    out_ref, look_ref, even_ref, odd_ref, acc_ref = refs[-5:]
    total = 2 * len(edges) + len(powers)
    rows = acc_ref.shape[0] // total
    step = pl.program_id(0)
    used = sorted({k for e in edges for k in e} | set(powers))
    buffers = (even_ref, odd_ref)

    @pl.when(step == 0)
    def _():
        column = lax.broadcasted_iota(jnp.int32, look_ref.shape, 0)
        begin = lax.broadcasted_iota(jnp.int32, look_ref.shape, 1) * RLOOK
        inside = (column >= begin) & (column < begin + RLOOK)
        look_ref[...] = inside.astype(jnp.float32).astype(jnp.bfloat16)

    def form(chunk):
        for part in range(CHUNK // LANES):
            lane = slice(chunk * CHUNK + part * LANES, chunk * CHUNK + (part + 1) * LANES)
            out_lane = slice(part * LANES, (part + 1) * LANES)
            for tile in range(rows // TILE):
                pixel = {}
                for k in used:
                    sources, date, row = places[k][tile]
                    pixel[k] = []
                    for c in (0, 1):
                        found = [refs[1 + s][c, date, row : row + TILE, lane] for s in sources]
                        if len(found) == 2:
                            found = [jnp.where(odd_device, found[1], found[0])]
                        pixel[k].append(found[0].astype(jnp.float32))
                results = []
                for i, j in edges:
                    results.append(pixel[i][0] * pixel[j][0] + pixel[i][1] * pixel[j][1])
                for i, j in edges:
                    results.append(pixel[i][1] * pixel[j][0] - pixel[i][0] * pixel[j][1])
                for k in powers:
                    results.append(pixel[k][0] * pixel[k][0] + pixel[k][1] * pixel[k][1])
                for p, value in enumerate(results):
                    first = p * rows + tile * TILE
                    buffers[chunk % 2][first : first + TILE, out_lane] = value.astype(jnp.bfloat16)

    def add_looks(chunk):
        row = pl.multiple_of(step % 2 * COLUMNS + chunk * CHUNK, CHUNK)
        part = jnp.dot(
            buffers[chunk % 2][...],
            look_ref[pl.ds(row, CHUNK), :],
            preferred_element_type=jnp.float32,
        )
        if chunk == 0:
            acc_ref[...] = part + jnp.where(step % 2 == 1, acc_ref[...], 0.0)
        else:
            acc_ref[...] += part

    chunks = COLUMNS // CHUNK
    form(0)
    for chunk in range(chunks):
        if chunk + 1 < chunks:
            form(chunk + 1)
        add_looks(chunk)

    @pl.when(step % 2 == 1)
    def _():
        for m, (first, last) in enumerate(groups):
            for p in range(0, total, 8):
                size = min(8, total - p)
                value = acc_ref[pl.ds(p * rows + first, size, stride=rows), :]
                for row in range(first + 1, last):
                    value += acc_ref[pl.ds(p * rows + row, size, stride=rows), :]
                out_ref[m, p : p + size, :] = value


def looked_products(odd, edges, powers, sources, places, groups, rows, columns):
    total = 2 * len(edges) + len(powers)

    def spec(block, index):
        return pl.BlockSpec(block + (COLUMNS,), lambda i: index + (i,))

    return pl.pallas_call(
        functools.partial(products_kernel, edges, powers, places, groups),
        out_shape=jax.ShapeDtypeStruct((len(groups), total, columns // RLOOK), jnp.float32),
        grid=(columns // COLUMNS,),
        in_specs=[pl.BlockSpec(memory_space=pltpu.SMEM)] + [spec(*s[1:]) for s in sources],
        out_specs=pl.BlockSpec((len(groups), total, LANES), lambda i: (0, 0, i // 2)),
        scratch_shapes=[
            pltpu.VMEM((2 * COLUMNS, LANES), jnp.bfloat16),
            pltpu.VMEM((total * rows, CHUNK), jnp.bfloat16),
            pltpu.VMEM((total * rows, CHUNK), jnp.bfloat16),
            pltpu.VMEM((total * rows, LANES), jnp.float32),
        ],
        compiler_params=pltpu.CompilerParams(vmem_limit_bytes=48 * MIB),
    )(odd, *[s[0] for s in sources])


def pack_kernel(runs, odd_ref, images_ref, across_ref, beside_ref, held_ref, in_sems, out_sems):
    first = (2 * odd_ref[0], 2 - 2 * odd_ref[0])
    loads, stores = [], []
    for n, out in enumerate((across_ref, beside_ref)):
        for c in range(2):
            for row, target, size in runs:
                held = held_ref.at[n, c, :, target : target + size, :]
                loads.append(
                    pltpu.make_async_copy(
                        images_ref.at[c, pl.ds(first[n], 2), row : row + size, :],
                        held,
                        in_sems.at[len(loads)],
                    )
                )
                stores.append(
                    pltpu.make_async_copy(
                        held, out.at[c, :, target : target + size, :], out_sems.at[len(stores)]
                    )
                )
    for load in loads:
        load.start()
    for load, store in zip(loads, stores):
        load.wait()
        store.start()
    for store in stores:
        store.wait()


def packed_rows(odd, images, tiles, limit):
    columns = images.shape[3]
    runs = []
    for n, t in enumerate(tiles):
        if runs and runs[-1][0] + runs[-1][2] == t * TILE:
            row, target, size = runs.pop()
            runs.append((row, target, size + TILE))
        else:
            runs.append((t * TILE, n * TILE, TILE))
    return pl.pallas_call(
        functools.partial(pack_kernel, runs),
        out_shape=[jax.ShapeDtypeStruct((2, 2, len(tiles) * TILE, columns), images.dtype)] * 2,
        in_specs=[pl.BlockSpec(memory_space=pltpu.SMEM), pl.BlockSpec(memory_space=pl.ANY)],
        out_specs=[pl.BlockSpec(memory_space=pl.ANY)] * 2,
        scratch_shapes=[
            pltpu.VMEM((2, 2, 2, len(tiles) * TILE, columns), images.dtype),
            pltpu.SemaphoreType.DMA((4 * len(runs),)),
            pltpu.SemaphoreType.DMA((4 * len(runs),)),
        ],
        compiler_params=pltpu.CompilerParams(vmem_limit_bytes=limit * MIB),
    )(odd, images)


def coherence_kernel(layout, *refs):
    odd_ref, inner_ref, first_ref, second_ref, before_ref, after_ref = refs[:6]
    outs = refs[6:9]
    across_ref, beside_ref = refs[9:]
    cells, n_first, width = inner_ref.shape
    n_in, n_out = len(INNER), len(OUTER)
    halves = width // LANES
    block = 2 * cells * halves

    def inner_at(m):
        if m < 0:
            return before_ref[0, :n_first]
        if m >= cells:
            return after_ref[0, :n_first]
        return inner_ref[m]

    def outer_at(m):
        if m < 0:
            return before_ref[0, n_first:]
        if m >= cells:
            return after_ref[0, n_first:]
        return sum(ref[n] for ref, n in zip((first_ref, second_ref), layout[m]) if n is not None)

    inners = [inner_at(m) for m in range(-1, cells + 1)]
    outers = [outer_at(m) for m in range(-1, cells + 1)]
    for m in range(cells):
        inner = inners[m] + 2.0 * inners[m + 1] + inners[m + 2]
        outer = outers[m] + 2.0 * outers[m + 1] + outers[m + 2]
        power = {}
        for n, k in enumerate(INNER_POWERS):
            power[k] = inner[2 * n_in + n : 2 * n_in + n + 1]
        for n, k in enumerate(OUTER_POWERS):
            power[k] = outer[2 * n_out + n : 2 * n_out + n + 1]
        for out, values, edges, start, count in (
            (outs[0], inner, INNER, 0, n_in),
            (outs[1], outer, LOWER, 0, n_out),
            (outs[2], outer, UPPER, len(LOWER), n_out),
        ):
            size = len(edges)
            first = jnp.concatenate([power[i] for i, _ in edges], axis=0)
            second = jnp.concatenate([power[j] for _, j in edges], axis=0)
            scale = lax.rsqrt(first * second + EPS_POWER)
            for part in range(2):
                begin = start + part * count
                value = values[begin : begin + size] * scale
                for h in range(halves):
                    row = (part * cells + m) * halves + h
                    out[pl.ds(row, size, stride=block), :] = value[:, h * LANES : (h + 1) * LANES]

    @pl.when(odd_ref[0] == 0)
    def _():
        across_ref[...] = outs[1][...]
        beside_ref[...] = outs[2][...]

    @pl.when(odd_ref[0] == 1)
    def _():
        across_ref[...] = outs[2][...]
        beside_ref[...] = outs[1][...]


def coherences(layout, odd, inner, first, second, before, after):
    cells, _, width = inner.shape
    block = 2 * cells * (width // LANES)
    vmem = pl.BlockSpec(memory_space=pltpu.VMEM)
    return pl.pallas_call(
        functools.partial(coherence_kernel, layout),
        out_shape=[
            jax.ShapeDtypeStruct((len(e) * block, LANES), jnp.float32)
            for e in (INNER, LOWER, UPPER, LOWER, UPPER)
        ],
        in_specs=[pl.BlockSpec(memory_space=pltpu.SMEM)] + [vmem] * 5,
        compiler_params=pltpu.CompilerParams(vmem_limit_bytes=32 * MIB),
    )(odd, inner, first, second, before, after)


def slots_kernel(odd_ref, slot_ref, sign_ref, *refs):
    out_ref, known_ref = refs[-2:]
    owners, block, _ = out_ref.shape
    start = 0
    own, (across, beside) = refs[:-4], refs[-4:-2]
    for table in own:
        known_ref[start : start + table.shape[0], :] = table[...]
        start += table.shape[0]
    size = across.shape[0]
    across_at = pl.multiple_of(start + odd_ref[0] * size, 8)
    beside_at = pl.multiple_of(start + (1 - odd_ref[0]) * size, 8)
    known_ref[pl.ds(across_at, size), :] = across[...]
    known_ref[pl.ds(beside_at, size), :] = beside[...]
    for o in range(owners):
        row = pl.multiple_of(slot_ref[o] * block, block)
        value = known_ref[pl.ds(row, block), :]
        half = block // 2
        scales = (jnp.abs(sign_ref[o]) * FIXED, sign_ref[o] * FIXED)
        for part in range(2):
            fixed = jnp.round(value[part * half : (part + 1) * half] * scales[part])
            out_ref[o, part * half : (part + 1) * half, :] = fixed.astype(jnp.int32).astype(jnp.int16)


def slots_of(odd, slot, sign, tables, owners, block):
    smem = pl.BlockSpec(memory_space=pltpu.SMEM)
    vmem = pl.BlockSpec(memory_space=pltpu.VMEM)
    return pl.pallas_call(
        slots_kernel,
        out_shape=[
            jax.ShapeDtypeStruct((owners, block, LANES), jnp.int16),
            jax.ShapeDtypeStruct((len(KNOWN) * block, LANES), jnp.float32),
        ],
        in_specs=[smem, smem, smem] + [vmem] * len(tables),
        compiler_params=pltpu.CompilerParams(vmem_limit_bytes=32 * MIB),
    )(odd, slot, sign, *tables)


def sums_kernel(count_ref, known_ref, out_ref, rows_ref):
    parts, dates, cell_count = out_ref.shape
    tiles = cell_count // LANES
    for part in range(parts):
        totals = [jnp.zeros((tiles, LANES), jnp.float32) for _ in range(dates)]
        for e, (low, high) in enumerate(KNOWN):
            row = (e * parts + part) * tiles
            value = known_ref[row : row + tiles, :] * count_ref[e]
            for d, k in enumerate(INNER_POWERS):
                if k == low or (k == high and part == 0):
                    totals[d] = totals[d] + value
                elif k == high:
                    totals[d] = totals[d] - value
        for d in range(dates):
            first = (part * dates + d) * tiles
            rows_ref[first : first + tiles, :] = totals[d]
    for part in range(parts):
        for t in range(tiles):
            out_ref[part, :, t * LANES : (t + 1) * LANES] = rows_ref[
                pl.ds(part * dates * tiles + t, dates, stride=tiles), :
            ]


def sums_of(count, known, local_dates, cell_count):
    smem = pl.BlockSpec(memory_space=pltpu.SMEM)
    vmem = pl.BlockSpec(memory_space=pltpu.VMEM)
    return pl.pallas_call(
        sums_kernel,
        out_shape=jax.ShapeDtypeStruct((2, local_dates, cell_count), jnp.float32),
        in_specs=[smem, vmem],
        scratch_shapes=[pltpu.VMEM((2 * local_dates * cell_count // LANES, LANES), jnp.float32)],
        compiler_params=pltpu.CompilerParams(vmem_limit_bytes=32 * MIB),
    )(count, known)


def table_kernel(arrived_ref, out_ref, rows_ref):
    parts, owners, cell_count = out_ref.shape
    tiles = cell_count // LANES
    for o in range(owners):
        rows_ref[o * parts * tiles : (o + 1) * parts * tiles, :] = arrived_ref[o].astype(
            jnp.int32
        ).astype(jnp.float32) * (1.0 / FIXED)
    for part in range(parts):
        for t in range(tiles):
            out_ref[part, :, t * LANES : (t + 1) * LANES] = rows_ref[
                pl.ds(part * tiles + t, owners, stride=parts * tiles), :
            ]


def as_table(arrived, cell_count):
    owners, block, _ = arrived.shape
    return pl.pallas_call(
        table_kernel,
        out_shape=jax.ShapeDtypeStruct((2, owners, cell_count), jnp.float32),
        scratch_shapes=[pltpu.VMEM((owners * block, LANES), jnp.float32)],
        compiler_params=pltpu.CompilerParams(vmem_limit_bytes=32 * MIB),
    )(arrived)


def shifted(value, axis, steps):
    count = lax.axis_size(axis)
    first, last = (max(0, -steps), min(count, count - steps))
    return lax.ppermute(value, axis, [(source, source + steps) for source in range(first, last)])


def swapped(across, beside):
    count = lax.axis_size("date")
    over = [(i, i + 1) for i in range(1, count - 1, 2)]
    within = [(i, i + 1) for i in range(0, count, 2)]
    return tuple(
        lax.ppermute(value, "date", pairs + [(b, a) for a, b in pairs])
        for value, pairs in ((across, over), (beside, within))
    )


def pair_tables(date_pairs, assignment, myself, owners, local_dates):
    anchor = myself * local_dates - 2
    first = date_pairs[:, 0] - anchor
    second = date_pairs[:, 1] - anchor
    low_date = jnp.minimum(first, second)
    high_date = jnp.maximum(first, second)
    known = jnp.array(KNOWN, jnp.int32)
    is_edge = (low_date[:, None] == known[None, :, 0]) & (high_date[:, None] == known[None, :, 1])
    count = jnp.sum(is_edge, axis=0).astype(jnp.float32)
    edge = jnp.sum(jnp.where(is_edge, jnp.arange(len(KNOWN))[None, :], 0), axis=1)
    mine = date_pairs[:, 0] // local_dates == myself
    matches = (assignment[None, :] // owners == jnp.arange(owners)[:, None]) & mine[None, :]
    slot = jnp.sum(jnp.where(matches, edge[None, :], 0), axis=1)
    sign = jnp.sum(jnp.where(matches, jnp.where(first < second, 1.0, -1.0)[None, :], 0.0), axis=1)
    return slot, sign, count


def row_groups(tiles, cells):
    held = [t * TILE + r for t in tiles for r in range(TILE)]
    groups, owners = [], []
    for m in range(cells):
        local = [n for n, row in enumerate(held) if row // ALOOK == m]
        if local:
            groups.append((local[0], local[-1] + 1))
            owners.append(m)
    return groups, owners


def on_device(images, date_pairs, assignment):
    owners = lax.axis_size("date")
    myself = lax.axis_index("date")
    _, local_dates, rows, columns = images.shape
    cells = rows // ALOOK
    cell_count = cells * (columns // RLOOK)
    pieces = ((0,) + tuple(range(3, rows // TILE)), (1, 2))

    odd = (myself % 2).astype(jnp.int32)[None]

    def sent(source, tiles, limit):
        return swapped(*packed_rows(odd, source, tiles, limit))

    slot, sign, count = pair_tables(date_pairs, assignment, myself, owners, local_dates)
    arrived = [sent(images, pieces[0], 60)]
    own_places = {
        2 + d: [((0,), d, t * TILE) for t in range(rows // TILE)] for d in range(local_dates)
    }
    inner = looked_products(
        odd,
        INNER,
        INNER_POWERS,
        [(images, (2, local_dates, rows), (0, 0, 0))],
        own_places,
        row_groups(range(rows // TILE), cells)[0],
        rows,
        columns,
    )
    later, inner = lax.optimization_barrier((images, inner))
    arrived.append(sent(later, pieces[1], 32))
    layout = [[None, None] for _ in range(cells)]
    outer = []
    for piece, (tiles, (across, beside)) in enumerate(zip(pieces, arrived)):
        size = len(tiles)
        block = (2, 2, size * TILE)
        sources = [(across, block, (0, 0, 0)), (beside, block, (0, 0, 0))]
        sources += [(images, (2, local_dates, TILE), (0, 0, t)) for t in tiles]
        places = {d: [((0, 1), d, t * TILE) for t in range(size)] for d in range(2)}
        places |= {6 + d: [((1, 0), d, t * TILE) for t in range(size)] for d in range(2)}
        places |= {2 + d: [((2 + t,), d, 0) for t in range(size)] for d in range(local_dates)}
        groups, where = row_groups(tiles, cells)
        for n, m in enumerate(where):
            layout[m][piece] = n
        outer.append(
            looked_products(
                odd, OUTER, OUTER_POWERS, sources, places, groups, size * TILE, columns
            )
        )
    before = shifted(jnp.concatenate([inner[cells - 1 :], outer[0][-1:]], axis=1), "strip", 1)
    after = shifted(jnp.concatenate([inner[:1], outer[0][:1]], axis=1), "strip", -1)
    own, low, up, *sides = coherences(layout, odd, inner, *outer, before, after)
    tables = (own, low, up, *swapped(*sides))
    outgoing, known = slots_of(odd, slot, sign, tables, owners, 2 * cell_count // LANES)
    table = lax.all_to_all(outgoing, "date", split_axis=0, concat_axis=0, tiled=True)
    sums = sums_of(count, known, local_dates, cell_count)
    return (as_table(table, cell_count), sums)


def solution(mesh):
    return jax.shard_map(
        on_device,
        mesh=mesh,
        in_specs=(P(None, "date", "strip", None), P(), P()),
        out_specs=(P(None, "date", "strip"), P(None, "date", "strip")),
        check_vma=False,
    )
```

time: 95.2 us -> 88.1 us (0.925)
  local copies, waits for them, and re-layouts: 2.89 us -> 0.04 us
  starting transfers between devices: 32.8 us -> 30.8 us
  other arithmetic: 1.67 us -> 0.47 us
    ppermute x8 -> x2, starting transfers between devices: 23.3 us -> 7.39 us  [shifted(): lax.ppermute(value, axis, [(source, source + steps) for source in range(f...]
    ppermute x0 -> x6, starting transfers between devices: none -> 12.3 us  [swapped(): lax.ppermute(value, 'date', pairs + [(b, a) for a, b in pairs])]
    ppermute x8 -> x2, waiting for transfers between devices: 9.48 us -> 0.01 us  [shifted(): lax.ppermute(value, axis, [(source, source + steps) for source in range(f...]
    ppermute x0 -> x6, waiting for transfers between devices: none -> 9.33 us  [swapped(): lax.ppermute(value, 'date', pairs + [(b, a) for a, b in pairs])]
    unnamed x10, local copies, waits for them, and re-layouts: 2.88 us -> 0.03 us
    all_to_all x1, starting transfers between devices: 9.48 us -> 11.1 us  [on_device(): lax.all_to_all(outgoing, 'date', split_axis=0, concat_axis=0, tiled=True)]
    pallas_call x3, Pallas kernels: 27.2 us -> 25.9 us  [looked_products(): pl.pallas_call(functools.partial(products_kernel, edges, powers, places,...]
    convert_element_type x1 -> x0, other arithmetic: 1.19 us -> none  [on_device(): look_matrix = (jnp.arange(2 * COLUMNS)[:, None] // RLOOK == jnp.arange(LA...]
  transfers between devices with their start and end apart: 9 -> 9, of which waited for: 4 -> 3; matrix products, arithmetic and copies ran while one was open for 2% -> 1% of each run, Pallas kernels for 33% -> 33%
where the time goes in v3:
time: 88.1 us; the launch traced here: 87.8 us
  Pallas kernels  35.8 us (41%)
  starting transfers between devices  30.8 us (35%)
  waiting for transfers between devices  19.7 us (22%)
  between operations  0.93 us (1%)
    pallas_call x3, Pallas kernels, looked_products(): pl.pallas_call(functools.partial(products_kernel, edges, powers, places,...  25.9 us
    ppermute x6, starting transfers between devices, swapped(): lax.ppermute(value, 'date', pairs + [(b, a) for a, b in pairs])  12.3 us
    all_to_all x1, starting transfers between devices, on_device(): lax.all_to_all(outgoing, 'date', split_axis=0, concat_axis=0, tiled=True)  11.1 us
    all_to_all x1, waiting for transfers between devices, on_device(): lax.all_to_all(outgoing, 'date', split_axis=0, concat_axis=0, tiled=True)  10.4 us
    ppermute x6, waiting for transfers between devices, swapped(): lax.ppermute(value, 'date', pairs + [(b, a) for a, b in pairs])  9.33 us
    ppermute x2, starting transfers between devices, shifted(): lax.ppermute(value, axis, [(source, source + steps) for source in range(f...  7.39 us
    pallas_call x2, Pallas kernels, packed_rows(): pl.pallas_call(functools.partial(pack_kernel, runs), out_shape=[jax.Shape...  5.49 us
  transfers between devices with their start and end apart: 9, of which 3 were waited for; matrix products, arithmetic and copies ran while one was open for 1% of the time, Pallas kernels for 33%

profile of v3, /device:TPU:9, one launch (start us, length us, event | category | flops | bytes accessed | tf_op | source)
XLA Modules:
  0.0 87.8 jit_solution(11017080755914664641)
XLA Ops:
  0.6 3.4 %shard_map.60 = (bf16[2,2,48,5120]{3,2,1,0:T(8,128)(2,1)}, bf16[2,2,48,5120]{3,2,1,0:T(8,128)(2,1)}) custom-call(s32[1]{0:T(128)} %bitcast.refs_0_.odd_ref, bf16[2,4,80,5120]{3,2,1,0:T(8,128)(2,1)} %refs_4_.3), custom_call_target="tpu_custom_call" | custom-call | tf_op jit(solution)/shard_map/pallas_call | solution.py:161
  4.1 4.1 %collective-permute-start = (bf16[2,2,48,5120]{3,2,1,0:T(8,128)(2,1)}, bf16[2,2,48,5120]{3,2,1,0:T(8,128)(2,1)S(1)}, u32[]{:S(2)}, u32[]{:S(2)}) collective-permute-start(bf16[2,2,48,5120]{3,2,1,0:T(8,128)(2,1)} %get-tuple-element.16), channel_id=1, source_target_pairs={{16,32},{48,64},{80,96},{112,128},{144,160},{176,192},{208,224},{3... | collective-permute-start | bytes 5898248 | tf_op jit(solution)/shard_map/ppermute | solution.py:357
  8.2 0.0 copy-start
  8.2 0.1 collective-permute-start.1
  8.3 9.6 %shard_map.59.refs_1_ = f32[16,16,256]{2,1,0:T(8,128)S(1)} custom-call(s32[1]{0:T(128)} %bitcast.refs_0_.odd_ref, bf16[2,4,80,5120]{3,2,1,0:T(8,128)(2,1)} %refs_4_.3), custom_call_target="tpu_custom_call" | custom-call | tf_op jit(solution)/shard_map/pallas_call | solution.py:108
  17.9 0.0 copy-done
  17.9 0.0 copy-start.1
  17.9 0.0 copy-start.4
  18.0 2.1 %shard_map.62 = (bf16[2,2,32,5120]{3,2,1,0:T(8,128)(2,1)}, bf16[2,2,32,5120]{3,2,1,0:T(8,128)(2,1)}) custom-call(s32[1]{0:T(128)} %bitcast.refs_0_.odd_ref, bf16[2,4,80,5120]{3,2,1,0:T(8,128)(2,1)S(1)} %copy-done), custom_call_target="tpu_custom_call" | custom-call | tf_op jit(solution)/shard_map/pallas_call | solution.py:161
  20.0 3.8 %collective-permute-start.2 = (bf16[2,2,32,5120]{3,2,1,0:T(8,128)(2,1)}, bf16[2,2,32,5120]{3,2,1,0:T(8,128)(2,1)S(1)}, u32[]{:S(2)}, u32[]{:S(2)}) collective-permute-start(bf16[2,2,32,5120]{3,2,1,0:T(8,128)(2,1)} %get-tuple-element.19), channel_id=1, source_target_pairs={{16,32},{48,64},{80,96},{112,128},{144,160},{176,192},{208,224},{3... | collective-permute-start | bytes 3932168 | tf_op jit(solution)/shard_map/ppermute | solution.py:357
  23.8 0.1 collective-permute-start.3
  23.9 0.0 copy-done.1
  23.9 0.0 copy-done.4
  24.0 0.0 copy-start.2
  24.0 0.0 copy-start.3
  24.0 6.7 %collective-permute-done.refs_1_ = bf16[2,2,48,5120]{3,2,1,0:T(8,128)(2,1)S(1)} collective-permute-done((bf16[2,2,48,5120]{3,2,1,0:T(8,128)(2,1)}, bf16[2,2,48,5120]{3,2,1,0:T(8,128)(2,1)S(1)}, u32[]{:S(2)}, u32[]{:S(2)}) %collective-permute-start) | collective-permute-done | bytes 1966112 | tf_op jit(solution)/shard_map/ppermute | solution.py:357
  30.7 0.0 collective-permute-done.1.refs_2_
  30.7 9.3 %shard_map.61.refs_2_ = f32[11,24,256]{2,1,0:T(8,128)S(1)} custom-call(s32[1]{0:T(128)} %bitcast.refs_0_.odd_ref, bf16[2,2,48,5120]{3,2,1,0:T(8,128)(2,1)S(1)} %collective-permute-done.refs_1_, bf16[2,2,48,5120]{3,2,1,0:T(8,128)(2,1)} %collective-permute-done.1.refs_2_, bf16[2,4,80,5120]{3,2,1,0:T(8,128)(2,1)} %refs_4_.3, bf16[2,4,80,5120]{3,2,1,0:T(8,128)(2,1)} %refs_4_.3, ...), custom_call_target="tpu_custom_call" | custom-call | tf_op jit(solution)/shard_map/pallas_call | solution.py:108
  40.0 3.1 %collective-permute-start.4 = (f32[1,40,256]{2,1,0:T(8,128)S(1)}, f32[1,40,256]{2,1,0:T(8,128)S(1)}, u32[]{:S(2)}, u32[]{:S(2)}) collective-permute-start(f32[1,40,256]{2,1,0:T(8,128)S(1)} %pad_maximum_fusion), channel_id=1, source_target_pairs={{0,1},{1,2},{2,3},{3,4},{4,5},{5,6},{6,7},{7,8},{8,9},{9,10},{10,1... | collective-permute-start | bytes 122888 | tf_op jit(solution)/shard_map/ppermute | solution.py:349
  43.2 4.3 %collective-permute-start.5 = (f32[1,40,256]{2,1,0:T(8,128)S(1)}, f32[1,40,256]{2,1,0:T(8,128)S(1)}, u32[]{:S(2)}, u32[]{:S(2)}) collective-permute-start(f32[1,40,256]{2,1,0:T(8,128)S(1)} %pad_maximum_fusion.1), channel_id=1, source_target_pairs={{1,0},{2,1},{3,2},{4,3},{5,4},{6,5},{7,6},{8,7},{9,8},{10,9},{11,1... | collective-permute-start | bytes 122888 | tf_op jit(solution)/shard_map/ppermute | solution.py:349
  47.5 0.0 copy-done.2
  47.5 0.0 copy-done.3
  47.5 0.2 convert_reduce_fusion
  47.7 0.0 collective-permute-done.2.refs_1_
  47.7 0.0 collective-permute-done.3.refs_2_
  47.7 7.0 %shard_map.63.refs_3_ = f32[7,24,256]{2,1,0:T(8,128)S(1)} custom-call(s32[1]{0:T(128)} %bitcast.refs_0_.odd_ref, bf16[2,2,32,5120]{3,2,1,0:T(8,128)(2,1)S(1)} %collective-permute-done.2.refs_1_, bf16[2,2,32,5120]{3,2,1,0:T(8,128)(2,1)} %collective-permute-done.3.refs_2_, bf16[2,4,80,5120]{3,2,1,0:T(8,128)(2,1)} %refs_4_.3, bf16[2,4,80,5120]{3,2,1,0:T(8,128)(2,1)} %refs_4_.3), custom_call_target="tpu_custom_call" | custom-call | tf_op jit(solution)/shard_map/pallas_call | solution.py:108
  54.7 0.0 collective-permute-done.4.refs_4_
  54.7 0.0 collective-permute-done.5.refs_5_
  54.7 0.6 shard_map.64
  55.3 4.2 %collective-permute-start.6 = (f32[320,128]{1,0:T(8,128)S(1)}, f32[320,128]{1,0:T(8,128)S(1)}, u32[]{:S(2)}, u32[]{:S(2)}) collective-permute-start(f32[320,128]{1,0:T(8,128)S(1)} %get-tuple-element.24), channel_id=1, source_target_pairs={{16,32},{48,64},{80,96},{112,128},{144,160},{176,192},{208,224},{3... | collective-permute-start | bytes 491528 | tf_op jit(solution)/shard_map/ppermute | solution.py:357
  59.5 0.1 collective-permute-start.7
  59.6 0.1 select_reduce_fusion.2.slot_ref
  59.7 0.1 select_reduce_fusion.1.sign_ref
  59.8 2.7 %collective-permute-done.6.refs_3_ = f32[320,128]{1,0:T(8,128)S(1)} collective-permute-done((f32[320,128]{1,0:T(8,128)S(1)}, f32[320,128]{1,0:T(8,128)S(1)}, u32[]{:S(2)}, u32[]{:S(2)}) %collective-permute-start.6) | collective-permute-done | bytes 163872 | tf_op jit(solution)/shard_map/ppermute | solution.py:357
  62.5 0.0 collective-permute-done.7.refs_4_
  62.5 1.4 %shard_map.65 = (s16[16,64,128]{2,1,0:T(8,128)(2,1)}, f32[1664,128]{1,0:T(8,128)S(1)}) custom-call(s32[1]{0:T(128)} %bitcast.refs_0_.odd_ref, s32[16]{0:T(128)S(1)} %select_reduce_fusion.2.slot_ref, f32[16]{0:T(128)S(1)} %select_reduce_fusion.1.sign_ref, f32[384,128]{1,0:T(8,128)S(1)} %get-tuple-element.21.refs_0_, ...), custom_call_target="tpu_custom_call" | custom-call | tf_op jit(solution)/shard_map/pallas_call | solution.py:276
  63.8 11.1 %all-to-all-start = ((s16[16,64,128]{2,1,0:T(8,128)(2,1)}), s16[16,64,128]{2,1,0:T(8,128)(2,1)S(1)}, u32[]{:S(2)}, u32[]{:S(2)}) async-start(s16[16,64,128]{2,1,0:T(8,128)(2,1)} %get-tuple-element.26), calls=%async_computation | async-start | bytes 524288 | tf_op jit(solution)/shard_map/all_to_all | solution.py:443
  74.9 1.3 %shard_map.67 = f32[2,4,4096]{2,1,0:T(4,128)} custom-call(f32[26]{0:T(128)S(1)} %convert_element_type.7.count_ref, f32[1664,128]{1,0:T(8,128)S(1)} %get-tuple-element.27.known_ref), custom_call_target="tpu_custom_call" | custom-call | tf_op jit(solution)/shard_map/pallas_call | solution.py:313
  76.3 10.4 %all-to-all-done.arrived_ref = s16[16,64,128]{2,1,0:T(8,128)(2,1)S(1)} async-done(((s16[16,64,128]{2,1,0:T(8,128)(2,1)}), s16[16,64,128]{2,1,0:T(8,128)(2,1)S(1)}, u32[]{:S(2)}, u32[]{:S(2)}) %all-to-all-start) | async-done | bytes 262176 | tf_op jit(solution)/shard_map/all_to_all | solution.py:443
  86.6 1.1 %shard_map.66 = f32[2,16,4096]{2,1,0:T(8,128)} custom-call(s16[16,64,128]{2,1,0:T(8,128)(2,1)S(1)} %all-to-all-done.arrived_ref), custom_call_target="tpu_custom_call" | custom-call | tf_op jit(solution)/shard_map/pallas_call | solution.py:338
  (9 shorter events, 0.1 us)
Async XLA Ops:
  4.1 26.6 %collective-permute-start = (bf16[2,2,48,5120]{3,2,1,0:T(8,128)(2,1)}, bf16[2,2,48,5120]{3,2,1,0:T(8,128)(2,1)S(1)}, u32[]{:S(2)}, u32[]{:S(2)}) collective-permute-start(bf16[2,2,48,5120]{3,2,1,0:T(8,128)(2,1)} %get-tuple-element.16), channel_id=1, source_target_pairs={{16,32},{48,64},{80,96},{112,128},{144,160},{176,192},{208,224},{3... | collective-permute-start | bytes 5898248 | tf_op jit(solution)/shard_map/ppermute | solution.py:357
  8.2 9.7 %copy-start = (bf16[2,4,80,5120]{3,2,1,0:T(8,128)(2,1)S(1)}, bf16[2,4,80,5120]{3,2,1,0:T(8,128)(2,1)}, u32[]{:S(2)}) copy-start(bf16[2,4,80,5120]{3,2,1,0:T(8,128)(2,1)} %refs_4_.3) | copy-start | bytes 19660804
  8.2 22.5 %collective-permute-start.1 = (bf16[2,2,48,5120]{3,2,1,0:T(8,128)(2,1)}, bf16[2,2,48,5120]{3,2,1,0:T(8,128)(2,1)}, u32[]{:S(2)}, u32[]{:S(2)}) collective-permute-start(bf16[2,2,48,5120]{3,2,1,0:T(8,128)(2,1)} %get-tuple-element.17), channel_id=1, source_target_pairs={{0,16},{32,48},{64,80},{96,112},{128,144},{160,176},{192,208},{224... | collective-permute-start | bytes 5898248 | tf_op jit(solution)/shard_map/ppermute | solution.py:357
  17.9 6.0 %copy-start.1 = (s32[128,2]{0,1:T(2,128)S(1)}, s32[128,2]{0,1:T(2,128)}, u32[]{:S(2)}) copy-start(s32[128,2]{0,1:T(2,128)} %param.5) | copy-start | bytes 3076
  17.9 6.0 %copy-start.4 = (s32[128]{0:T(128)S(1)}, s32[128]{0:T(128)}, u32[]{:S(2)}) copy-start(s32[128]{0:T(128)} %param.6) | copy-start | bytes 1540
  20.0 27.6 %collective-permute-start.2 = (bf16[2,2,32,5120]{3,2,1,0:T(8,128)(2,1)}, bf16[2,2,32,5120]{3,2,1,0:T(8,128)(2,1)S(1)}, u32[]{:S(2)}, u32[]{:S(2)}) collective-permute-start(bf16[2,2,32,5120]{3,2,1,0:T(8,128)(2,1)} %get-tuple-element.19), channel_id=1, source_target_pairs={{16,32},{48,64},{80,96},{112,128},{144,160},{176,192},{208,224},{3... | collective-permute-start | bytes 3932168 | tf_op jit(solution)/shard_map/ppermute | solution.py:357
  23.8 23.9 %collective-permute-start.3 = (bf16[2,2,32,5120]{3,2,1,0:T(8,128)(2,1)}, bf16[2,2,32,5120]{3,2,1,0:T(8,128)(2,1)}, u32[]{:S(2)}, u32[]{:S(2)}) collective-permute-start(bf16[2,2,32,5120]{3,2,1,0:T(8,128)(2,1)} %get-tuple-element.20), channel_id=1, source_target_pairs={{0,16},{32,48},{64,80},{96,112},{128,144},{160,176},{192,208},{224... | collective-permute-start | bytes 3932168 | tf_op jit(solution)/shard_map/ppermute | solution.py:357
  24.0 23.5 %copy-start.2 = (s32[26]{0:T(128)S(1)}, s32[26]{0:T(128)}, u32[]{:S(2)}) copy-start(s32[26]{0:T(128)} %constant.58) | copy-start | bytes 316
  24.0 23.5 %copy-start.3 = (s32[26]{0:T(128)S(1)}, s32[26]{0:T(128)}, u32[]{:S(2)}) copy-start(s32[26]{0:T(128)} %constant.60) | copy-start | bytes 316
  40.0 14.6 %collective-permute-start.4 = (f32[1,40,256]{2,1,0:T(8,128)S(1)}, f32[1,40,256]{2,1,0:T(8,128)S(1)}, u32[]{:S(2)}, u32[]{:S(2)}) collective-permute-start(f32[1,40,256]{2,1,0:T(8,128)S(1)} %pad_maximum_fusion), channel_id=1, source_target_pairs={{0,1},{1,2},{2,3},{3,4},{4,5},{5,6},{6,7},{7,8},{8,9},{9,10},{10,1... | collective-permute-start | bytes 122888 | tf_op jit(solution)/shard_map/ppermute | solution.py:349
  43.2 11.5 %collective-permute-start.5 = (f32[1,40,256]{2,1,0:T(8,128)S(1)}, f32[1,40,256]{2,1,0:T(8,128)S(1)}, u32[]{:S(2)}, u32[]{:S(2)}) collective-permute-start(f32[1,40,256]{2,1,0:T(8,128)S(1)} %pad_maximum_fusion.1), channel_id=1, source_target_pairs={{1,0},{2,1},{3,2},{4,3},{5,4},{6,5},{7,6},{8,7},{9,8},{10,9},{11,1... | collective-permute-start | bytes 122888 | tf_op jit(solution)/shard_map/ppermute | solution.py:349
  55.3 7.2 %collective-permute-start.6 = (f32[320,128]{1,0:T(8,128)S(1)}, f32[320,128]{1,0:T(8,128)S(1)}, u32[]{:S(2)}, u32[]{:S(2)}) collective-permute-start(f32[320,128]{1,0:T(8,128)S(1)} %get-tuple-element.24), channel_id=1, source_target_pairs={{16,32},{48,64},{80,96},{112,128},{144,160},{176,192},{208,224},{3... | collective-permute-start | bytes 491528 | tf_op jit(solution)/shard_map/ppermute | solution.py:357
  59.5 3.0 %collective-permute-start.7 = (f32[320,128]{1,0:T(8,128)S(1)}, f32[320,128]{1,0:T(8,128)S(1)}, u32[]{:S(2)}, u32[]{:S(2)}) collective-permute-start(f32[320,128]{1,0:T(8,128)S(1)} %get-tuple-element.25), channel_id=1, source_target_pairs={{0,16},{32,48},{64,80},{96,112},{128,144},{160,176},{192,208},{224... | collective-permute-start | bytes 491528 | tf_op jit(solution)/shard_map/ppermute | solution.py:357
  63.8 22.8 %all-to-all-start = ((s16[16,64,128]{2,1,0:T(8,128)(2,1)}), s16[16,64,128]{2,1,0:T(8,128)(2,1)S(1)}, u32[]{:S(2)}, u32[]{:S(2)}) async-start(s16[16,64,128]{2,1,0:T(8,128)(2,1)} %get-tuple-element.26), calls=%async_computation | async-start | bytes 524288 | tf_op jit(solution)/shard_map/all_to_all | solution.py:443

commit v4 on v3

v4 whole, which is shorter than its diff:
```python
import functools

import jax
import jax.numpy as jnp
from jax import lax
from jax.experimental import pallas as pl
from jax.experimental.pallas import tpu as pltpu
from jax.sharding import PartitionSpec as P

ALOOK = 5
RLOOK = 20
LANES = 128
TILE = 16
COLUMNS = 1280
CHUNK = 256
FIXED = 32000.0
EPS_POWER = 1e-06
MIB = 2**20

INNER = ((2, 3), (2, 4), (2, 5), (3, 4), (3, 5), (4, 5))
SIDE = ((0, 4), (1, 4), (1, 5), (0, 2), (0, 3), (1, 2))
BACK = 4
RETURNED = tuple((3 - i, 3 - j) for i, j in SIDE[:BACK])
OWN_PLACES = (2, 3, 4, 5)
NEAR_PLACES = (0, 1)
KNOWN = tuple(
    (i, j, across)
    for edges, across in ((INNER, 0), (SIDE, 0), (SIDE, 1), (RETURNED, 1), (RETURNED, 0))
    for i, j in edges
)
FORMED = len(INNER) + 2 * len(SIDE)


def products_kernel(edges, powers, places, groups, *refs):
    flip = refs[0][0]
    out_ref, look_ref, even_ref, odd_ref, acc_ref = refs[-5:]
    total = 2 * len(edges) + len(powers)
    rows = acc_ref.shape[0] // total
    step = pl.program_id(0)
    used = sorted({k for e in edges for k in e} | set(powers))
    buffers = (even_ref, odd_ref)

    @pl.when(step == 0)
    def _():
        column = lax.broadcasted_iota(jnp.int32, look_ref.shape, 0)
        begin = lax.broadcasted_iota(jnp.int32, look_ref.shape, 1) * RLOOK
        inside = (column >= begin) & (column < begin + RLOOK)
        look_ref[...] = inside.astype(jnp.float32).astype(jnp.bfloat16)

    def form(chunk):
        for part in range(CHUNK // LANES):
            lane = slice(chunk * CHUNK + part * LANES, chunk * CHUNK + (part + 1) * LANES)
            out_lane = slice(part * LANES, (part + 1) * LANES)
            for tile in range(rows // TILE):
                pixel = {}
                for k in used:
                    source, date, row = places[k][tile]
                    ref = refs[1 + source]
                    date = date + flip * (ref.shape[1] - 1 - 2 * date)
                    pixel[k] = tuple(
                        ref[c, date, row : row + TILE, lane].astype(jnp.float32) for c in (0, 1)
                    )
                results = []
                for i, j in edges:
                    results.append(pixel[i][0] * pixel[j][0] + pixel[i][1] * pixel[j][1])
                for i, j in edges:
                    results.append(pixel[i][1] * pixel[j][0] - pixel[i][0] * pixel[j][1])
                for k in powers:
                    results.append(pixel[k][0] * pixel[k][0] + pixel[k][1] * pixel[k][1])
                for p, value in enumerate(results):
                    first = p * rows + tile * TILE
                    buffers[chunk % 2][first : first + TILE, out_lane] = value.astype(jnp.bfloat16)

    def add_looks(chunk):
        row = pl.multiple_of(step % 2 * COLUMNS + chunk * CHUNK, CHUNK)
        part = jnp.dot(
            buffers[chunk % 2][...],
            look_ref[pl.ds(row, CHUNK), :],
            preferred_element_type=jnp.float32,
        )
        if chunk == 0:
            acc_ref[...] = part + jnp.where(step % 2 == 1, acc_ref[...], 0.0)
        else:
            acc_ref[...] += part

    chunks = COLUMNS // CHUNK
    form(0)
    for chunk in range(chunks):
        if chunk + 1 < chunks:
            form(chunk + 1)
        add_looks(chunk)

    @pl.when(step % 2 == 1)
    def _():
        for m, (first, last) in enumerate(groups):
            for p in range(0, total, 8):
                size = min(8, total - p)
                value = acc_ref[pl.ds(p * rows + first, size, stride=rows), :]
                for row in range(first + 1, last):
                    value += acc_ref[pl.ds(p * rows + row, size, stride=rows), :]
                out_ref[m, p : p + size, :] = value


def looked_products(flip, edges, powers, sources, places, groups, rows, columns):
    total = 2 * len(edges) + len(powers)

    def spec(block, index):
        return pl.BlockSpec(block + (COLUMNS,), lambda i: index + (i,))

    return pl.pallas_call(
        functools.partial(products_kernel, edges, powers, places, groups),
        out_shape=jax.ShapeDtypeStruct((len(groups), total, columns // RLOOK), jnp.float32),
        grid=(columns // COLUMNS,),
        in_specs=[pl.BlockSpec(memory_space=pltpu.SMEM)] + [spec(*s[1:]) for s in sources],
        out_specs=pl.BlockSpec((len(groups), total, LANES), lambda i: (0, 0, i // 2)),
        scratch_shapes=[
            pltpu.VMEM((2 * COLUMNS, LANES), jnp.bfloat16),
            pltpu.VMEM((total * rows, CHUNK), jnp.bfloat16),
            pltpu.VMEM((total * rows, CHUNK), jnp.bfloat16),
            pltpu.VMEM((total * rows, LANES), jnp.float32),
        ],
        compiler_params=pltpu.CompilerParams(vmem_limit_bytes=48 * MIB),
    )(flip, *[s[0] for s in sources])


def pack_kernel(runs, flip_ref, images_ref, out_ref, held_ref, in_sems, out_sems):
    first = 2 * flip_ref[0]
    loads, stores = [], []
    for c in range(2):
        for row, target, size in runs:
            held = held_ref.at[c, :, target : target + size, :]
            loads.append(
                pltpu.make_async_copy(
                    images_ref.at[c, pl.ds(first, 2), row : row + size, :],
                    held,
                    in_sems.at[len(loads)],
                )
            )
            stores.append(
                pltpu.make_async_copy(
                    held, out_ref.at[c, :, target : target + size, :], out_sems.at[len(stores)]
                )
            )
    for load in loads:
        load.start()
    for load, store in zip(loads, stores):
        load.wait()
        store.start()
    for store in stores:
        store.wait()


def packed_rows(flip, images, runs, limit):
    columns = images.shape[3]
    rows = sum(size for _, _, size in runs)
    return pl.pallas_call(
        functools.partial(pack_kernel, runs),
        out_shape=jax.ShapeDtypeStruct((2, 2, rows, columns), images.dtype),
        in_specs=[pl.BlockSpec(memory_space=pltpu.SMEM), pl.BlockSpec(memory_space=pl.ANY)],
        out_specs=pl.BlockSpec(memory_space=pl.ANY),
        scratch_shapes=[
            pltpu.VMEM((2, 2, rows, columns), images.dtype),
            pltpu.SemaphoreType.DMA((2 * len(runs),)),
            pltpu.SemaphoreType.DMA((2 * len(runs),)),
        ],
        compiler_params=pltpu.CompilerParams(vmem_limit_bytes=limit * MIB),
    )(flip, images)


def coherence_kernel(layout, *refs):
    inner_ref, beside_ref, first_ref, second_ref, before_ref, after_ref = refs[:6]
    formed_ref, across_back_ref, beside_back_ref = refs[6:]
    cells, n_first, width = inner_ref.shape
    n_second = beside_ref.shape[1]
    halves = width // LANES
    block = 2 * cells * halves

    def padded(at, start, size):
        planes = slice(start, start + size)
        return (
            [before_ref[0, planes]] + [at(m) for m in range(cells)] + [after_ref[0, planes]]
        )

    def across_at(m):
        return sum(ref[n] for ref, n in zip((first_ref, second_ref), layout[m]) if n is not None)

    rows = (
        padded(lambda m: inner_ref[m], 0, n_first),
        padded(lambda m: beside_ref[m], n_first, n_second),
        padded(across_at, n_first + n_second, n_second),
    )
    for m in range(cells):
        inner, beside, across = (r[m] + 2.0 * r[m + 1] + r[m + 2] for r in rows)

        def power_of(smooth, edges, n):
            return smooth[2 * len(edges) + n : 2 * len(edges) + n + 1]

        beside_power = {k: power_of(beside, SIDE, n) for n, k in enumerate(NEAR_PLACES)}
        across_power = {k: power_of(across, SIDE, n) for n, k in enumerate(NEAR_PLACES)}
        for n, k in enumerate(OWN_PLACES):
            beside_power[k] = power_of(inner, INNER, n)
            across_power[7 - k] = beside_power[k]
        start = 0
        for values, edges, power, back_ref in (
            (inner, INNER, beside_power, None),
            (beside, SIDE, beside_power, beside_back_ref),
            (across, SIDE, across_power, across_back_ref),
        ):
            size = len(edges)
            first = jnp.concatenate([power[i] for i, _ in edges], axis=0)
            second = jnp.concatenate([power[j] for _, j in edges], axis=0)
            scale = lax.rsqrt(first * second + EPS_POWER)
            for part in range(2):
                value = values[part * size : (part + 1) * size] * scale
                for h in range(halves):
                    row = (part * cells + m) * halves + h
                    piece = value[:, h * LANES : (h + 1) * LANES]
                    formed_ref[pl.ds(start * block + row, size, stride=block), :] = piece
                    if back_ref is not None:
                        back_ref[pl.ds(row, BACK, stride=block), :] = piece[:BACK]
            start += size


def coherences(layout, inner, beside, first, second, before, after):
    cells, _, width = inner.shape
    block = 2 * cells * (width // LANES)
    return pl.pallas_call(
        functools.partial(coherence_kernel, layout),
        out_shape=[
            jax.ShapeDtypeStruct((n * block, LANES), jnp.float32) for n in (FORMED, BACK, BACK)
        ],
        compiler_params=pltpu.CompilerParams(vmem_limit_bytes=32 * MIB),
    )(inner, beside, first, second, before, after)


def slots_kernel(odd_ref, slot_ref, sign_ref, count_ref, *refs):
    out_ref, sums_ref, known_ref, rows_ref = refs[-4:]
    owners, block, _ = out_ref.shape
    start = 0
    for table in refs[:-4]:
        known_ref[start : start + table.shape[0], :] = table[...]
        start += table.shape[0]
    for o in range(owners):
        row = pl.multiple_of(slot_ref[o] * block, block)
        value = known_ref[pl.ds(row, block), :]
        half = block // 2
        scales = (jnp.abs(sign_ref[o]) * FIXED, sign_ref[o] * FIXED)
        for part in range(2):
            fixed = jnp.round(value[part * half : (part + 1) * half] * scales[part])
            out_ref[o, part * half : (part + 1) * half, :] = fixed.astype(jnp.int32).astype(jnp.int16)
    parts, dates, cell_count = sums_ref.shape
    tiles = cell_count // LANES
    for part in range(parts):
        totals = {k: jnp.zeros((tiles, LANES), jnp.float32) for k in OWN_PLACES}
        for e, (first, second, across) in enumerate(KNOWN):
            row = (e * parts + part) * tiles
            value = known_ref[row : row + tiles, :] * count_ref[e]
            for k in OWN_PLACES:
                place = k if across else 7 - k
                if place == first or (place == second and part == 0):
                    totals[k] = totals[k] + value
                elif place == second:
                    totals[k] = totals[k] - value
        for d, k in enumerate(OWN_PLACES):
            date = d + odd_ref[0] * (dates - 1 - 2 * d)
            first = pl.multiple_of((part * dates + date) * tiles, tiles)
            rows_ref[pl.ds(first, tiles), :] = totals[k]
    for part in range(parts):
        for t in range(tiles):
            sums_ref[part, :, t * LANES : (t + 1) * LANES] = rows_ref[
                pl.ds(part * dates * tiles + t, dates, stride=tiles), :
            ]


def slots_and_sums(odd, slot, sign, count, tables, owners, local_dates, cell_count):
    smem = pl.BlockSpec(memory_space=pltpu.SMEM)
    vmem = pl.BlockSpec(memory_space=pltpu.VMEM)
    block = 2 * cell_count // LANES
    return pl.pallas_call(
        slots_kernel,
        out_shape=[
            jax.ShapeDtypeStruct((owners, block, LANES), jnp.int16),
            jax.ShapeDtypeStruct((2, local_dates, cell_count), jnp.float32),
        ],
        in_specs=[smem] * 4 + [vmem] * len(tables),
        scratch_shapes=[
            pltpu.VMEM((len(KNOWN) * block, LANES), jnp.float32),
            pltpu.VMEM((local_dates * block, LANES), jnp.float32),
        ],
        compiler_params=pltpu.CompilerParams(vmem_limit_bytes=32 * MIB),
    )(odd, slot, sign, count, *tables)


def table_kernel(arrived_ref, out_ref, rows_ref):
    parts, owners, cell_count = out_ref.shape
    tiles = cell_count // LANES
    for o in range(owners):
        rows_ref[o * parts * tiles : (o + 1) * parts * tiles, :] = arrived_ref[o].astype(
            jnp.int32
        ).astype(jnp.float32) * (1.0 / FIXED)
    for part in range(parts):
        for t in range(tiles):
            out_ref[part, :, t * LANES : (t + 1) * LANES] = rows_ref[
                pl.ds(part * tiles + t, owners, stride=parts * tiles), :
            ]


def as_table(arrived, cell_count):
    owners, block, _ = arrived.shape
    return pl.pallas_call(
        table_kernel,
        out_shape=jax.ShapeDtypeStruct((2, owners, cell_count), jnp.float32),
        scratch_shapes=[pltpu.VMEM((owners * block, LANES), jnp.float32)],
        compiler_params=pltpu.CompilerParams(vmem_limit_bytes=32 * MIB),
    )(arrived)


def shifted(value, axis, steps):
    count = lax.axis_size(axis)
    first, last = (max(0, -steps), min(count, count - steps))
    return lax.ppermute(value, axis, [(source, source + steps) for source in range(first, last)])


def swapped_across(value):
    pairs = [(i, i + 1) for i in range(1, lax.axis_size("date") - 1, 2)]
    return lax.ppermute(value, "date", pairs + [(b, a) for a, b in pairs])


def swapped_beside(value):
    pairs = [(i, i + 1) for i in range(0, lax.axis_size("date"), 2)]
    return lax.ppermute(value, "date", pairs + [(b, a) for a, b in pairs])


def pair_tables(date_pairs, assignment, myself, owners, local_dates):
    anchor = myself * local_dates - 2
    first = date_pairs[:, 0] - anchor
    second = date_pairs[:, 1] - anchor
    known = jnp.array(KNOWN, jnp.int32)
    flipped = (known[:, 2] == 1) == (myself % 2 == 1)
    known_first = jnp.where(flipped, 7 - known[:, 0], known[:, 0])[None, :]
    known_second = jnp.where(flipped, 7 - known[:, 1], known[:, 1])[None, :]
    first, second = first[:, None], second[:, None]
    forward = (first == known_first) & (second == known_second)
    backward = (first == known_second) & (second == known_first)
    is_edge = forward | backward
    count = jnp.sum(is_edge, axis=0).astype(jnp.float32)
    edge = jnp.sum(jnp.where(is_edge, jnp.arange(len(KNOWN))[None, :], 0), axis=1)
    way = jnp.sum(forward.astype(jnp.float32) - backward.astype(jnp.float32), axis=1)
    mine = date_pairs[:, 0] // local_dates == myself
    matches = (assignment[None, :] // owners == jnp.arange(owners)[:, None]) & mine[None, :]
    slot = jnp.sum(jnp.where(matches, edge[None, :], 0), axis=1)
    sign = jnp.sum(jnp.where(matches, way[None, :], 0.0), axis=1)
    return slot, sign, count


def row_groups(tiles, cells):
    held = [t * TILE + r for t in tiles for r in range(TILE)]
    groups, owners = [], []
    for m in range(cells):
        local = [n for n, row in enumerate(held) if row // ALOOK == m]
        if local:
            groups.append((local[0], local[-1] + 1))
            owners.append(m)
    return groups, owners


def on_device(images, date_pairs, assignment):
    owners = lax.axis_size("date")
    myself = lax.axis_index("date")
    _, local_dates, rows, columns = images.shape
    cells = rows // ALOOK
    cell_count = cells * (columns // RLOOK)
    tiles = rows // TILE
    pieces = ((0,) + tuple(range(3, tiles)), (1, 2))
    runs = (((0, 0, TILE), (3 * TILE, TILE, rows - 3 * TILE)), ((TILE, 0, 2 * TILE),))
    odd = (myself % 2).astype(jnp.int32)[None]
    even = 1 - odd

    beside = swapped_beside(images)
    across = [swapped_across(packed_rows(odd, images, runs[0], 60))]
    slot, sign, count = pair_tables(date_pairs, assignment, myself, owners, local_dates)

    all_groups = row_groups(range(tiles), cells)[0]
    own_source = (images, (2, local_dates, rows), (0, 0, 0))
    own_places = {
        2 + d: [(0, d, t * TILE) for t in range(tiles)] for d in range(local_dates)
    }
    inner = looked_products(
        even, INNER, OWN_PLACES, [own_source], own_places, all_groups, rows, columns
    )
    later, inner = lax.optimization_barrier((images, inner))
    across.append(swapped_across(packed_rows(odd, later, runs[1], 60)))

    side_places = own_places | {
        d: [(1, local_dates - 2 + d, t * TILE) for t in range(tiles)] for d in range(2)
    }
    beside_looked = looked_products(
        even,
        SIDE,
        NEAR_PLACES,
        [own_source, (beside, (2, local_dates, rows), (0, 0, 0))],
        side_places,
        all_groups,
        rows,
        columns,
    )
    later, beside_looked = lax.optimization_barrier((images, beside_looked))
    layout = [[None, None] for _ in range(cells)]
    across_looked = []
    for n, (piece, arrived) in enumerate(zip(pieces, across)):
        size = len(piece)
        sources = [(arrived, (2, 2, size * TILE), (0, 0, 0))]
        sources += [(later, (2, local_dates, TILE), (0, 0, t)) for t in piece]
        places = {d: [(0, d, t * TILE) for t in range(size)] for d in range(2)}
        places |= {2 + d: [(1 + t, d, 0) for t in range(size)] for d in range(local_dates)}
        groups, where = row_groups(piece, cells)
        for g, m in enumerate(where):
            layout[m][n] = g
        across_looked.append(
            looked_products(odd, SIDE, NEAR_PLACES, sources, places, groups, size * TILE, columns)
        )

    def edge_cells(cut):
        return jnp.concatenate([inner[cut], beside_looked[cut], across_looked[0][cut]], axis=1)

    before = shifted(edge_cells(slice(-1, None)), "strip", 1)
    after = shifted(edge_cells(slice(0, 1)), "strip", -1)
    formed, across_back, beside_back = coherences(
        layout, inner, beside_looked, *across_looked, before, after
    )
    tables = (formed, swapped_across(across_back), swapped_beside(beside_back))
    outgoing, sums = slots_and_sums(
        odd, slot, sign, count, tables, owners, local_dates, cell_count
    )
    table = lax.all_to_all(outgoing, "date", split_axis=0, concat_axis=0, tiled=True)
    return (as_table(table, cell_count), sums)


def solution(mesh):
    return jax.shard_map(
        on_device,
        mesh=mesh,
        in_specs=(P(None, "date", "strip", None), P(), P()),
        out_specs=(P(None, "date", "strip"), P(None, "date", "strip")),
        check_vma=False,
    )
```

time: 88.1 us -> 85 us (0.965)
  blocking collectives: 0 us -> 22.6 us
  waiting for transfers between devices: 19.7 us -> 2.31 us
  starting transfers between devices: 30.8 us -> 17.2 us
  Pallas kernels: 35.8 us -> 38.9 us
  other arithmetic: 0.47 us -> 1.9 us
    all_to_all x0 -> x1, blocking collectives: none -> 22.6 us  [on_device(): lax.all_to_all(outgoing, 'date', split_axis=0, concat_axis=0, tiled=True)]
    all_to_all x1 -> x0, starting transfers between devices: 11.1 us -> none  [on_device(): lax.all_to_all(outgoing, 'date', split_axis=0, concat_axis=0, tiled=True)]
    all_to_all x1 -> x0, waiting for transfers between devices: 10.4 us -> none  [on_device(): lax.all_to_all(outgoing, 'date', split_axis=0, concat_axis=0, tiled=True)]
    ppermute x6 -> x5, waiting for transfers between devices: 9.33 us -> 2.31 us  [the longest x3 2.3 us: swapped_across(): return lax.ppermute(value, 'date', pairs + [(b, a) for a, b in pairs])]
    pallas_call x3 -> x4, Pallas kernels: 25.9 us -> 30.8 us  [looked_products(): pl.pallas_call(functools.partial(products_kernel, edges, powers, places,...]
    pallas_call x4 -> x3, Pallas kernels: 8.2 us -> 6.21 us  [the longest x2 4.75 us: packed_rows(): pl.pallas_call(functools.partial(pack_kernel, runs), out_shape=jax.ShapeD...]
    ppermute x6 -> x5, starting transfers between devices: 12.3 us -> 11 us  [the longest x3 10.1 us: swapped_across(): return lax.ppermute(value, 'date', pairs + [(b, a) for a, b in pairs])]
    ppermute x2, starting transfers between devices: 7.39 us -> 6.19 us  [shifted(): lax.ppermute(value, axis, [(source, source + steps) for source in range(f...]
  transfers between devices with their start and end apart: 9 -> 7, of which waited for: 3 -> 1; matrix products, arithmetic and copies ran while one was open for 1% -> 2% of each run, Pallas kernels for 33% -> 42%
where the time goes in v4:
time: 85 us; the launch traced here: 83.8 us
  Pallas kernels  38.9 us (46%)
  blocking collectives  22.6 us (27%)
  starting transfers between devices  17.2 us (20%)
  waiting for transfers between devices  2.31 us (3%)
  other arithmetic  1.9 us (2%)
  between operations  0.89 us (1%)
    pallas_call x4, Pallas kernels, looked_products(): pl.pallas_call(functools.partial(products_kernel, edges, powers, places,...  30.8 us
    all_to_all x1, blocking collectives, on_device(): lax.all_to_all(outgoing, 'date', split_axis=0, concat_axis=0, tiled=True)  22.6 us
    ppermute x3, starting transfers between devices, swapped_across(): return lax.ppermute(value, 'date', pairs + [(b, a) for a, b in pairs])  10.1 us
    ppermute x2, starting transfers between devices, shifted(): lax.ppermute(value, axis, [(source, source + steps) for source in range(f...  6.19 us
    pallas_call x2, Pallas kernels, packed_rows(): pl.pallas_call(functools.partial(pack_kernel, runs), out_shape=jax.ShapeD...  4.75 us
    ppermute x3, waiting for transfers between devices, swapped_across(): return lax.ppermute(value, 'date', pairs + [(b, a) for a, b in pairs])  2.3 us
  transfers between devices with their start and end apart: 7, of which 1 were waited for; matrix products, arithmetic and copies ran while one was open for 2% of the time, Pallas kernels for 42%

profile of v4, /device:TPU:9, one launch (start us, length us, event | category | flops | bytes accessed | tf_op | source)
XLA Modules:
  0.0 83.8 jit_solution(559650932483349014)
XLA Ops:
  0.6 0.8 collective-permute-start
  1.4 2.5 %shard_map.61 = bf16[2,2,48,5120]{3,2,1,0:T(8,128)(2,1)} custom-call(s32[1]{0:T(128)} %bitcast.flip_ref.refs_0_.odd_ref, bf16[2,4,80,5120]{3,2,1,0:T(8,128)(2,1)} %refs_3_.1), custom_call_target="tpu_custom_call" | custom-call | tf_op jit(solution)/shard_map/pallas_call | solution.py:156
  3.9 3.5 %collective-permute-start.1 = (bf16[2,2,48,5120]{3,2,1,0:T(8,128)(2,1)}, bf16[2,2,48,5120]{3,2,1,0:T(8,128)(2,1)S(1)}, u32[]{:S(2)}, u32[]{:S(2)}) collective-permute-start(bf16[2,2,48,5120]{3,2,1,0:T(8,128)(2,1)} %shard_map.61), channel_id=1, source_target_pairs={{16,32},{48,64},{80,96},{112,128},{144,160},{176,192},{208,224},{3... | collective-permute-start | bytes 5898248 | tf_op jit(solution)/shard_map/ppermute | solution.py:326
  7.3 9.5 %shard_map.59.refs_0_ = f32[16,16,256]{2,1,0:T(8,128)S(1)} custom-call(s32[1]{0:T(128)S(6)} %sub.56.refs_0_, bf16[2,4,80,5120]{3,2,1,0:T(8,128)(2,1)} %refs_3_.1), custom_call_target="tpu_custom_call" | custom-call | tf_op jit(solution)/shard_map/pallas_call | solution.py:110
  16.9 0.0 copy-start
  16.9 0.0 copy-start.1
  16.9 0.0 copy-start.2
  16.9 0.0 copy-start.3
  16.9 2.3 %shard_map.63 = bf16[2,2,32,5120]{3,2,1,0:T(8,128)(2,1)} custom-call(s32[1]{0:T(128)} %bitcast.flip_ref.refs_0_.odd_ref, bf16[2,4,80,5120]{3,2,1,0:T(8,128)(2,1)} %refs_3_.1), custom_call_target="tpu_custom_call" | custom-call | tf_op jit(solution)/shard_map/pallas_call | solution.py:156
  19.2 2.2 %collective-permute-start.2 = (bf16[2,2,32,5120]{3,2,1,0:T(8,128)(2,1)}, bf16[2,2,32,5120]{3,2,1,0:T(8,128)(2,1)S(1)}, u32[]{:S(2)}, u32[]{:S(2)}) collective-permute-start(bf16[2,2,32,5120]{3,2,1,0:T(8,128)(2,1)} %shard_map.63), channel_id=1, source_target_pairs={{16,32},{48,64},{80,96},{112,128},{144,160},{176,192},{208,224},{3... | collective-permute-start | bytes 3932168 | tf_op jit(solution)/shard_map/ppermute | solution.py:326
  21.4 0.7 and_select_fusion.1
  22.1 0.0 copy-done
  22.1 0.0 copy-done.1
  22.1 0.0 copy-done.2
  22.1 0.0 copy-done.3
  22.1 0.7 fusion.3
  22.8 0.1 subtract_reduce_fusion
  22.9 0.0 collective-permute-done.refs_2_
  22.9 9.7 %shard_map.60.refs_1_ = f32[16,14,256]{2,1,0:T(8,128)S(1)} custom-call(s32[1]{0:T(128)S(6)} %sub.56.refs_0_, bf16[2,4,80,5120]{3,2,1,0:T(8,128)(2,1)} %refs_3_.1, bf16[2,4,80,5120]{3,2,1,0:T(8,128)(2,1)} %collective-permute-done.refs_2_), custom_call_target="tpu_custom_call" | custom-call | tf_op jit(solution)/shard_map/pallas_call | solution.py:110
  32.7 0.0 collective-permute-done.1.refs_1_
  32.7 6.3 %shard_map.62.refs_2_ = f32[11,14,256]{2,1,0:T(8,128)S(1)} custom-call(s32[1]{0:T(128)} %bitcast.flip_ref.refs_0_.odd_ref, bf16[2,2,48,5120]{3,2,1,0:T(8,128)(2,1)S(1)} %collective-permute-done.1.refs_1_, bf16[2,4,80,5120]{3,2,1,0:T(8,128)(2,1)} %refs_3_.1, bf16[2,4,80,5120]{3,2,1,0:T(8,128)(2,1)} %refs_3_.1, bf16[2,4,80,5120]{3,2,1,0:T(8,128)(2,1)} %refs_3_.1), custom_call_target="tpu_custom_call" | custom-call | tf_op jit(solution)/shard_map/pallas_call | solution.py:110
  39.0 4.3 %collective-permute-start.4 = (f32[1,44,256]{2,1,0:T(8,128)S(1)}, f32[1,44,256]{2,1,0:T(8,128)S(1)}, u32[]{:S(2)}, u32[]{:S(2)}) collective-permute-start(f32[1,44,256]{2,1,0:T(8,128)S(1)} %pad_maximum_fusion.1), channel_id=1, source_target_pairs={{1,0},{2,1},{3,2},{4,3},{5,4},{6,5},{7,6},{8,7},{9,8},{10,9},{11,1... | collective-permute-start | bytes 135176 | tf_op jit(solution)/shard_map/ppermute | solution.py:321
  43.3 1.9 %collective-permute-start.3 = (f32[1,44,256]{2,1,0:T(8,128)S(1)}, f32[1,44,256]{2,1,0:T(8,128)S(1)}, u32[]{:S(2)}, u32[]{:S(2)}) collective-permute-start(f32[1,44,256]{2,1,0:T(8,128)S(1)} %pad_maximum_fusion), channel_id=1, source_target_pairs={{0,1},{1,2},{2,3},{3,4},{4,5},{5,6},{6,7},{7,8},{8,9},{9,10},{10,1... | collective-permute-start | bytes 135176 | tf_op jit(solution)/shard_map/ppermute | solution.py:321
  45.3 0.2 convert_reduce_fusion
  45.5 0.0 collective-permute-done.2.refs_1_
  45.5 5.2 %shard_map.64.refs_3_ = f32[7,14,256]{2,1,0:T(8,128)S(1)} custom-call(s32[1]{0:T(128)} %bitcast.flip_ref.refs_0_.odd_ref, bf16[2,2,32,5120]{3,2,1,0:T(8,128)(2,1)S(1)} %collective-permute-done.2.refs_1_, bf16[2,4,80,5120]{3,2,1,0:T(8,128)(2,1)} %refs_3_.1, bf16[2,4,80,5120]{3,2,1,0:T(8,128)(2,1)} %refs_3_.1), custom_call_target="tpu_custom_call" | custom-call | tf_op jit(solution)/shard_map/pallas_call | solution.py:110
  50.6 0.0 collective-permute-done.4.refs_5_
  50.7 0.0 collective-permute-done.3.refs_4_
  50.7 0.8 shard_map.65
  51.5 4.5 %collective-permute-start.5 = (f32[256,128]{1,0:T(8,128)S(1)}, f32[256,128]{1,0:T(8,128)S(1)}, u32[]{:S(2)}, u32[]{:S(2)}) collective-permute-start(f32[256,128]{1,0:T(8,128)S(1)} %get-tuple-element.16), channel_id=1, source_target_pairs={{16,32},{48,64},{80,96},{112,128},{144,160},{176,192},{208,224},{3... | collective-permute-start | bytes 393224 | tf_op jit(solution)/shard_map/ppermute | solution.py:326
  56.0 0.1 collective-permute-start.6
  56.1 0.1 select_reduce_fusion.1.sign_ref
  56.2 0.1 select_reduce_fusion.2.slot_ref
  56.3 2.3 %collective-permute-done.5.refs_1_ = f32[256,128]{1,0:T(8,128)S(1)} collective-permute-done((f32[256,128]{1,0:T(8,128)S(1)}, f32[256,128]{1,0:T(8,128)S(1)}, u32[]{:S(2)}, u32[]{:S(2)}) %collective-permute-start.5) | collective-permute-done | bytes 131104 | tf_op jit(solution)/shard_map/ppermute | solution.py:326
  58.6 0.0 collective-permute-done.6.refs_2_
  58.6 1.5 %shard_map.66 = (s16[16,64,128]{2,1,0:T(8,128)(2,1)S(1)}, f32[2,4,4096]{2,1,0:T(4,128)}) custom-call(s32[1]{0:T(128)} %bitcast.flip_ref.refs_0_.odd_ref, s32[16]{0:T(128)S(1)} %select_reduce_fusion.2.slot_ref, f32[16]{0:T(128)S(1)} %select_reduce_fusion.1.sign_ref, f32[26]{0:T(128)S(1)} %convert_element_type.15.count_ref, ...), custom_call_target="tpu_custom_call" | custom-call | tf_op jit(solution)/shard_map/pallas_call | solution.py:279
  60.1 22.6 %all_to_all.5.arrived_ref = s16[16,64,128]{2,1,0:T(8,128)(2,1)S(1)} all-to-all(s16[16,64,128]{2,1,0:T(8,128)(2,1)S(1)} %get-tuple-element.18), channel_id=1, replica_groups=mesh['date'=16,'strip'=16] {'date'}, dimensions={0} | all-to-all | bytes 524288 | tf_op jit(solution)/shard_map/all_to_all | solution.py:435
  82.7 1.1 %shard_map.67 = f32[2,16,4096]{2,1,0:T(8,128)} custom-call(s16[16,64,128]{2,1,0:T(8,128)(2,1)S(1)} %all_to_all.5.arrived_ref), custom_call_target="tpu_custom_call" | custom-call | tf_op jit(solution)/shard_map/pallas_call | solution.py:310
  (8 shorter events, 0.1 us)
Async XLA Ops:
  0.6 22.3 %collective-permute-start = (bf16[2,4,80,5120]{3,2,1,0:T(8,128)(2,1)}, bf16[2,4,80,5120]{3,2,1,0:T(8,128)(2,1)}, u32[]{:S(2)}, u32[]{:S(2)}) collective-permute-start(bf16[2,4,80,5120]{3,2,1,0:T(8,128)(2,1)} %refs_3_.1), channel_id=1, source_target_pairs={{0,16},{32,48},{64,80},{96,112},{128,144},{160,176},{192,208},{224... | collective-permute-start | bytes 19660808 | tf_op jit(solution)/shard_map/ppermute | solution.py:331
  3.9 28.8 %collective-permute-start.1 = (bf16[2,2,48,5120]{3,2,1,0:T(8,128)(2,1)}, bf16[2,2,48,5120]{3,2,1,0:T(8,128)(2,1)S(1)}, u32[]{:S(2)}, u32[]{:S(2)}) collective-permute-start(bf16[2,2,48,5120]{3,2,1,0:T(8,128)(2,1)} %shard_map.61), channel_id=1, source_target_pairs={{16,32},{48,64},{80,96},{112,128},{144,160},{176,192},{208,224},{3... | collective-permute-start | bytes 5898248 | tf_op jit(solution)/shard_map/ppermute | solution.py:326
  16.9 5.2 %copy-start = (s32[128,2]{0,1:T(2,128)S(1)}, s32[128,2]{0,1:T(2,128)}, u32[]{:S(2)}) copy-start(s32[128,2]{0,1:T(2,128)} %param.5) | copy-start | bytes 3076
  16.9 5.2 %copy-start.1 = (pred[26,1]{0,1:T(4,128)(4,1)S(1)}, pred[26,1]{0,1:T(4,128)(4,1)}, u32[]{:S(2)}) copy-start(pred[26,1]{0,1:T(4,128)(4,1)} %constant.62) | copy-start | bytes 82
  16.9 5.2 %copy-start.2 = (s32[26,1]{0,1:T(1,128)S(1)}, s32[26,1]{0,1:T(1,128)}, u32[]{:S(2)}) copy-start(s32[26,1]{0,1:T(1,128)} %constant.69) | copy-start | bytes 316
  16.9 5.2 %copy-start.3 = (s32[26,1]{0,1:T(1,128)S(1)}, s32[26,1]{0,1:T(1,128)}, u32[]{:S(2)}) copy-start(s32[26,1]{0,1:T(1,128)} %constant.70) | copy-start | bytes 316
  19.2 26.2 %collective-permute-start.2 = (bf16[2,2,32,5120]{3,2,1,0:T(8,128)(2,1)}, bf16[2,2,32,5120]{3,2,1,0:T(8,128)(2,1)S(1)}, u32[]{:S(2)}, u32[]{:S(2)}) collective-permute-start(bf16[2,2,32,5120]{3,2,1,0:T(8,128)(2,1)} %shard_map.63), channel_id=1, source_target_pairs={{16,32},{48,64},{80,96},{112,128},{144,160},{176,192},{208,224},{3... | collective-permute-start | bytes 3932168 | tf_op jit(solution)/shard_map/ppermute | solution.py:326
  39.0 11.6 %collective-permute-start.4 = (f32[1,44,256]{2,1,0:T(8,128)S(1)}, f32[1,44,256]{2,1,0:T(8,128)S(1)}, u32[]{:S(2)}, u32[]{:S(2)}) collective-permute-start(f32[1,44,256]{2,1,0:T(8,128)S(1)} %pad_maximum_fusion.1), channel_id=1, source_target_pairs={{1,0},{2,1},{3,2},{4,3},{5,4},{6,5},{7,6},{8,7},{9,8},{10,9},{11,1... | collective-permute-start | bytes 135176 | tf_op jit(solution)/shard_map/ppermute | solution.py:321
  43.3 7.3 %collective-permute-start.3 = (f32[1,44,256]{2,1,0:T(8,128)S(1)}, f32[1,44,256]{2,1,0:T(8,128)S(1)}, u32[]{:S(2)}, u32[]{:S(2)}) collective-permute-start(f32[1,44,256]{2,1,0:T(8,128)S(1)} %pad_maximum_fusion), channel_id=1, source_target_pairs={{0,1},{1,2},{2,3},{3,4},{4,5},{5,6},{6,7},{7,8},{8,9},{9,10},{10,1... | collective-permute-start | bytes 135176 | tf_op jit(solution)/shard_map/ppermute | solution.py:321
  51.5 7.1 %collective-permute-start.5 = (f32[256,128]{1,0:T(8,128)S(1)}, f32[256,128]{1,0:T(8,128)S(1)}, u32[]{:S(2)}, u32[]{:S(2)}) collective-permute-start(f32[256,128]{1,0:T(8,128)S(1)} %get-tuple-element.16), channel_id=1, source_target_pairs={{16,32},{48,64},{80,96},{112,128},{144,160},{176,192},{208,224},{3... | collective-permute-start | bytes 393224 | tf_op jit(solution)/shard_map/ppermute | solution.py:326
  56.0 2.6 %collective-permute-start.6 = (f32[256,128]{1,0:T(8,128)S(1)}, f32[256,128]{1,0:T(8,128)S(1)}, u32[]{:S(2)}, u32[]{:S(2)}) collective-permute-start(f32[256,128]{1,0:T(8,128)S(1)} %get-tuple-element.17), channel_id=1, source_target_pairs={{0,16},{32,48},{64,80},{96,112},{128,144},{160,176},{192,208},{224... | collective-permute-start | bytes 393224 | tf_op jit(solution)/shard_map/ppermute | solution.py:331

commit v5 on v4

--- a/solution.py
+++ b/solution.py
@@ -12,7 +12,6 @@
 LANES = 128
 TILE = 16
 COLUMNS = 1280
-CHUNK = 256
 FIXED = 32000.0
 EPS_POWER = 1e-06
 MIB = 2**20
@@ -33,12 +32,11 @@
 
 def products_kernel(edges, powers, places, groups, *refs):
     flip = refs[0][0]
-    out_ref, look_ref, even_ref, odd_ref, acc_ref = refs[-5:]
+    out_ref, look_ref, acc_ref = refs[-3:]
     total = 2 * len(edges) + len(powers)
-    rows = acc_ref.shape[0] // total
+    tiles = acc_ref.shape[0] // (total * TILE)
     step = pl.program_id(0)
     used = sorted({k for e in edges for k in e} | set(powers))
-    buffers = (even_ref, odd_ref)
 
     @pl.when(step == 0)
     def _():
@@ -47,57 +45,45 @@
         inside = (column >= begin) & (column < begin + RLOOK)
         look_ref[...] = inside.astype(jnp.float32).astype(jnp.bfloat16)
 
-    def form(chunk):
-        for part in range(CHUNK // LANES):
-            lane = slice(chunk * CHUNK + part * LANES, chunk * CHUNK + (part + 1) * LANES)
-            out_lane = slice(part * LANES, (part + 1) * LANES)
-            for tile in range(rows // TILE):
-                pixel = {}
-                for k in used:
-                    source, date, row = places[k][tile]
-                    ref = refs[1 + source]
-                    date = date + flip * (ref.shape[1] - 1 - 2 * date)
-                    pixel[k] = tuple(
-                        ref[c, date, row : row + TILE, lane].astype(jnp.float32) for c in (0, 1)
-                    )
-                results = []
-                for i, j in edges:
-                    results.append(pixel[i][0] * pixel[j][0] + pixel[i][1] * pixel[j][1])
-                for i, j in edges:
-                    results.append(pixel[i][1] * pixel[j][0] - pixel[i][0] * pixel[j][1])
-                for k in powers:
-                    results.append(pixel[k][0] * pixel[k][0] + pixel[k][1] * pixel[k][1])
-                for p, value in enumerate(results):
-                    first = p * rows + tile * TILE
-                    buffers[chunk % 2][first : first + TILE, out_lane] = value.astype(jnp.bfloat16)
-
-    def add_looks(chunk):
-        row = pl.multiple_of(step % 2 * COLUMNS + chunk * CHUNK, CHUNK)
-        part = jnp.dot(
-            buffers[chunk % 2][...],
-            look_ref[pl.ds(row, CHUNK), :],
-            preferred_element_type=jnp.float32,
-        )
-        if chunk == 0:
-            acc_ref[...] = part + jnp.where(step % 2 == 1, acc_ref[...], 0.0)
-        else:
-            acc_ref[...] += part
-
-    chunks = COLUMNS // CHUNK
-    form(0)
-    for chunk in range(chunks):
-        if chunk + 1 < chunks:
-            form(chunk + 1)
-        add_looks(chunk)
+    def planes(tile, start):
+        pixel = {}
+        for k in used:
+            source, date, row = places[k][tile]
+            ref = refs[1 + source]
+            date = date + flip * (ref.shape[1] - 1 - 2 * date)
+            pixel[k] = tuple(
+                ref[c, date, row : row + TILE, start : start + LANES].astype(jnp.float32)
+                for c in (0, 1)
+            )
+        results = []
+        for i, j in edges:
+            results.append(pixel[i][0] * pixel[j][0] + pixel[i][1] * pixel[j][1])
+        for i, j in edges:
+            results.append(pixel[i][1] * pixel[j][0] - pixel[i][0] * pixel[j][1])
+        for k in powers:
+            results.append(pixel[k][0] * pixel[k][0] + pixel[k][1] * pixel[k][1])
+        return jnp.concatenate([r.astype(jnp.bfloat16) for r in results], axis=0)
+
+    look = look_ref[pl.ds(pl.multiple_of(step % 2 * COLUMNS, COLUMNS), COLUMNS), :]
+    for tile in range(tiles):
+        formed = jnp.concatenate([planes(tile, s) for s in range(0, COLUMNS, LANES)], axis=1)
+        part = jnp.dot(formed, look, preferred_element_type=jnp.float32)
+        span = slice(tile * total * TILE, (tile + 1) * total * TILE)
+        acc_ref[span, :] = part + jnp.where(step % 2 == 1, acc_ref[span, :], 0.0)
 
     @pl.when(step % 2 == 1)
     def _():
         for m, (first, last) in enumerate(groups):
             for p in range(0, total, 8):
                 size = min(8, total - p)
-                value = acc_ref[pl.ds(p * rows + first, size, stride=rows), :]
+
+                def plane_rows(row):
+                    start = (row // TILE * total + p) * TILE + row % TILE
+                    return acc_ref[pl.ds(start, size, stride=TILE), :]
+
+                value = plane_rows(first)
                 for row in range(first + 1, last):
-                    value += acc_ref[pl.ds(p * rows + row, size, stride=rows), :]
+                    value += plane_rows(row)
                 out_ref[m, p : p + size, :] = value
 
 
@@ -115,8 +101,6 @@
         out_specs=pl.BlockSpec((len(groups), total, LANES), lambda i: (0, 0, i // 2)),
         scratch_shapes=[
             pltpu.VMEM((2 * COLUMNS, LANES), jnp.bfloat16),
-            pltpu.VMEM((total * rows, CHUNK), jnp.bfloat16),
-            pltpu.VMEM((total * rows, CHUNK), jnp.bfloat16),
             pltpu.VMEM((total * rows, LANES), jnp.float32),
         ],
         compiler_params=pltpu.CompilerParams(vmem_limit_bytes=48 * MIB),
@@ -201,10 +185,10 @@
             beside_power[k] = power_of(inner, INNER, n)
             across_power[7 - k] = beside_power[k]
         start = 0
-        for values, edges, power, back_ref in (
-            (inner, INNER, beside_power, None),
-            (beside, SIDE, beside_power, beside_back_ref),
-            (across, SIDE, across_power, across_back_ref),
+        for values, edges, power in (
+            (inner, INNER, beside_power),
+            (beside, SIDE, beside_power),
+            (across, SIDE, across_power),
         ):
             size = len(edges)
             first = jnp.concatenate([power[i] for i, _ in edges], axis=0)
@@ -216,9 +200,14 @@
                     row = (part * cells + m) * halves + h
                     piece = value[:, h * LANES : (h + 1) * LANES]
                     formed_ref[pl.ds(start * block + row, size, stride=block), :] = piece
-                    if back_ref is not None:
-                        back_ref[pl.ds(row, BACK, stride=block), :] = piece[:BACK]
             start += size
+    size = BACK * block
+    for back_ref, first in (
+        (beside_back_ref, len(INNER) * block),
+        (across_back_ref, (len(INNER) + len(SIDE)) * block),
+    ):
+        fixed = jnp.round(formed_ref[first : first + size, :] * FIXED)
+        back_ref[...] = fixed.astype(jnp.int32).astype(jnp.int16)
 
 
 def coherences(layout, inner, beside, first, second, before, after):
@@ -227,7 +216,8 @@
     return pl.pallas_call(
         functools.partial(coherence_kernel, layout),
         out_shape=[
-            jax.ShapeDtypeStruct((n * block, LANES), jnp.float32) for n in (FORMED, BACK, BACK)
+            jax.ShapeDtypeStruct((n * block, LANES), dtype)
+            for n, dtype in ((FORMED, jnp.float32), (BACK, jnp.int16), (BACK, jnp.int16))
         ],
         compiler_params=pltpu.CompilerParams(vmem_limit_bytes=32 * MIB),
     )(inner, beside, first, second, before, after)
@@ -238,7 +228,10 @@
     owners, block, _ = out_ref.shape
     start = 0
     for table in refs[:-4]:
-        known_ref[start : start + table.shape[0], :] = table[...]
+        value = table[...]
+        if table.dtype == jnp.int16:
+            value = value.astype(jnp.int32).astype(jnp.float32) * (1.0 / FIXED)
+        known_ref[start : start + table.shape[0], :] = value
         start += table.shape[0]
     for o in range(owners):
         row = pl.multiple_of(slot_ref[o] * block, block)
@@ -376,8 +369,10 @@
     odd = (myself % 2).astype(jnp.int32)[None]
     even = 1 - odd
 
-    beside = swapped_beside(images)
-    across = [swapped_across(packed_rows(odd, images, runs[0], 60))]
+    packed = packed_rows(odd, images, runs[0], 60)
+    later, packed = lax.optimization_barrier((images, packed))
+    across = [swapped_across(packed)]
+    beside = swapped_beside(later)
     slot, sign, count = pair_tables(date_pairs, assignment, myself, owners, local_dates)
 
     all_groups = row_groups(range(tiles), cells)[0]

time: 85 us -> 81.2 us (0.955)
  Pallas kernels: 38.9 us -> 34.2 us
  waiting for transfers between devices: 2.31 us -> 4.26 us
  starting transfers between devices: 17.2 us -> 16.2 us
    pallas_call x4, Pallas kernels: 30.8 us -> 26.2 us  [looked_products(): pl.pallas_call(functools.partial(products_kernel, edges, powers, places,...]
    ppermute x3, waiting for transfers between devices: 2.3 us -> 4.25 us  [swapped_across(): return lax.ppermute(value, 'date', pairs + [(b, a) for a, b in pairs])]
    ppermute x3, starting transfers between devices: 10.1 us -> 9.15 us  [swapped_across(): return lax.ppermute(value, 'date', pairs + [(b, a) for a, b in pairs])]
  transfers between devices with their start and end apart: 7 -> 7, of which waited for: 1 -> 3; matrix products, arithmetic and copies ran while one was open for 2% -> 2% of each run, Pallas kernels for 42% -> 36%
where the time goes in v5:
time: 81.2 us; the launch traced here: 79.9 us
  Pallas kernels  34.2 us (42%)
  blocking collectives  22.4 us (28%)
  starting transfers between devices  16.2 us (20%)
  waiting for transfers between devices  4.26 us (5%)
  other arithmetic  1.9 us (2%)
  between operations  0.9 us (1%)
    pallas_call x4, Pallas kernels, looked_products(): pl.pallas_call(functools.partial(products_kernel, edges, powers, places,...  26.2 us
    all_to_all x1, blocking collectives, on_device(): lax.all_to_all(outgoing, 'date', split_axis=0, concat_axis=0, tiled=True)  22.4 us
    ppermute x3, starting transfers between devices, swapped_across(): return lax.ppermute(value, 'date', pairs + [(b, a) for a, b in pairs])  9.15 us
    ppermute x2, starting transfers between devices, shifted(): lax.ppermute(value, axis, [(source, source + steps) for source in range(f...  6.19 us
    pallas_call x2, Pallas kernels, packed_rows(): pl.pallas_call(functools.partial(pack_kernel, runs), out_shape=jax.ShapeD...  4.75 us
    ppermute x3, waiting for transfers between devices, swapped_across(): return lax.ppermute(value, 'date', pairs + [(b, a) for a, b in pairs])  4.25 us
  transfers between devices with their start and end apart: 7, of which 3 were waited for; matrix products, arithmetic and copies ran while one was open for 2% of the time, Pallas kernels for 36%

profile of v5, /device:TPU:9, one launch (start us, length us, event | category | flops | bytes accessed | tf_op | source)
XLA Modules:
  0.0 79.9 jit_solution(7139442648242937039)
XLA Ops:
  0.6 2.5 %shard_map.60 = bf16[2,2,48,5120]{3,2,1,0:T(8,128)(2,1)} custom-call(s32[1]{0:T(128)} %bitcast.flip_ref.refs_0_.odd_ref, bf16[2,4,80,5120]{3,2,1,0:T(8,128)(2,1)} %refs_3_.1), custom_call_target="tpu_custom_call" | custom-call | tf_op jit(solution)/shard_map/pallas_call | solution.py:140
  3.1 0.8 collective-permute-start
  3.9 3.4 %collective-permute-start.1 = (bf16[2,2,48,5120]{3,2,1,0:T(8,128)(2,1)}, bf16[2,2,48,5120]{3,2,1,0:T(8,128)(2,1)S(1)}, u32[]{:S(2)}, u32[]{:S(2)}) collective-permute-start(bf16[2,2,48,5120]{3,2,1,0:T(8,128)(2,1)} %shard_map.60), channel_id=1, source_target_pairs={{16,32},{48,64},{80,96},{112,128},{144,160},{176,192},{208,224},{3... | collective-permute-start | bytes 5898248 | tf_op jit(solution)/shard_map/ppermute | solution.py:319
  7.3 7.5 %shard_map.59.refs_0_ = f32[16,16,256]{2,1,0:T(8,128)S(1)} custom-call(s32[1]{0:T(128)S(6)} %sub.56.refs_0_, bf16[2,4,80,5120]{3,2,1,0:T(8,128)(2,1)} %refs_3_.1), custom_call_target="tpu_custom_call" | custom-call | tf_op jit(solution)/shard_map/pallas_call | solution.py:96
  14.9 0.0 copy-start
  14.9 0.0 copy-start.1
  14.9 0.0 copy-start.2
  14.9 0.0 copy-start.3
  14.9 2.3 %shard_map.63 = bf16[2,2,32,5120]{3,2,1,0:T(8,128)(2,1)} custom-call(s32[1]{0:T(128)} %bitcast.flip_ref.refs_0_.odd_ref, bf16[2,4,80,5120]{3,2,1,0:T(8,128)(2,1)} %refs_3_.1), custom_call_target="tpu_custom_call" | custom-call | tf_op jit(solution)/shard_map/pallas_call | solution.py:140
  17.2 2.3 %collective-permute-start.2 = (bf16[2,2,32,5120]{3,2,1,0:T(8,128)(2,1)}, bf16[2,2,32,5120]{3,2,1,0:T(8,128)(2,1)S(1)}, u32[]{:S(2)}, u32[]{:S(2)}) collective-permute-start(bf16[2,2,32,5120]{3,2,1,0:T(8,128)(2,1)} %shard_map.63), channel_id=1, source_target_pairs={{16,32},{48,64},{80,96},{112,128},{144,160},{176,192},{208,224},{3... | collective-permute-start | bytes 3932168 | tf_op jit(solution)/shard_map/ppermute | solution.py:319
  19.5 0.0 copy-done
  19.5 0.0 copy-done.1
  19.6 0.0 copy-done.2
  19.6 0.0 copy-done.3
  19.6 0.7 fusion.3
  20.3 0.1 subtract_reduce_fusion
  20.4 0.7 and_select_fusion.1
  21.0 0.2 convert_reduce_fusion
  21.2 0.0 collective-permute-done.refs_2_
  21.2 8.5 %shard_map.61.refs_1_ = f32[16,14,256]{2,1,0:T(8,128)S(1)} custom-call(s32[1]{0:T(128)S(6)} %sub.56.refs_0_, bf16[2,4,80,5120]{3,2,1,0:T(8,128)(2,1)} %refs_3_.1, bf16[2,4,80,5120]{3,2,1,0:T(8,128)(2,1)} %collective-permute-done.refs_2_), custom_call_target="tpu_custom_call" | custom-call | tf_op jit(solution)/shard_map/pallas_call | solution.py:96
  29.8 0.3 collective-permute-done.1.refs_1_
  30.0 5.6 %shard_map.62.refs_2_ = f32[11,14,256]{2,1,0:T(8,128)S(1)} custom-call(s32[1]{0:T(128)} %bitcast.flip_ref.refs_0_.odd_ref, bf16[2,2,48,5120]{3,2,1,0:T(8,128)(2,1)S(1)} %collective-permute-done.1.refs_1_, bf16[2,4,80,5120]{3,2,1,0:T(8,128)(2,1)} %refs_3_.1, bf16[2,4,80,5120]{3,2,1,0:T(8,128)(2,1)} %refs_3_.1, bf16[2,4,80,5120]{3,2,1,0:T(8,128)(2,1)} %refs_3_.1), custom_call_target="tpu_custom_call" | custom-call | tf_op jit(solution)/shard_map/pallas_call | solution.py:96
  35.7 4.3 %collective-permute-start.4 = (f32[1,44,256]{2,1,0:T(8,128)S(1)}, f32[1,44,256]{2,1,0:T(8,128)S(1)}, u32[]{:S(2)}, u32[]{:S(2)}) collective-permute-start(f32[1,44,256]{2,1,0:T(8,128)S(1)} %pad_maximum_fusion.1), channel_id=1, source_target_pairs={{1,0},{2,1},{3,2},{4,3},{5,4},{6,5},{7,6},{8,7},{9,8},{10,9},{11,1... | collective-permute-start | bytes 135176 | tf_op jit(solution)/shard_map/ppermute | solution.py:314
  40.0 1.9 %collective-permute-start.3 = (f32[1,44,256]{2,1,0:T(8,128)S(1)}, f32[1,44,256]{2,1,0:T(8,128)S(1)}, u32[]{:S(2)}, u32[]{:S(2)}) collective-permute-start(f32[1,44,256]{2,1,0:T(8,128)S(1)} %pad_maximum_fusion), channel_id=1, source_target_pairs={{0,1},{1,2},{2,3},{3,4},{4,5},{5,6},{6,7},{7,8},{8,9},{9,10},{10,1... | collective-permute-start | bytes 135176 | tf_op jit(solution)/shard_map/ppermute | solution.py:314
  41.9 0.1 select_reduce_fusion.1.sign_ref
  42.0 2.0 %collective-permute-done.2.refs_1_ = bf16[2,2,32,5120]{3,2,1,0:T(8,128)(2,1)S(1)} collective-permute-done((bf16[2,2,32,5120]{3,2,1,0:T(8,128)(2,1)}, bf16[2,2,32,5120]{3,2,1,0:T(8,128)(2,1)S(1)}, u32[]{:S(2)}, u32[]{:S(2)}) %collective-permute-start.2) | collective-permute-done | bytes 1310752 | tf_op jit(solution)/shard_map/ppermute | solution.py:319
  44.1 4.5 %shard_map.64.refs_3_ = f32[7,14,256]{2,1,0:T(8,128)S(1)} custom-call(s32[1]{0:T(128)} %bitcast.flip_ref.refs_0_.odd_ref, bf16[2,2,32,5120]{3,2,1,0:T(8,128)(2,1)S(1)} %collective-permute-done.2.refs_1_, bf16[2,4,80,5120]{3,2,1,0:T(8,128)(2,1)} %refs_3_.1, bf16[2,4,80,5120]{3,2,1,0:T(8,128)(2,1)} %refs_3_.1), custom_call_target="tpu_custom_call" | custom-call | tf_op jit(solution)/shard_map/pallas_call | solution.py:96
  48.6 0.0 collective-permute-done.4.refs_5_
  48.6 0.0 collective-permute-done.3.refs_4_
  48.6 0.6 shard_map.65
  49.3 3.4 %collective-permute-start.5 = (s16[256,128]{1,0:T(8,128)(2,1)S(1)}, s16[256,128]{1,0:T(8,128)(2,1)S(1)}, u32[]{:S(2)}, u32[]{:S(2)}) collective-permute-start(s16[256,128]{1,0:T(8,128)(2,1)S(1)} %get-tuple-element.20), channel_id=1, source_target_pairs={{16,32},{48,64},{80,96},{112,128},{144,160},{176,192},{208,224},{3... | collective-permute-start | bytes 196616 | tf_op jit(solution)/shard_map/ppermute | solution.py:319
  52.7 0.1 collective-permute-start.6
  52.8 0.1 select_reduce_fusion.2.slot_ref
  52.9 2.0 %collective-permute-done.5.refs_1_ = s16[256,128]{1,0:T(8,128)(2,1)S(1)} collective-permute-done((s16[256,128]{1,0:T(8,128)(2,1)S(1)}, s16[256,128]{1,0:T(8,128)(2,1)S(1)}, u32[]{:S(2)}, u32[]{:S(2)}) %collective-permute-start.5) | collective-permute-done | bytes 65568 | tf_op jit(solution)/shard_map/ppermute | solution.py:319
  54.9 0.0 collective-permute-done.6.refs_2_
  54.9 1.5 %shard_map.66 = (s16[16,64,128]{2,1,0:T(8,128)(2,1)S(1)}, f32[2,4,4096]{2,1,0:T(4,128)}) custom-call(s32[1]{0:T(128)} %bitcast.flip_ref.refs_0_.odd_ref, s32[16]{0:T(128)S(1)} %select_reduce_fusion.2.slot_ref, f32[16]{0:T(128)S(1)} %select_reduce_fusion.1.sign_ref, f32[26]{0:T(128)S(1)} %convert_element_type.15.count_ref, ...), custom_call_target="tpu_custom_call" | custom-call | tf_op jit(solution)/shard_map/pallas_call | solution.py:272
  56.3 22.4 %all_to_all.5.arrived_ref = s16[16,64,128]{2,1,0:T(8,128)(2,1)S(1)} all-to-all(s16[16,64,128]{2,1,0:T(8,128)(2,1)S(1)} %get-tuple-element.22), channel_id=1, replica_groups=mesh['date'=16,'strip'=16] {'date'}, dimensions={0} | all-to-all | bytes 524288 | tf_op jit(solution)/shard_map/all_to_all | solution.py:430
  78.7 1.1 %shard_map.67 = f32[2,16,4096]{2,1,0:T(8,128)} custom-call(s16[16,64,128]{2,1,0:T(8,128)(2,1)S(1)} %all_to_all.5.arrived_ref), custom_call_target="tpu_custom_call" | custom-call | tf_op jit(solution)/shard_map/pallas_call | solution.py:303
  (8 shorter events, 0.1 us)
Async XLA Ops:
  3.1 18.1 %collective-permute-start = (bf16[2,4,80,5120]{3,2,1,0:T(8,128)(2,1)}, bf16[2,4,80,5120]{3,2,1,0:T(8,128)(2,1)}, u32[]{:S(2)}, u32[]{:S(2)}) collective-permute-start(bf16[2,4,80,5120]{3,2,1,0:T(8,128)(2,1)} %refs_3_.1), channel_id=1, source_target_pairs={{0,16},{32,48},{64,80},{96,112},{128,144},{160,176},{192,208},{224... | collective-permute-start | bytes 19660808 | tf_op jit(solution)/shard_map/ppermute | solution.py:324
  3.9 26.1 %collective-permute-start.1 = (bf16[2,2,48,5120]{3,2,1,0:T(8,128)(2,1)}, bf16[2,2,48,5120]{3,2,1,0:T(8,128)(2,1)S(1)}, u32[]{:S(2)}, u32[]{:S(2)}) collective-permute-start(bf16[2,2,48,5120]{3,2,1,0:T(8,128)(2,1)} %shard_map.60), channel_id=1, source_target_pairs={{16,32},{48,64},{80,96},{112,128},{144,160},{176,192},{208,224},{3... | collective-permute-start | bytes 5898248 | tf_op jit(solution)/shard_map/ppermute | solution.py:319
  14.9 4.7 %copy-start = (s32[128,2]{0,1:T(2,128)S(1)}, s32[128,2]{0,1:T(2,128)}, u32[]{:S(2)}) copy-start(s32[128,2]{0,1:T(2,128)} %param.5) | copy-start | bytes 3076
  14.9 4.7 %copy-start.1 = (pred[26,1]{0,1:T(4,128)(4,1)S(1)}, pred[26,1]{0,1:T(4,128)(4,1)}, u32[]{:S(2)}) copy-start(pred[26,1]{0,1:T(4,128)(4,1)} %constant.62) | copy-start | bytes 82
  14.9 4.7 %copy-start.2 = (s32[26,1]{0,1:T(1,128)S(1)}, s32[26,1]{0,1:T(1,128)}, u32[]{:S(2)}) copy-start(s32[26,1]{0,1:T(1,128)} %constant.69) | copy-start | bytes 316
  14.9 4.7 %copy-start.3 = (s32[26,1]{0,1:T(1,128)S(1)}, s32[26,1]{0,1:T(1,128)}, u32[]{:S(2)}) copy-start(s32[26,1]{0,1:T(1,128)} %constant.70) | copy-start | bytes 316
  17.2 26.9 %collective-permute-start.2 = (bf16[2,2,32,5120]{3,2,1,0:T(8,128)(2,1)}, bf16[2,2,32,5120]{3,2,1,0:T(8,128)(2,1)S(1)}, u32[]{:S(2)}, u32[]{:S(2)}) collective-permute-start(bf16[2,2,32,5120]{3,2,1,0:T(8,128)(2,1)} %shard_map.63), channel_id=1, source_target_pairs={{16,32},{48,64},{80,96},{112,128},{144,160},{176,192},{208,224},{3... | collective-permute-start | bytes 3932168 | tf_op jit(solution)/shard_map/ppermute | solution.py:319
  35.7 12.9 %collective-permute-start.4 = (f32[1,44,256]{2,1,0:T(8,128)S(1)}, f32[1,44,256]{2,1,0:T(8,128)S(1)}, u32[]{:S(2)}, u32[]{:S(2)}) collective-permute-start(f32[1,44,256]{2,1,0:T(8,128)S(1)} %pad_maximum_fusion.1), channel_id=1, source_target_pairs={{1,0},{2,1},{3,2},{4,3},{5,4},{6,5},{7,6},{8,7},{9,8},{10,9},{11,1... | collective-permute-start | bytes 135176 | tf_op jit(solution)/shard_map/ppermute | solution.py:314
  40.0 8.6 %collective-permute-start.3 = (f32[1,44,256]{2,1,0:T(8,128)S(1)}, f32[1,44,256]{2,1,0:T(8,128)S(1)}, u32[]{:S(2)}, u32[]{:S(2)}) collective-permute-start(f32[1,44,256]{2,1,0:T(8,128)S(1)} %pad_maximum_fusion), channel_id=1, source_target_pairs={{0,1},{1,2},{2,3},{3,4},{4,5},{5,6},{6,7},{7,8},{8,9},{9,10},{10,1... | collective-permute-start | bytes 135176 | tf_op jit(solution)/shard_map/ppermute | solution.py:314
  49.3 5.6 %collective-permute-start.5 = (s16[256,128]{1,0:T(8,128)(2,1)S(1)}, s16[256,128]{1,0:T(8,128)(2,1)S(1)}, u32[]{:S(2)}, u32[]{:S(2)}) collective-permute-start(s16[256,128]{1,0:T(8,128)(2,1)S(1)} %get-tuple-element.20), channel_id=1, source_target_pairs={{16,32},{48,64},{80,96},{112,128},{144,160},{176,192},{208,224},{3... | collective-permute-start | bytes 196616 | tf_op jit(solution)/shard_map/ppermute | solution.py:319
  52.7 2.2 %collective-permute-start.6 = (s16[256,128]{1,0:T(8,128)(2,1)S(1)}, s16[256,128]{1,0:T(8,128)(2,1)S(1)}, u32[]{:S(2)}, u32[]{:S(2)}) collective-permute-start(s16[256,128]{1,0:T(8,128)(2,1)S(1)} %get-tuple-element.21), channel_id=1, source_target_pairs={{0,16},{32,48},{64,80},{96,112},{128,144},{160,176},{192,208},{224... | collective-permute-start | bytes 196616 | tf_op jit(solution)/shard_map/ppermute | solution.py:324

commit v6 on v5

--- a/solution.py
+++ b/solution.py
@@ -107,31 +107,22 @@
     )(flip, *[s[0] for s in sources])
 
 
-def pack_kernel(runs, flip_ref, images_ref, out_ref, held_ref, in_sems, out_sems):
+def pack_kernel(runs, flip_ref, images_ref, out_ref, semaphores):
     first = 2 * flip_ref[0]
-    loads, stores = [], []
+    copies = []
     for c in range(2):
         for row, target, size in runs:
-            held = held_ref.at[c, :, target : target + size, :]
-            loads.append(
+            copies.append(
                 pltpu.make_async_copy(
                     images_ref.at[c, pl.ds(first, 2), row : row + size, :],
-                    held,
-                    in_sems.at[len(loads)],
+                    out_ref.at[c, :, target : target + size, :],
+                    semaphores.at[len(copies)],
                 )
             )
-            stores.append(
-                pltpu.make_async_copy(
-                    held, out_ref.at[c, :, target : target + size, :], out_sems.at[len(stores)]
-                )
-            )
-    for load in loads:
-        load.start()
-    for load, store in zip(loads, stores):
-        load.wait()
-        store.start()
-    for store in stores:
-        store.wait()
+    for copy in copies:
+        copy.start()
+    for copy in copies:
+        copy.wait()
 
 
 def packed_rows(flip, images, runs, limit):
@@ -141,12 +132,8 @@
         functools.partial(pack_kernel, runs),
         out_shape=jax.ShapeDtypeStruct((2, 2, rows, columns), images.dtype),
         in_specs=[pl.BlockSpec(memory_space=pltpu.SMEM), pl.BlockSpec(memory_space=pl.ANY)],
-        out_specs=pl.BlockSpec(memory_space=pl.ANY),
-        scratch_shapes=[
-            pltpu.VMEM((2, 2, rows, columns), images.dtype),
-            pltpu.SemaphoreType.DMA((2 * len(runs),)),
-            pltpu.SemaphoreType.DMA((2 * len(runs),)),
-        ],
+        out_specs=pl.BlockSpec(memory_space=pltpu.VMEM),
+        scratch_shapes=[pltpu.SemaphoreType.DMA((2 * len(runs),))],
         compiler_params=pltpu.CompilerParams(vmem_limit_bytes=limit * MIB),
     )(flip, images)
 
@@ -223,9 +210,10 @@
     )(inner, beside, first, second, before, after)
 
 
-def slots_kernel(odd_ref, slot_ref, sign_ref, count_ref, *refs):
+def slots_kernel(scalar_ref, *refs):
     out_ref, sums_ref, known_ref, rows_ref = refs[-4:]
     owners, block, _ = out_ref.shape
+    odd = scalar_ref[0]
     start = 0
     for table in refs[:-4]:
         value = table[...]
@@ -234,10 +222,11 @@
         known_ref[start : start + table.shape[0], :] = value
         start += table.shape[0]
     for o in range(owners):
-        row = pl.multiple_of(slot_ref[o] * block, block)
+        row = pl.multiple_of(scalar_ref[1 + o] * block, block)
         value = known_ref[pl.ds(row, block), :]
         half = block // 2
-        scales = (jnp.abs(sign_ref[o]) * FIXED, sign_ref[o] * FIXED)
+        sign = scalar_ref[1 + owners + o].astype(jnp.float32)
+        scales = (jnp.abs(sign) * FIXED, sign * FIXED)
         for part in range(2):
             fixed = jnp.round(value[part * half : (part + 1) * half] * scales[part])
             out_ref[o, part * half : (part + 1) * half, :] = fixed.astype(jnp.int32).astype(jnp.int16)
@@ -247,7 +236,8 @@
         totals = {k: jnp.zeros((tiles, LANES), jnp.float32) for k in OWN_PLACES}
         for e, (first, second, across) in enumerate(KNOWN):
             row = (e * parts + part) * tiles
-            value = known_ref[row : row + tiles, :] * count_ref[e]
+            count = scalar_ref[1 + 2 * owners + e].astype(jnp.float32)
+            value = known_ref[row : row + tiles, :] * count
             for k in OWN_PLACES:
                 place = k if across else 7 - k
                 if place == first or (place == second and part == 0):
@@ -255,7 +245,7 @@
                 elif place == second:
                     totals[k] = totals[k] - value
         for d, k in enumerate(OWN_PLACES):
-            date = d + odd_ref[0] * (dates - 1 - 2 * d)
+            date = d + odd * (dates - 1 - 2 * d)
             first = pl.multiple_of((part * dates + date) * tiles, tiles)
             rows_ref[pl.ds(first, tiles), :] = totals[k]
     for part in range(parts):
@@ -265,7 +255,7 @@
             ]
 
 
-def slots_and_sums(odd, slot, sign, count, tables, owners, local_dates, cell_count):
+def slots_and_sums(scalars, tables, owners, local_dates, cell_count):
     smem = pl.BlockSpec(memory_space=pltpu.SMEM)
     vmem = pl.BlockSpec(memory_space=pltpu.VMEM)
     block = 2 * cell_count // LANES
@@ -275,13 +265,13 @@
             jax.ShapeDtypeStruct((owners, block, LANES), jnp.int16),
             jax.ShapeDtypeStruct((2, local_dates, cell_count), jnp.float32),
         ],
-        in_specs=[smem] * 4 + [vmem] * len(tables),
+        in_specs=[smem] + [vmem] * len(tables),
         scratch_shapes=[
             pltpu.VMEM((len(KNOWN) * block, LANES), jnp.float32),
             pltpu.VMEM((local_dates * block, LANES), jnp.float32),
         ],
         compiler_params=pltpu.CompilerParams(vmem_limit_bytes=32 * MIB),
-    )(odd, slot, sign, count, *tables)
+    )(scalars, *tables)
 
 
 def table_kernel(arrived_ref, out_ref, rows_ref):
@@ -336,14 +326,14 @@
     forward = (first == known_first) & (second == known_second)
     backward = (first == known_second) & (second == known_first)
     is_edge = forward | backward
-    count = jnp.sum(is_edge, axis=0).astype(jnp.float32)
+    count = jnp.sum(is_edge.astype(jnp.int32), axis=0)
     edge = jnp.sum(jnp.where(is_edge, jnp.arange(len(KNOWN))[None, :], 0), axis=1)
-    way = jnp.sum(forward.astype(jnp.float32) - backward.astype(jnp.float32), axis=1)
+    way = jnp.sum(forward.astype(jnp.int32) - backward.astype(jnp.int32), axis=1)
     mine = date_pairs[:, 0] // local_dates == myself
     matches = (assignment[None, :] // owners == jnp.arange(owners)[:, None]) & mine[None, :]
     slot = jnp.sum(jnp.where(matches, edge[None, :], 0), axis=1)
-    sign = jnp.sum(jnp.where(matches, way[None, :], 0.0), axis=1)
-    return slot, sign, count
+    sign = jnp.sum(jnp.where(matches, way[None, :], 0), axis=1)
+    return jnp.concatenate([(myself % 2)[None], slot, sign, count]).astype(jnp.int32)
 
 
 def row_groups(tiles, cells):
@@ -369,11 +359,11 @@
     odd = (myself % 2).astype(jnp.int32)[None]
     even = 1 - odd
 
-    packed = packed_rows(odd, images, runs[0], 60)
+    packed = packed_rows(odd, images, runs[0], 40)
     later, packed = lax.optimization_barrier((images, packed))
     across = [swapped_across(packed)]
     beside = swapped_beside(later)
-    slot, sign, count = pair_tables(date_pairs, assignment, myself, owners, local_dates)
+    scalars = pair_tables(date_pairs, assignment, myself, owners, local_dates)
 
     all_groups = row_groups(range(tiles), cells)[0]
     own_source = (images, (2, local_dates, rows), (0, 0, 0))
@@ -384,7 +374,7 @@
         even, INNER, OWN_PLACES, [own_source], own_places, all_groups, rows, columns
     )
     later, inner = lax.optimization_barrier((images, inner))
-    across.append(swapped_across(packed_rows(odd, later, runs[1], 60)))
+    across.append(swapped_across(packed_rows(odd, later, runs[1], 40)))
 
     side_places = own_places | {
         d: [(1, local_dates - 2 + d, t * TILE) for t in range(tiles)] for d in range(2)
@@ -424,9 +414,7 @@
         layout, inner, beside_looked, *across_looked, before, after
     )
     tables = (formed, swapped_across(across_back), swapped_beside(beside_back))
-    outgoing, sums = slots_and_sums(
-        odd, slot, sign, count, tables, owners, local_dates, cell_count
-    )
+    outgoing, sums = slots_and_sums(scalars, tables, owners, local_dates, cell_count)
     table = lax.all_to_all(outgoing, "date", split_axis=0, concat_axis=0, tiled=True)
     return (as_table(table, cell_count), sums)
 

time: 81.2 us -> 80 us (0.985)
  transfers between devices with their start and end apart: 7 -> 7, of which waited for: 3 -> 3; matrix products, arithmetic and copies ran while one was open for 2% -> 2% of each run, Pallas kernels for 36% -> 37%
where the time goes in v6:
time: 80 us; the launch traced here: 78.7 us
  Pallas kernels  33.7 us (42%)
  blocking collectives  22.4 us (28%)
  starting transfers between devices  16.3 us (20%)
  waiting for transfers between devices  3.72 us (5%)
  other arithmetic  1.76 us (2%)
  between operations  0.89 us (1%)
    pallas_call x4, Pallas kernels, looked_products(): pl.pallas_call(functools.partial(products_kernel, edges, powers, places,...  26.4 us
    all_to_all x1, blocking collectives, on_device(): lax.all_to_all(outgoing, 'date', split_axis=0, concat_axis=0, tiled=True)  22.4 us
    ppermute x3, starting transfers between devices, swapped_across(): return lax.ppermute(value, 'date', pairs + [(b, a) for a, b in pairs])  9.21 us
    ppermute x2, starting transfers between devices, shifted(): lax.ppermute(value, axis, [(source, source + steps) for source in range(f...  6.19 us
    pallas_call x2, Pallas kernels, packed_rows(): pl.pallas_call(functools.partial(pack_kernel, runs), out_shape=jax.ShapeD...  3.98 us
    ppermute x3, waiting for transfers between devices, swapped_across(): return lax.ppermute(value, 'date', pairs + [(b, a) for a, b in pairs])  3.71 us
  transfers between devices with their start and end apart: 7, of which 3 were waited for; matrix products, arithmetic and copies ran while one was open for 2% of the time, Pallas kernels for 37%

profile of v6, /device:TPU:9, one launch (start us, length us, event | category | flops | bytes accessed | tf_op | source)
XLA Modules:
  0.0 78.7 jit_solution(3450254929753453170)
XLA Ops:
  0.6 1.5 %shard_map.60 = bf16[2,2,48,5120]{3,2,1,0:T(8,128)(2,1)S(1)} custom-call(s32[1]{0:T(128)} %bitcast.flip_ref.refs_0_, bf16[2,4,80,5120]{3,2,1,0:T(8,128)(2,1)} %refs_3_.1), custom_call_target="tpu_custom_call" | custom-call | tf_op jit(solution)/shard_map/pallas_call | solution.py:131
  2.2 0.8 collective-permute-start
  2.9 3.4 %collective-permute-start.1 = (bf16[2,2,48,5120]{3,2,1,0:T(8,128)(2,1)S(1)}, bf16[2,2,48,5120]{3,2,1,0:T(8,128)(2,1)}, u32[]{:S(2)}, u32[]{:S(2)}) collective-permute-start(bf16[2,2,48,5120]{3,2,1,0:T(8,128)(2,1)S(1)} %shard_map.60), channel_id=1, source_target_pairs={{16,32},{48,64},{80,96},{112,128},{144,160},{176,192},{208,224},{3... | collective-permute-start | bytes 5898248 | tf_op jit(solution)/shard_map/ppermute | solution.py:309
  6.4 7.5 %shard_map.59.refs_0_ = f32[16,16,256]{2,1,0:T(8,128)S(1)} custom-call(s32[1]{0:T(128)S(6)} %sub.56.refs_0_, bf16[2,4,80,5120]{3,2,1,0:T(8,128)(2,1)} %refs_3_.1), custom_call_target="tpu_custom_call" | custom-call | tf_op jit(solution)/shard_map/pallas_call | solution.py:96
  13.9 0.0 copy-start
  13.9 0.0 copy-start.1
  13.9 0.0 copy-start.2
  14.0 0.0 copy-start.3
  14.0 2.5 %shard_map.63 = bf16[2,2,32,5120]{3,2,1,0:T(8,128)(2,1)} custom-call(s32[1]{0:T(128)} %bitcast.flip_ref.refs_0_, bf16[2,4,80,5120]{3,2,1,0:T(8,128)(2,1)} %refs_3_.1), custom_call_target="tpu_custom_call" | custom-call | tf_op jit(solution)/shard_map/pallas_call | solution.py:131
  16.4 2.3 %collective-permute-start.2 = (bf16[2,2,32,5120]{3,2,1,0:T(8,128)(2,1)}, bf16[2,2,32,5120]{3,2,1,0:T(8,128)(2,1)S(1)}, u32[]{:S(2)}, u32[]{:S(2)}) collective-permute-start(bf16[2,2,32,5120]{3,2,1,0:T(8,128)(2,1)} %shard_map.63), channel_id=1, source_target_pairs={{16,32},{48,64},{80,96},{112,128},{144,160},{176,192},{208,224},{3... | collective-permute-start | bytes 3932168 | tf_op jit(solution)/shard_map/ppermute | solution.py:309
  18.7 0.7 and_select_fusion.1
  19.4 0.0 copy-done
  19.4 0.0 copy-done.1
  19.4 0.0 copy-done.2
  19.5 0.0 copy-done.3
  19.5 0.7 fusion.3
  20.1 0.2 select_reduce_fusion
  20.4 0.0 collective-permute-done.refs_2_
  20.4 8.5 %shard_map.61.refs_1_ = f32[16,14,256]{2,1,0:T(8,128)S(1)} custom-call(s32[1]{0:T(128)S(6)} %sub.56.refs_0_, bf16[2,4,80,5120]{3,2,1,0:T(8,128)(2,1)} %refs_3_.1, bf16[2,4,80,5120]{3,2,1,0:T(8,128)(2,1)} %collective-permute-done.refs_2_), custom_call_target="tpu_custom_call" | custom-call | tf_op jit(solution)/shard_map/pallas_call | solution.py:96
  28.9 0.1 collective-permute-done.1.refs_1_
  29.0 5.8 %shard_map.62.refs_2_ = f32[11,14,256]{2,1,0:T(8,128)S(1)} custom-call(s32[1]{0:T(128)} %bitcast.flip_ref.refs_0_, bf16[2,2,48,5120]{3,2,1,0:T(8,128)(2,1)} %collective-permute-done.1.refs_1_, bf16[2,4,80,5120]{3,2,1,0:T(8,128)(2,1)} %refs_3_.1, bf16[2,4,80,5120]{3,2,1,0:T(8,128)(2,1)} %refs_3_.1, bf16[2,4,80,5120]{3,2,1,0:T(8,128)(2,1)} %refs_3_.1), custom_call_target="tpu_custom_call" | custom-call | tf_op jit(solution)/shard_map/pallas_call | solution.py:96
  34.9 4.3 %collective-permute-start.4 = (f32[1,44,256]{2,1,0:T(8,128)S(1)}, f32[1,44,256]{2,1,0:T(8,128)S(1)}, u32[]{:S(2)}, u32[]{:S(2)}) collective-permute-start(f32[1,44,256]{2,1,0:T(8,128)S(1)} %pad_maximum_fusion.1), channel_id=1, source_target_pairs={{1,0},{2,1},{3,2},{4,3},{5,4},{6,5},{7,6},{8,7},{9,8},{10,9},{11,1... | collective-permute-start | bytes 135176 | tf_op jit(solution)/shard_map/ppermute | solution.py:304
  39.2 1.9 %collective-permute-start.3 = (f32[1,44,256]{2,1,0:T(8,128)S(1)}, f32[1,44,256]{2,1,0:T(8,128)S(1)}, u32[]{:S(2)}, u32[]{:S(2)}) collective-permute-start(f32[1,44,256]{2,1,0:T(8,128)S(1)} %pad_maximum_fusion), channel_id=1, source_target_pairs={{0,1},{1,2},{2,3},{3,4},{4,5},{5,6},{6,7},{7,8},{8,9},{9,10},{10,1... | collective-permute-start | bytes 135176 | tf_op jit(solution)/shard_map/ppermute | solution.py:304
  41.1 0.1 select_reduce_fusion.2
  41.2 1.7 %collective-permute-done.2.refs_1_ = bf16[2,2,32,5120]{3,2,1,0:T(8,128)(2,1)S(1)} collective-permute-done((bf16[2,2,32,5120]{3,2,1,0:T(8,128)(2,1)}, bf16[2,2,32,5120]{3,2,1,0:T(8,128)(2,1)S(1)}, u32[]{:S(2)}, u32[]{:S(2)}) %collective-permute-start.2) | collective-permute-done | bytes 1310752 | tf_op jit(solution)/shard_map/ppermute | solution.py:309
  42.9 4.5 %shard_map.64.refs_3_ = f32[7,14,256]{2,1,0:T(8,128)S(1)} custom-call(s32[1]{0:T(128)} %bitcast.flip_ref.refs_0_, bf16[2,2,32,5120]{3,2,1,0:T(8,128)(2,1)S(1)} %collective-permute-done.2.refs_1_, bf16[2,4,80,5120]{3,2,1,0:T(8,128)(2,1)} %refs_3_.1, bf16[2,4,80,5120]{3,2,1,0:T(8,128)(2,1)} %refs_3_.1), custom_call_target="tpu_custom_call" | custom-call | tf_op jit(solution)/shard_map/pallas_call | solution.py:96
  47.5 0.0 collective-permute-done.4.refs_5_
  47.5 0.0 collective-permute-done.3.refs_4_
  47.5 0.6 shard_map.65
  48.1 3.5 %collective-permute-start.5 = (s16[256,128]{1,0:T(8,128)(2,1)S(1)}, s16[256,128]{1,0:T(8,128)(2,1)S(1)}, u32[]{:S(2)}, u32[]{:S(2)}) collective-permute-start(s16[256,128]{1,0:T(8,128)(2,1)S(1)} %get-tuple-element.20), channel_id=1, source_target_pairs={{16,32},{48,64},{80,96},{112,128},{144,160},{176,192},{208,224},{3... | collective-permute-start | bytes 196616 | tf_op jit(solution)/shard_map/ppermute | solution.py:309
  51.6 0.1 collective-permute-start.6
  51.7 0.1 pad_add_fusion.scalar_ref
  51.8 1.9 %collective-permute-done.5.refs_1_ = s16[256,128]{1,0:T(8,128)(2,1)S(1)} collective-permute-done((s16[256,128]{1,0:T(8,128)(2,1)S(1)}, s16[256,128]{1,0:T(8,128)(2,1)S(1)}, u32[]{:S(2)}, u32[]{:S(2)}) %collective-permute-start.5) | collective-permute-done | bytes 65568 | tf_op jit(solution)/shard_map/ppermute | solution.py:309
  53.7 0.0 collective-permute-done.6.refs_2_
  53.7 1.5 %shard_map.66 = (s16[16,64,128]{2,1,0:T(8,128)(2,1)S(1)}, f32[2,4,4096]{2,1,0:T(4,128)}) custom-call(s32[59]{0:T(128)S(1)} %pad_add_fusion.scalar_ref, f32[1152,128]{1,0:T(8,128)S(1)} %get-tuple-element.19.refs_0_, s16[256,128]{1,0:T(8,128)(2,1)S(1)} %collective-permute-done.5.refs_1_, s16[256,128]{1,0:T(8,128)(2,1)S(1)} %collective-permute-done.6.refs_2_), custom_call_target="tpu_custom_call" | custom-call | tf_op jit(solution)/shard_map/pallas_call | solution.py:262
  55.2 22.4 %all_to_all.5.arrived_ref = s16[16,64,128]{2,1,0:T(8,128)(2,1)S(1)} all-to-all(s16[16,64,128]{2,1,0:T(8,128)(2,1)S(1)} %get-tuple-element.22), channel_id=1, replica_groups=mesh['date'=16,'strip'=16] {'date'}, dimensions={0} | all-to-all | bytes 524288 | tf_op jit(solution)/shard_map/all_to_all | solution.py:418
  77.6 1.1 %shard_map.67 = f32[2,16,4096]{2,1,0:T(8,128)} custom-call(s16[16,64,128]{2,1,0:T(8,128)(2,1)S(1)} %all_to_all.5.arrived_ref), custom_call_target="tpu_custom_call" | custom-call | tf_op jit(solution)/shard_map/pallas_call | solution.py:293
  (7 shorter events, 0.0 us)
Async XLA Ops:
  2.2 18.2 %collective-permute-start = (bf16[2,4,80,5120]{3,2,1,0:T(8,128)(2,1)}, bf16[2,4,80,5120]{3,2,1,0:T(8,128)(2,1)}, u32[]{:S(2)}, u32[]{:S(2)}) collective-permute-start(bf16[2,4,80,5120]{3,2,1,0:T(8,128)(2,1)} %refs_3_.1), channel_id=1, source_target_pairs={{0,16},{32,48},{64,80},{96,112},{128,144},{160,176},{192,208},{224... | collective-permute-start | bytes 19660808 | tf_op jit(solution)/shard_map/ppermute | solution.py:314
  2.9 26.0 %collective-permute-start.1 = (bf16[2,2,48,5120]{3,2,1,0:T(8,128)(2,1)S(1)}, bf16[2,2,48,5120]{3,2,1,0:T(8,128)(2,1)}, u32[]{:S(2)}, u32[]{:S(2)}) collective-permute-start(bf16[2,2,48,5120]{3,2,1,0:T(8,128)(2,1)S(1)} %shard_map.60), channel_id=1, source_target_pairs={{16,32},{48,64},{80,96},{112,128},{144,160},{176,192},{208,224},{3... | collective-permute-start | bytes 5898248 | tf_op jit(solution)/shard_map/ppermute | solution.py:309
  13.9 5.5 %copy-start = (s32[128,2]{0,1:T(2,128)S(1)}, s32[128,2]{0,1:T(2,128)}, u32[]{:S(2)}) copy-start(s32[128,2]{0,1:T(2,128)} %param.5) | copy-start | bytes 3076
  13.9 5.5 %copy-start.1 = (pred[26,1]{0,1:T(4,128)(4,1)S(1)}, pred[26,1]{0,1:T(4,128)(4,1)}, u32[]{:S(2)}) copy-start(pred[26,1]{0,1:T(4,128)(4,1)} %constant.62) | copy-start | bytes 82
  13.9 5.5 %copy-start.2 = (s32[26,1]{0,1:T(1,128)S(1)}, s32[26,1]{0,1:T(1,128)}, u32[]{:S(2)}) copy-start(s32[26,1]{0,1:T(1,128)} %constant.69) | copy-start | bytes 316
  14.0 5.5 %copy-start.3 = (s32[26,1]{0,1:T(1,128)S(1)}, s32[26,1]{0,1:T(1,128)}, u32[]{:S(2)}) copy-start(s32[26,1]{0,1:T(1,128)} %constant.70) | copy-start | bytes 316
  16.4 26.5 %collective-permute-start.2 = (bf16[2,2,32,5120]{3,2,1,0:T(8,128)(2,1)}, bf16[2,2,32,5120]{3,2,1,0:T(8,128)(2,1)S(1)}, u32[]{:S(2)}, u32[]{:S(2)}) collective-permute-start(bf16[2,2,32,5120]{3,2,1,0:T(8,128)(2,1)} %shard_map.63), channel_id=1, source_target_pairs={{16,32},{48,64},{80,96},{112,128},{144,160},{176,192},{208,224},{3... | collective-permute-start | bytes 3932168 | tf_op jit(solution)/shard_map/ppermute | solution.py:309
  34.9 12.6 %collective-permute-start.4 = (f32[1,44,256]{2,1,0:T(8,128)S(1)}, f32[1,44,256]{2,1,0:T(8,128)S(1)}, u32[]{:S(2)}, u32[]{:S(2)}) collective-permute-start(f32[1,44,256]{2,1,0:T(8,128)S(1)} %pad_maximum_fusion.1), channel_id=1, source_target_pairs={{1,0},{2,1},{3,2},{4,3},{5,4},{6,5},{7,6},{8,7},{9,8},{10,9},{11,1... | collective-permute-start | bytes 135176 | tf_op jit(solution)/shard_map/ppermute | solution.py:304
  39.2 8.3 %collective-permute-start.3 = (f32[1,44,256]{2,1,0:T(8,128)S(1)}, f32[1,44,256]{2,1,0:T(8,128)S(1)}, u32[]{:S(2)}, u32[]{:S(2)}) collective-permute-start(f32[1,44,256]{2,1,0:T(8,128)S(1)} %pad_maximum_fusion), channel_id=1, source_target_pairs={{0,1},{1,2},{2,3},{3,4},{4,5},{5,6},{6,7},{7,8},{8,9},{9,10},{10,1... | collective-permute-start | bytes 135176 | tf_op jit(solution)/shard_map/ppermute | solution.py:304
  48.1 5.6 %collective-permute-start.5 = (s16[256,128]{1,0:T(8,128)(2,1)S(1)}, s16[256,128]{1,0:T(8,128)(2,1)S(1)}, u32[]{:S(2)}, u32[]{:S(2)}) collective-permute-start(s16[256,128]{1,0:T(8,128)(2,1)S(1)} %get-tuple-element.20), channel_id=1, source_target_pairs={{16,32},{48,64},{80,96},{112,128},{144,160},{176,192},{208,224},{3... | collective-permute-start | bytes 196616 | tf_op jit(solution)/shard_map/ppermute | solution.py:309
  51.6 2.1 %collective-permute-start.6 = (s16[256,128]{1,0:T(8,128)(2,1)S(1)}, s16[256,128]{1,0:T(8,128)(2,1)S(1)}, u32[]{:S(2)}, u32[]{:S(2)}) collective-permute-start(s16[256,128]{1,0:T(8,128)(2,1)S(1)} %get-tuple-element.21), channel_id=1, source_target_pairs={{0,16},{32,48},{64,80},{96,112},{128,144},{160,176},{192,208},{224... | collective-permute-start | bytes 196616 | tf_op jit(solution)/shard_map/ppermute | solution.py:314

commit v7 on v6

--- a/solution.py
+++ b/solution.py
@@ -12,6 +12,7 @@
 LANES = 128
 TILE = 16
 COLUMNS = 1280
+WIDTHS = (1280, 2560)
 FIXED = 32000.0
 EPS_POWER = 1e-06
 MIB = 2**20
@@ -30,11 +31,12 @@
 FORMED = len(INNER) + 2 * len(SIDE)
 
 
-def products_kernel(edges, powers, places, groups, *refs):
+def products_kernel(edges, powers, places, groups, width, *refs):
     flip = refs[0][0]
     out_ref, look_ref, acc_ref = refs[-3:]
     total = 2 * len(edges) + len(powers)
     tiles = acc_ref.shape[0] // (total * TILE)
+    steps = look_ref.shape[0] // width
     step = pl.program_id(0)
     used = sorted({k for e in edges for k in e} | set(powers))
 
@@ -64,14 +66,16 @@
             results.append(pixel[k][0] * pixel[k][0] + pixel[k][1] * pixel[k][1])
         return jnp.concatenate([r.astype(jnp.bfloat16) for r in results], axis=0)
 
-    look = look_ref[pl.ds(pl.multiple_of(step % 2 * COLUMNS, COLUMNS), COLUMNS), :]
+    look = look_ref[pl.ds(pl.multiple_of(step % steps * width, width), width), :]
     for tile in range(tiles):
-        formed = jnp.concatenate([planes(tile, s) for s in range(0, COLUMNS, LANES)], axis=1)
+        formed = jnp.concatenate([planes(tile, s) for s in range(0, width, LANES)], axis=1)
         part = jnp.dot(formed, look, preferred_element_type=jnp.float32)
         span = slice(tile * total * TILE, (tile + 1) * total * TILE)
-        acc_ref[span, :] = part + jnp.where(step % 2 == 1, acc_ref[span, :], 0.0)
-
-    @pl.when(step % 2 == 1)
+        if steps > 1:
+            part = part + jnp.where(step % steps > 0, acc_ref[span, :], 0.0)
+        acc_ref[span, :] = part
+
+    @pl.when(step % steps == steps - 1)
     def _():
         for m, (first, last) in enumerate(groups):
             for p in range(0, total, 8):
@@ -87,20 +91,21 @@
                 out_ref[m, p : p + size, :] = value
 
 
-def looked_products(flip, edges, powers, sources, places, groups, rows, columns):
+def looked_products(flip, edges, powers, sources, places, groups, rows, columns, width):
     total = 2 * len(edges) + len(powers)
+    steps = LANES * RLOOK // width
 
     def spec(block, index):
-        return pl.BlockSpec(block + (COLUMNS,), lambda i: index + (i,))
+        return pl.BlockSpec(block + (width,), lambda i: index + (i,))
 
     return pl.pallas_call(
-        functools.partial(products_kernel, edges, powers, places, groups),
+        functools.partial(products_kernel, edges, powers, places, groups, width),
         out_shape=jax.ShapeDtypeStruct((len(groups), total, columns // RLOOK), jnp.float32),
-        grid=(columns // COLUMNS,),
+        grid=(columns // width,),
         in_specs=[pl.BlockSpec(memory_space=pltpu.SMEM)] + [spec(*s[1:]) for s in sources],
-        out_specs=pl.BlockSpec((len(groups), total, LANES), lambda i: (0, 0, i // 2)),
+        out_specs=pl.BlockSpec((len(groups), total, LANES), lambda i: (0, 0, i // steps)),
         scratch_shapes=[
-            pltpu.VMEM((2 * COLUMNS, LANES), jnp.bfloat16),
+            pltpu.VMEM((LANES * RLOOK, LANES), jnp.bfloat16),
             pltpu.VMEM((total * rows, LANES), jnp.float32),
         ],
         compiler_params=pltpu.CompilerParams(vmem_limit_bytes=48 * MIB),
@@ -371,7 +376,7 @@
         2 + d: [(0, d, t * TILE) for t in range(tiles)] for d in range(local_dates)
     }
     inner = looked_products(
-        even, INNER, OWN_PLACES, [own_source], own_places, all_groups, rows, columns
+        even, INNER, OWN_PLACES, [own_source], own_places, all_groups, rows, columns, COLUMNS
     )
     later, inner = lax.optimization_barrier((images, inner))
     across.append(swapped_across(packed_rows(odd, later, runs[1], 40)))
@@ -388,6 +393,7 @@
         all_groups,
         rows,
         columns,
+        COLUMNS,
     )
     later, beside_looked = lax.optimization_barrier((images, beside_looked))
     layout = [[None, None] for _ in range(cells)]
@@ -402,7 +408,17 @@
         for g, m in enumerate(where):
             layout[m][n] = g
         across_looked.append(
-            looked_products(odd, SIDE, NEAR_PLACES, sources, places, groups, size * TILE, columns)
+            looked_products(
+                odd,
+                SIDE,
+                NEAR_PLACES,
+                sources,
+                places,
+                groups,
+                size * TILE,
+                columns,
+                WIDTHS[n],
+            )
         )
 
     def edge_cells(cut):

time: 80 us -> 79.5 us (level)
  Pallas kernels: 33.7 us -> 32.9 us
  transfers between devices with their start and end apart: 7 -> 7, of which waited for: 3 -> 3; matrix products, arithmetic and copies ran while one was open for 2% -> 2% of each run, Pallas kernels for 37% -> 36%
where the time goes in v7:
time: 79.5 us; the launch traced here: 78.7 us
  Pallas kernels  32.9 us (41%)
  blocking collectives  22.6 us (28%)
  starting transfers between devices  17 us (21%)
  waiting for transfers between devices  3.55 us (4%)
  other arithmetic  1.76 us (2%)
  between operations  0.89 us (1%)
    pallas_call x4, Pallas kernels, looked_products(): pl.pallas_call(functools.partial(products_kernel, edges, powers, places,...  25.7 us
    all_to_all x1, blocking collectives, on_device(): lax.all_to_all(outgoing, 'date', split_axis=0, concat_axis=0, tiled=True)  22.6 us
    ppermute x3, starting transfers between devices, swapped_across(): return lax.ppermute(value, 'date', pairs + [(b, a) for a, b in pairs])  9.95 us
    ppermute x2, starting transfers between devices, shifted(): lax.ppermute(value, axis, [(source, source + steps) for source in range(f...  6.19 us
    pallas_call x2, Pallas kernels, packed_rows(): pl.pallas_call(functools.partial(pack_kernel, runs), out_shape=jax.ShapeD...  3.98 us
    ppermute x3, waiting for transfers between devices, swapped_across(): return lax.ppermute(value, 'date', pairs + [(b, a) for a, b in pairs])  3.54 us
  transfers between devices with their start and end apart: 7, of which 3 were waited for; matrix products, arithmetic and copies ran while one was open for 2% of the time, Pallas kernels for 36%

profile of v7, /device:TPU:9, one launch (start us, length us, event | category | flops | bytes accessed | tf_op | source)
XLA Modules:
  0.0 78.7 jit_solution(16591363461996929714)
XLA Ops:
  0.6 1.5 %shard_map.60 = bf16[2,2,48,5120]{3,2,1,0:T(8,128)(2,1)S(1)} custom-call(s32[1]{0:T(128)} %bitcast.flip_ref.refs_0_, bf16[2,4,80,5120]{3,2,1,0:T(8,128)(2,1)} %refs_3_.1), custom_call_target="tpu_custom_call" | custom-call | tf_op jit(solution)/shard_map/pallas_call | solution.py:136
  2.2 0.8 collective-permute-start
  2.9 3.4 %collective-permute-start.1 = (bf16[2,2,48,5120]{3,2,1,0:T(8,128)(2,1)S(1)}, bf16[2,2,48,5120]{3,2,1,0:T(8,128)(2,1)}, u32[]{:S(2)}, u32[]{:S(2)}) collective-permute-start(bf16[2,2,48,5120]{3,2,1,0:T(8,128)(2,1)S(1)} %shard_map.60), channel_id=1, source_target_pairs={{16,32},{48,64},{80,96},{112,128},{144,160},{176,192},{208,224},{3... | collective-permute-start | bytes 5898248 | tf_op jit(solution)/shard_map/ppermute | solution.py:314
  6.4 7.5 %shard_map.59.refs_0_ = f32[16,16,256]{2,1,0:T(8,128)S(1)} custom-call(s32[1]{0:T(128)S(6)} %sub.56.refs_0_, bf16[2,4,80,5120]{3,2,1,0:T(8,128)(2,1)} %refs_3_.1), custom_call_target="tpu_custom_call" | custom-call | tf_op jit(solution)/shard_map/pallas_call | solution.py:101
  13.9 0.0 copy-start
  13.9 0.0 copy-start.1
  13.9 0.0 copy-start.2
  14.0 0.0 copy-start.3
  14.0 2.5 %shard_map.63 = bf16[2,2,32,5120]{3,2,1,0:T(8,128)(2,1)} custom-call(s32[1]{0:T(128)} %bitcast.flip_ref.refs_0_, bf16[2,4,80,5120]{3,2,1,0:T(8,128)(2,1)} %refs_3_.1), custom_call_target="tpu_custom_call" | custom-call | tf_op jit(solution)/shard_map/pallas_call | solution.py:136
  16.4 2.3 %collective-permute-start.2 = (bf16[2,2,32,5120]{3,2,1,0:T(8,128)(2,1)}, bf16[2,2,32,5120]{3,2,1,0:T(8,128)(2,1)S(1)}, u32[]{:S(2)}, u32[]{:S(2)}) collective-permute-start(bf16[2,2,32,5120]{3,2,1,0:T(8,128)(2,1)} %shard_map.63), channel_id=1, source_target_pairs={{16,32},{48,64},{80,96},{112,128},{144,160},{176,192},{208,224},{3... | collective-permute-start | bytes 3932168 | tf_op jit(solution)/shard_map/ppermute | solution.py:314
  18.7 0.7 and_select_fusion.1
  19.4 0.0 copy-done
  19.4 0.0 copy-done.1
  19.4 0.0 copy-done.2
  19.5 0.0 copy-done.3
  19.5 0.7 fusion.3
  20.1 0.2 select_reduce_fusion
  20.4 0.0 collective-permute-done.refs_2_
  20.4 8.5 %shard_map.61.refs_1_ = f32[16,14,256]{2,1,0:T(8,128)S(1)} custom-call(s32[1]{0:T(128)S(6)} %sub.56.refs_0_, bf16[2,4,80,5120]{3,2,1,0:T(8,128)(2,1)} %refs_3_.1, bf16[2,4,80,5120]{3,2,1,0:T(8,128)(2,1)} %collective-permute-done.refs_2_), custom_call_target="tpu_custom_call" | custom-call | tf_op jit(solution)/shard_map/pallas_call | solution.py:101
  28.9 0.1 collective-permute-done.1.refs_1_
  29.0 5.8 %shard_map.62.refs_2_ = f32[11,14,256]{2,1,0:T(8,128)S(1)} custom-call(s32[1]{0:T(128)} %bitcast.flip_ref.refs_0_, bf16[2,2,48,5120]{3,2,1,0:T(8,128)(2,1)} %collective-permute-done.1.refs_1_, bf16[2,4,80,5120]{3,2,1,0:T(8,128)(2,1)} %refs_3_.1, bf16[2,4,80,5120]{3,2,1,0:T(8,128)(2,1)} %refs_3_.1, bf16[2,4,80,5120]{3,2,1,0:T(8,128)(2,1)} %refs_3_.1), custom_call_target="tpu_custom_call" | custom-call | tf_op jit(solution)/shard_map/pallas_call | solution.py:101
  34.9 4.3 %collective-permute-start.4 = (f32[1,44,256]{2,1,0:T(8,128)S(1)}, f32[1,44,256]{2,1,0:T(8,128)S(1)}, u32[]{:S(2)}, u32[]{:S(2)}) collective-permute-start(f32[1,44,256]{2,1,0:T(8,128)S(1)} %pad_maximum_fusion.1), channel_id=1, source_target_pairs={{1,0},{2,1},{3,2},{4,3},{5,4},{6,5},{7,6},{8,7},{9,8},{10,9},{11,1... | collective-permute-start | bytes 135176 | tf_op jit(solution)/shard_map/ppermute | solution.py:309
  39.2 1.9 %collective-permute-start.3 = (f32[1,44,256]{2,1,0:T(8,128)S(1)}, f32[1,44,256]{2,1,0:T(8,128)S(1)}, u32[]{:S(2)}, u32[]{:S(2)}) collective-permute-start(f32[1,44,256]{2,1,0:T(8,128)S(1)} %pad_maximum_fusion), channel_id=1, source_target_pairs={{0,1},{1,2},{2,3},{3,4},{4,5},{5,6},{6,7},{7,8},{8,9},{9,10},{10,1... | collective-permute-start | bytes 135176 | tf_op jit(solution)/shard_map/ppermute | solution.py:309
  41.1 0.1 select_reduce_fusion.2
  41.2 1.7 %collective-permute-done.2.refs_1_ = bf16[2,2,32,5120]{3,2,1,0:T(8,128)(2,1)S(1)} collective-permute-done((bf16[2,2,32,5120]{3,2,1,0:T(8,128)(2,1)}, bf16[2,2,32,5120]{3,2,1,0:T(8,128)(2,1)S(1)}, u32[]{:S(2)}, u32[]{:S(2)}) %collective-permute-start.2) | collective-permute-done | bytes 1310752 | tf_op jit(solution)/shard_map/ppermute | solution.py:314
  42.9 3.8 %shard_map.64.refs_3_ = f32[7,14,256]{2,1,0:T(8,128)S(1)} custom-call(s32[1]{0:T(128)} %bitcast.flip_ref.refs_0_, bf16[2,2,32,5120]{3,2,1,0:T(8,128)(2,1)S(1)} %collective-permute-done.2.refs_1_, bf16[2,4,80,5120]{3,2,1,0:T(8,128)(2,1)} %refs_3_.1, bf16[2,4,80,5120]{3,2,1,0:T(8,128)(2,1)} %refs_3_.1), custom_call_target="tpu_custom_call" | custom-call | tf_op jit(solution)/shard_map/pallas_call | solution.py:101
  46.7 0.0 collective-permute-done.4.refs_5_
  46.7 0.0 collective-permute-done.3.refs_4_
  46.7 0.6 shard_map.65
  47.4 4.2 %collective-permute-start.5 = (s16[256,128]{1,0:T(8,128)(2,1)S(1)}, s16[256,128]{1,0:T(8,128)(2,1)S(1)}, u32[]{:S(2)}, u32[]{:S(2)}) collective-permute-start(s16[256,128]{1,0:T(8,128)(2,1)S(1)} %get-tuple-element.20), channel_id=1, source_target_pairs={{16,32},{48,64},{80,96},{112,128},{144,160},{176,192},{208,224},{3... | collective-permute-start | bytes 196616 | tf_op jit(solution)/shard_map/ppermute | solution.py:314
  51.6 0.1 collective-permute-start.6
  51.7 0.1 pad_add_fusion.scalar_ref
  51.8 1.8 %collective-permute-done.5.refs_1_ = s16[256,128]{1,0:T(8,128)(2,1)S(1)} collective-permute-done((s16[256,128]{1,0:T(8,128)(2,1)S(1)}, s16[256,128]{1,0:T(8,128)(2,1)S(1)}, u32[]{:S(2)}, u32[]{:S(2)}) %collective-permute-start.5) | collective-permute-done | bytes 65568 | tf_op jit(solution)/shard_map/ppermute | solution.py:314
  53.6 0.0 collective-permute-done.6.refs_2_
  53.6 1.5 %shard_map.66 = (s16[16,64,128]{2,1,0:T(8,128)(2,1)S(1)}, f32[2,4,4096]{2,1,0:T(4,128)}) custom-call(s32[59]{0:T(128)S(1)} %pad_add_fusion.scalar_ref, f32[1152,128]{1,0:T(8,128)S(1)} %get-tuple-element.19.refs_0_, s16[256,128]{1,0:T(8,128)(2,1)S(1)} %collective-permute-done.5.refs_1_, s16[256,128]{1,0:T(8,128)(2,1)S(1)} %collective-permute-done.6.refs_2_), custom_call_target="tpu_custom_call" | custom-call | tf_op jit(solution)/shard_map/pallas_call | solution.py:267
  55.0 22.6 %all_to_all.5.arrived_ref = s16[16,64,128]{2,1,0:T(8,128)(2,1)S(1)} all-to-all(s16[16,64,128]{2,1,0:T(8,128)(2,1)S(1)} %get-tuple-element.22), channel_id=1, replica_groups=mesh['date'=16,'strip'=16] {'date'}, dimensions={0} | all-to-all | bytes 524288 | tf_op jit(solution)/shard_map/all_to_all | solution.py:434
  77.6 1.1 %shard_map.67 = f32[2,16,4096]{2,1,0:T(8,128)} custom-call(s16[16,64,128]{2,1,0:T(8,128)(2,1)S(1)} %all_to_all.5.arrived_ref), custom_call_target="tpu_custom_call" | custom-call | tf_op jit(solution)/shard_map/pallas_call | solution.py:298
  (7 shorter events, 0.1 us)
Async XLA Ops:
  2.2 18.2 %collective-permute-start = (bf16[2,4,80,5120]{3,2,1,0:T(8,128)(2,1)}, bf16[2,4,80,5120]{3,2,1,0:T(8,128)(2,1)}, u32[]{:S(2)}, u32[]{:S(2)}) collective-permute-start(bf16[2,4,80,5120]{3,2,1,0:T(8,128)(2,1)} %refs_3_.1), channel_id=1, source_target_pairs={{0,16},{32,48},{64,80},{96,112},{128,144},{160,176},{192,208},{224... | collective-permute-start | bytes 19660808 | tf_op jit(solution)/shard_map/ppermute | solution.py:319
  2.9 26.0 %collective-permute-start.1 = (bf16[2,2,48,5120]{3,2,1,0:T(8,128)(2,1)S(1)}, bf16[2,2,48,5120]{3,2,1,0:T(8,128)(2,1)}, u32[]{:S(2)}, u32[]{:S(2)}) collective-permute-start(bf16[2,2,48,5120]{3,2,1,0:T(8,128)(2,1)S(1)} %shard_map.60), channel_id=1, source_target_pairs={{16,32},{48,64},{80,96},{112,128},{144,160},{176,192},{208,224},{3... | collective-permute-start | bytes 5898248 | tf_op jit(solution)/shard_map/ppermute | solution.py:314
  13.9 5.5 %copy-start = (s32[128,2]{0,1:T(2,128)S(1)}, s32[128,2]{0,1:T(2,128)}, u32[]{:S(2)}) copy-start(s32[128,2]{0,1:T(2,128)} %param.5) | copy-start | bytes 3076
  13.9 5.5 %copy-start.1 = (pred[26,1]{0,1:T(4,128)(4,1)S(1)}, pred[26,1]{0,1:T(4,128)(4,1)}, u32[]{:S(2)}) copy-start(pred[26,1]{0,1:T(4,128)(4,1)} %constant.62) | copy-start | bytes 82
  13.9 5.5 %copy-start.2 = (s32[26,1]{0,1:T(1,128)S(1)}, s32[26,1]{0,1:T(1,128)}, u32[]{:S(2)}) copy-start(s32[26,1]{0,1:T(1,128)} %constant.69) | copy-start | bytes 316
  14.0 5.5 %copy-start.3 = (s32[26,1]{0,1:T(1,128)S(1)}, s32[26,1]{0,1:T(1,128)}, u32[]{:S(2)}) copy-start(s32[26,1]{0,1:T(1,128)} %constant.70) | copy-start | bytes 316
  16.4 26.5 %collective-permute-start.2 = (bf16[2,2,32,5120]{3,2,1,0:T(8,128)(2,1)}, bf16[2,2,32,5120]{3,2,1,0:T(8,128)(2,1)S(1)}, u32[]{:S(2)}, u32[]{:S(2)}) collective-permute-start(bf16[2,2,32,5120]{3,2,1,0:T(8,128)(2,1)} %shard_map.63), channel_id=1, source_target_pairs={{16,32},{48,64},{80,96},{112,128},{144,160},{176,192},{208,224},{3... | collective-permute-start | bytes 3932168 | tf_op jit(solution)/shard_map/ppermute | solution.py:314
  34.9 11.8 %collective-permute-start.4 = (f32[1,44,256]{2,1,0:T(8,128)S(1)}, f32[1,44,256]{2,1,0:T(8,128)S(1)}, u32[]{:S(2)}, u32[]{:S(2)}) collective-permute-start(f32[1,44,256]{2,1,0:T(8,128)S(1)} %pad_maximum_fusion.1), channel_id=1, source_target_pairs={{1,0},{2,1},{3,2},{4,3},{5,4},{6,5},{7,6},{8,7},{9,8},{10,9},{11,1... | collective-permute-start | bytes 135176 | tf_op jit(solution)/shard_map/ppermute | solution.py:309
  39.2 7.6 %collective-permute-start.3 = (f32[1,44,256]{2,1,0:T(8,128)S(1)}, f32[1,44,256]{2,1,0:T(8,128)S(1)}, u32[]{:S(2)}, u32[]{:S(2)}) collective-permute-start(f32[1,44,256]{2,1,0:T(8,128)S(1)} %pad_maximum_fusion), channel_id=1, source_target_pairs={{0,1},{1,2},{2,3},{3,4},{4,5},{5,6},{6,7},{7,8},{8,9},{9,10},{10,1... | collective-permute-start | bytes 135176 | tf_op jit(solution)/shard_map/ppermute | solution.py:309
  47.4 6.2 %collective-permute-start.5 = (s16[256,128]{1,0:T(8,128)(2,1)S(1)}, s16[256,128]{1,0:T(8,128)(2,1)S(1)}, u32[]{:S(2)}, u32[]{:S(2)}) collective-permute-start(s16[256,128]{1,0:T(8,128)(2,1)S(1)} %get-tuple-element.20), channel_id=1, source_target_pairs={{16,32},{48,64},{80,96},{112,128},{144,160},{176,192},{208,224},{3... | collective-permute-start | bytes 196616 | tf_op jit(solution)/shard_map/ppermute | solution.py:314
  51.6 1.9 %collective-permute-start.6 = (s16[256,128]{1,0:T(8,128)(2,1)S(1)}, s16[256,128]{1,0:T(8,128)(2,1)S(1)}, u32[]{:S(2)}, u32[]{:S(2)}) collective-permute-start(s16[256,128]{1,0:T(8,128)(2,1)S(1)} %get-tuple-element.21), channel_id=1, source_target_pairs={{0,16},{32,48},{64,80},{96,112},{128,144},{160,176},{192,208},{224... | collective-permute-start | bytes 196616 | tf_op jit(solution)/shard_map/ppermute | solution.py:319

commit v8 on v7

--- a/solution.py
+++ b/solution.py
@@ -11,8 +11,8 @@
 RLOOK = 20
 LANES = 128
 TILE = 16
-COLUMNS = 1280
-WIDTHS = (1280, 2560)
+COLUMNS = 2560
+WIDTHS = (2560, 2560)
 FIXED = 32000.0
 EPS_POWER = 1e-06
 MIB = 2**20

time: 79.5 us -> 79.2 us (level)
  waiting for transfers between devices: 3.55 us -> 4.87 us
  starting transfers between devices: 17 us -> 16 us
    ppermute x3, waiting for transfers between devices: 3.54 us -> 4.86 us  [swapped_across(): return lax.ppermute(value, 'date', pairs + [(b, a) for a, b in pairs])]
    ppermute x3, starting transfers between devices: 9.95 us -> 8.95 us  [swapped_across(): return lax.ppermute(value, 'date', pairs + [(b, a) for a, b in pairs])]
  transfers between devices with their start and end apart: 7 -> 7, of which waited for: 3 -> 3; matrix products, arithmetic and copies ran while one was open for 2% -> 2% of each run, Pallas kernels for 36% -> 35%
where the time goes in v8:
time: 79.2 us; the launch traced here: 78.2 us
  Pallas kernels  32.3 us (41%)
  blocking collectives  22.3 us (28%)
  starting transfers between devices  16 us (20%)
  waiting for transfers between devices  4.87 us (6%)
  other arithmetic  1.76 us (2%)
  between operations  0.89 us (1%)
    pallas_call x4, Pallas kernels, looked_products(): pl.pallas_call(functools.partial(products_kernel, edges, powers, places,...  25.1 us
    all_to_all x1, blocking collectives, on_device(): lax.all_to_all(outgoing, 'date', split_axis=0, concat_axis=0, tiled=True)  22.3 us
    ppermute x3, starting transfers between devices, swapped_across(): return lax.ppermute(value, 'date', pairs + [(b, a) for a, b in pairs])  8.95 us
    ppermute x2, starting transfers between devices, shifted(): lax.ppermute(value, axis, [(source, source + steps) for source in range(f...  6.19 us
    ppermute x3, waiting for transfers between devices, swapped_across(): return lax.ppermute(value, 'date', pairs + [(b, a) for a, b in pairs])  4.86 us
    pallas_call x2, Pallas kernels, packed_rows(): pl.pallas_call(functools.partial(pack_kernel, runs), out_shape=jax.ShapeD...  3.98 us
  transfers between devices with their start and end apart: 7, of which 3 were waited for; matrix products, arithmetic and copies ran while one was open for 2% of the time, Pallas kernels for 35%

profile of v8, /device:TPU:9, one launch (start us, length us, event | category | flops | bytes accessed | tf_op | source)
XLA Modules:
  0.0 78.2 jit_solution(3239439310066697317)
XLA Ops:
  0.6 1.5 %shard_map.60 = bf16[2,2,48,5120]{3,2,1,0:T(8,128)(2,1)S(1)} custom-call(s32[1]{0:T(128)} %bitcast.flip_ref.refs_0_, bf16[2,4,80,5120]{3,2,1,0:T(8,128)(2,1)} %refs_3_.1), custom_call_target="tpu_custom_call" | custom-call | tf_op jit(solution)/shard_map/pallas_call | solution.py:136
  2.2 0.8 collective-permute-start
  2.9 3.4 %collective-permute-start.1 = (bf16[2,2,48,5120]{3,2,1,0:T(8,128)(2,1)S(1)}, bf16[2,2,48,5120]{3,2,1,0:T(8,128)(2,1)}, u32[]{:S(2)}, u32[]{:S(2)}) collective-permute-start(bf16[2,2,48,5120]{3,2,1,0:T(8,128)(2,1)S(1)} %shard_map.60), channel_id=1, source_target_pairs={{16,32},{48,64},{80,96},{112,128},{144,160},{176,192},{208,224},{3... | collective-permute-start | bytes 5898248 | tf_op jit(solution)/shard_map/ppermute | solution.py:314
  6.4 7.6 %shard_map.59.refs_0_ = f32[16,16,256]{2,1,0:T(8,128)S(1)} custom-call(s32[1]{0:T(128)S(6)} %sub.56.refs_0_, bf16[2,4,80,5120]{3,2,1,0:T(8,128)(2,1)} %refs_3_.1), custom_call_target="tpu_custom_call" | custom-call | tf_op jit(solution)/shard_map/pallas_call | solution.py:101
  14.0 0.0 copy-start
  14.0 0.0 copy-start.1
  14.0 0.0 copy-start.2
  14.1 0.0 copy-start.3
  14.1 2.5 %shard_map.63 = bf16[2,2,32,5120]{3,2,1,0:T(8,128)(2,1)} custom-call(s32[1]{0:T(128)} %bitcast.flip_ref.refs_0_, bf16[2,4,80,5120]{3,2,1,0:T(8,128)(2,1)} %refs_3_.1), custom_call_target="tpu_custom_call" | custom-call | tf_op jit(solution)/shard_map/pallas_call | solution.py:136
  16.5 2.1 %collective-permute-start.2 = (bf16[2,2,32,5120]{3,2,1,0:T(8,128)(2,1)}, bf16[2,2,32,5120]{3,2,1,0:T(8,128)(2,1)S(1)}, u32[]{:S(2)}, u32[]{:S(2)}) collective-permute-start(bf16[2,2,32,5120]{3,2,1,0:T(8,128)(2,1)} %shard_map.63), channel_id=1, source_target_pairs={{16,32},{48,64},{80,96},{112,128},{144,160},{176,192},{208,224},{3... | collective-permute-start | bytes 3932168 | tf_op jit(solution)/shard_map/ppermute | solution.py:314
  18.7 0.7 and_select_fusion.1
  19.3 0.0 copy-done
  19.3 0.0 copy-done.1
  19.3 0.0 copy-done.2
  19.4 0.0 copy-done.3
  19.4 0.7 fusion.3
  20.0 0.2 select_reduce_fusion
  20.3 0.0 collective-permute-done.refs_2_
  20.3 8.4 %shard_map.61.refs_1_ = f32[16,14,256]{2,1,0:T(8,128)S(1)} custom-call(s32[1]{0:T(128)S(6)} %sub.56.refs_0_, bf16[2,4,80,5120]{3,2,1,0:T(8,128)(2,1)} %refs_3_.1, bf16[2,4,80,5120]{3,2,1,0:T(8,128)(2,1)} %collective-permute-done.refs_2_), custom_call_target="tpu_custom_call" | custom-call | tf_op jit(solution)/shard_map/pallas_call | solution.py:101
  28.7 0.3 collective-permute-done.1.refs_1_
  29.0 5.2 %shard_map.62.refs_2_ = f32[11,14,256]{2,1,0:T(8,128)S(1)} custom-call(s32[1]{0:T(128)} %bitcast.flip_ref.refs_0_, bf16[2,2,48,5120]{3,2,1,0:T(8,128)(2,1)} %collective-permute-done.1.refs_1_, bf16[2,4,80,5120]{3,2,1,0:T(8,128)(2,1)} %refs_3_.1, bf16[2,4,80,5120]{3,2,1,0:T(8,128)(2,1)} %refs_3_.1, bf16[2,4,80,5120]{3,2,1,0:T(8,128)(2,1)} %refs_3_.1), custom_call_target="tpu_custom_call" | custom-call | tf_op jit(solution)/shard_map/pallas_call | solution.py:101
  34.3 4.3 %collective-permute-start.4 = (f32[1,44,256]{2,1,0:T(8,128)S(1)}, f32[1,44,256]{2,1,0:T(8,128)S(1)}, u32[]{:S(2)}, u32[]{:S(2)}) collective-permute-start(f32[1,44,256]{2,1,0:T(8,128)S(1)} %pad_maximum_fusion.1), channel_id=1, source_target_pairs={{1,0},{2,1},{3,2},{4,3},{5,4},{6,5},{7,6},{8,7},{9,8},{10,9},{11,1... | collective-permute-start | bytes 135176 | tf_op jit(solution)/shard_map/ppermute | solution.py:309
  38.6 1.9 %collective-permute-start.3 = (f32[1,44,256]{2,1,0:T(8,128)S(1)}, f32[1,44,256]{2,1,0:T(8,128)S(1)}, u32[]{:S(2)}, u32[]{:S(2)}) collective-permute-start(f32[1,44,256]{2,1,0:T(8,128)S(1)} %pad_maximum_fusion), channel_id=1, source_target_pairs={{0,1},{1,2},{2,3},{3,4},{4,5},{5,6},{6,7},{7,8},{8,9},{9,10},{10,1... | collective-permute-start | bytes 135176 | tf_op jit(solution)/shard_map/ppermute | solution.py:309
  40.5 0.1 select_reduce_fusion.2
  40.6 2.6 %collective-permute-done.2.refs_1_ = bf16[2,2,32,5120]{3,2,1,0:T(8,128)(2,1)S(1)} collective-permute-done((bf16[2,2,32,5120]{3,2,1,0:T(8,128)(2,1)}, bf16[2,2,32,5120]{3,2,1,0:T(8,128)(2,1)S(1)}, u32[]{:S(2)}, u32[]{:S(2)}) %collective-permute-start.2) | collective-permute-done | bytes 1310752 | tf_op jit(solution)/shard_map/ppermute | solution.py:314
  43.2 3.8 %shard_map.64.refs_3_ = f32[7,14,256]{2,1,0:T(8,128)S(1)} custom-call(s32[1]{0:T(128)} %bitcast.flip_ref.refs_0_, bf16[2,2,32,5120]{3,2,1,0:T(8,128)(2,1)S(1)} %collective-permute-done.2.refs_1_, bf16[2,4,80,5120]{3,2,1,0:T(8,128)(2,1)} %refs_3_.1, bf16[2,4,80,5120]{3,2,1,0:T(8,128)(2,1)} %refs_3_.1), custom_call_target="tpu_custom_call" | custom-call | tf_op jit(solution)/shard_map/pallas_call | solution.py:101
  47.0 0.0 collective-permute-done.4.refs_5_
  47.0 0.0 collective-permute-done.3.refs_4_
  47.0 0.6 shard_map.65
  47.7 3.4 %collective-permute-start.5 = (s16[256,128]{1,0:T(8,128)(2,1)S(1)}, s16[256,128]{1,0:T(8,128)(2,1)S(1)}, u32[]{:S(2)}, u32[]{:S(2)}) collective-permute-start(s16[256,128]{1,0:T(8,128)(2,1)S(1)} %get-tuple-element.20), channel_id=1, source_target_pairs={{16,32},{48,64},{80,96},{112,128},{144,160},{176,192},{208,224},{3... | collective-permute-start | bytes 196616 | tf_op jit(solution)/shard_map/ppermute | solution.py:314
  51.1 0.1 collective-permute-start.6
  51.2 0.1 pad_add_fusion.scalar_ref
  51.3 2.0 %collective-permute-done.5.refs_1_ = s16[256,128]{1,0:T(8,128)(2,1)S(1)} collective-permute-done((s16[256,128]{1,0:T(8,128)(2,1)S(1)}, s16[256,128]{1,0:T(8,128)(2,1)S(1)}, u32[]{:S(2)}, u32[]{:S(2)}) %collective-permute-start.5) | collective-permute-done | bytes 65568 | tf_op jit(solution)/shard_map/ppermute | solution.py:314
  53.3 0.0 collective-permute-done.6.refs_2_
  53.3 1.5 %shard_map.66 = (s16[16,64,128]{2,1,0:T(8,128)(2,1)S(1)}, f32[2,4,4096]{2,1,0:T(4,128)}) custom-call(s32[59]{0:T(128)S(1)} %pad_add_fusion.scalar_ref, f32[1152,128]{1,0:T(8,128)S(1)} %get-tuple-element.19.refs_0_, s16[256,128]{1,0:T(8,128)(2,1)S(1)} %collective-permute-done.5.refs_1_, s16[256,128]{1,0:T(8,128)(2,1)S(1)} %collective-permute-done.6.refs_2_), custom_call_target="tpu_custom_call" | custom-call | tf_op jit(solution)/shard_map/pallas_call | solution.py:267
  54.8 22.3 %all_to_all.5.arrived_ref = s16[16,64,128]{2,1,0:T(8,128)(2,1)S(1)} all-to-all(s16[16,64,128]{2,1,0:T(8,128)(2,1)S(1)} %get-tuple-element.22), channel_id=1, replica_groups=mesh['date'=16,'strip'=16] {'date'}, dimensions={0} | all-to-all | bytes 524288 | tf_op jit(solution)/shard_map/all_to_all | solution.py:434
  77.1 1.1 %shard_map.67 = f32[2,16,4096]{2,1,0:T(8,128)} custom-call(s16[16,64,128]{2,1,0:T(8,128)(2,1)S(1)} %all_to_all.5.arrived_ref), custom_call_target="tpu_custom_call" | custom-call | tf_op jit(solution)/shard_map/pallas_call | solution.py:298
  (7 shorter events, 0.1 us)
Async XLA Ops:
  2.2 18.1 %collective-permute-start = (bf16[2,4,80,5120]{3,2,1,0:T(8,128)(2,1)}, bf16[2,4,80,5120]{3,2,1,0:T(8,128)(2,1)}, u32[]{:S(2)}, u32[]{:S(2)}) collective-permute-start(bf16[2,4,80,5120]{3,2,1,0:T(8,128)(2,1)} %refs_3_.1), channel_id=1, source_target_pairs={{0,16},{32,48},{64,80},{96,112},{128,144},{160,176},{192,208},{224... | collective-permute-start | bytes 19660808 | tf_op jit(solution)/shard_map/ppermute | solution.py:319
  2.9 26.0 %collective-permute-start.1 = (bf16[2,2,48,5120]{3,2,1,0:T(8,128)(2,1)S(1)}, bf16[2,2,48,5120]{3,2,1,0:T(8,128)(2,1)}, u32[]{:S(2)}, u32[]{:S(2)}) collective-permute-start(bf16[2,2,48,5120]{3,2,1,0:T(8,128)(2,1)S(1)} %shard_map.60), channel_id=1, source_target_pairs={{16,32},{48,64},{80,96},{112,128},{144,160},{176,192},{208,224},{3... | collective-permute-start | bytes 5898248 | tf_op jit(solution)/shard_map/ppermute | solution.py:314
  14.0 5.3 %copy-start = (s32[128,2]{0,1:T(2,128)S(1)}, s32[128,2]{0,1:T(2,128)}, u32[]{:S(2)}) copy-start(s32[128,2]{0,1:T(2,128)} %param.5) | copy-start | bytes 3076
  14.0 5.3 %copy-start.1 = (pred[26,1]{0,1:T(4,128)(4,1)S(1)}, pred[26,1]{0,1:T(4,128)(4,1)}, u32[]{:S(2)}) copy-start(pred[26,1]{0,1:T(4,128)(4,1)} %constant.62) | copy-start | bytes 82
  14.0 5.3 %copy-start.2 = (s32[26,1]{0,1:T(1,128)S(1)}, s32[26,1]{0,1:T(1,128)}, u32[]{:S(2)}) copy-start(s32[26,1]{0,1:T(1,128)} %constant.69) | copy-start | bytes 316
  14.1 5.3 %copy-start.3 = (s32[26,1]{0,1:T(1,128)S(1)}, s32[26,1]{0,1:T(1,128)}, u32[]{:S(2)}) copy-start(s32[26,1]{0,1:T(1,128)} %constant.70) | copy-start | bytes 316
  16.5 26.7 %collective-permute-start.2 = (bf16[2,2,32,5120]{3,2,1,0:T(8,128)(2,1)}, bf16[2,2,32,5120]{3,2,1,0:T(8,128)(2,1)S(1)}, u32[]{:S(2)}, u32[]{:S(2)}) collective-permute-start(bf16[2,2,32,5120]{3,2,1,0:T(8,128)(2,1)} %shard_map.63), channel_id=1, source_target_pairs={{16,32},{48,64},{80,96},{112,128},{144,160},{176,192},{208,224},{3... | collective-permute-start | bytes 3932168 | tf_op jit(solution)/shard_map/ppermute | solution.py:314
  34.3 12.7 %collective-permute-start.4 = (f32[1,44,256]{2,1,0:T(8,128)S(1)}, f32[1,44,256]{2,1,0:T(8,128)S(1)}, u32[]{:S(2)}, u32[]{:S(2)}) collective-permute-start(f32[1,44,256]{2,1,0:T(8,128)S(1)} %pad_maximum_fusion.1), channel_id=1, source_target_pairs={{1,0},{2,1},{3,2},{4,3},{5,4},{6,5},{7,6},{8,7},{9,8},{10,9},{11,1... | collective-permute-start | bytes 135176 | tf_op jit(solution)/shard_map/ppermute | solution.py:309
  38.6 8.5 %collective-permute-start.3 = (f32[1,44,256]{2,1,0:T(8,128)S(1)}, f32[1,44,256]{2,1,0:T(8,128)S(1)}, u32[]{:S(2)}, u32[]{:S(2)}) collective-permute-start(f32[1,44,256]{2,1,0:T(8,128)S(1)} %pad_maximum_fusion), channel_id=1, source_target_pairs={{0,1},{1,2},{2,3},{3,4},{4,5},{5,6},{6,7},{7,8},{8,9},{9,10},{10,1... | collective-permute-start | bytes 135176 | tf_op jit(solution)/shard_map/ppermute | solution.py:309
  47.7 5.6 %collective-permute-start.5 = (s16[256,128]{1,0:T(8,128)(2,1)S(1)}, s16[256,128]{1,0:T(8,128)(2,1)S(1)}, u32[]{:S(2)}, u32[]{:S(2)}) collective-permute-start(s16[256,128]{1,0:T(8,128)(2,1)S(1)} %get-tuple-element.20), channel_id=1, source_target_pairs={{16,32},{48,64},{80,96},{112,128},{144,160},{176,192},{208,224},{3... | collective-permute-start | bytes 196616 | tf_op jit(solution)/shard_map/ppermute | solution.py:314
  51.1 2.2 %collective-permute-start.6 = (s16[256,128]{1,0:T(8,128)(2,1)S(1)}, s16[256,128]{1,0:T(8,128)(2,1)S(1)}, u32[]{:S(2)}, u32[]{:S(2)}) collective-permute-start(s16[256,128]{1,0:T(8,128)(2,1)S(1)} %get-tuple-element.21), channel_id=1, source_target_pairs={{0,16},{32,48},{64,80},{96,112},{128,144},{160,176},{192,208},{224... | collective-permute-start | bytes 196616 | tf_op jit(solution)/shard_map/ppermute | solution.py:319

commit v9 on v8

--- a/solution.py
+++ b/solution.py
@@ -11,7 +11,7 @@
 RLOOK = 20
 LANES = 128
 TILE = 16
-COLUMNS = 2560
+COLUMNS = 1280
 WIDTHS = (2560, 2560)
 FIXED = 32000.0
 EPS_POWER = 1e-06

time: 79.2 us -> 79.2 us (level)
  no operation moved by 1% of the time
where the time goes in v9:
time: 79.2 us; the launch traced here: 78.3 us
  Pallas kernels  32.3 us (41%)
  blocking collectives  22.4 us (28%)
  starting transfers between devices  16.2 us (20%)
  waiting for transfers between devices  4.68 us (6%)
  other arithmetic  1.76 us (2%)
  between operations  0.89 us (1%)
    pallas_call x4, Pallas kernels, looked_products(): pl.pallas_call(functools.partial(products_kernel, edges, powers, places,...  25.1 us
    all_to_all x1, blocking collectives, on_device(): lax.all_to_all(outgoing, 'date', split_axis=0, concat_axis=0, tiled=True)  22.4 us
    ppermute x3, starting transfers between devices, swapped_across(): return lax.ppermute(value, 'date', pairs + [(b, a) for a, b in pairs])  9.14 us
    ppermute x2, starting transfers between devices, shifted(): lax.ppermute(value, axis, [(source, source + steps) for source in range(f...  6.19 us
    ppermute x3, waiting for transfers between devices, swapped_across(): return lax.ppermute(value, 'date', pairs + [(b, a) for a, b in pairs])  4.67 us
    pallas_call x2, Pallas kernels, packed_rows(): pl.pallas_call(functools.partial(pack_kernel, runs), out_shape=jax.ShapeD...  3.98 us
  transfers between devices with their start and end apart: 7, of which 3 were waited for; matrix products, arithmetic and copies ran while one was open for 2% of the time, Pallas kernels for 35%

profile of v9, /device:TPU:9, one launch (start us, length us, event | category | flops | bytes accessed | tf_op | source)
XLA Modules:
  0.0 78.3 jit_solution(12710261446480686522)
XLA Ops:
  0.6 1.5 %shard_map.60 = bf16[2,2,48,5120]{3,2,1,0:T(8,128)(2,1)S(1)} custom-call(s32[1]{0:T(128)} %bitcast.flip_ref.refs_0_, bf16[2,4,80,5120]{3,2,1,0:T(8,128)(2,1)} %refs_3_.1), custom_call_target="tpu_custom_call" | custom-call | tf_op jit(solution)/shard_map/pallas_call | solution.py:136
  2.2 0.8 collective-permute-start
  2.9 3.4 %collective-permute-start.1 = (bf16[2,2,48,5120]{3,2,1,0:T(8,128)(2,1)S(1)}, bf16[2,2,48,5120]{3,2,1,0:T(8,128)(2,1)}, u32[]{:S(2)}, u32[]{:S(2)}) collective-permute-start(bf16[2,2,48,5120]{3,2,1,0:T(8,128)(2,1)S(1)} %shard_map.60), channel_id=1, source_target_pairs={{16,32},{48,64},{80,96},{112,128},{144,160},{176,192},{208,224},{3... | collective-permute-start | bytes 5898248 | tf_op jit(solution)/shard_map/ppermute | solution.py:314
  6.4 7.5 %shard_map.59.refs_0_ = f32[16,16,256]{2,1,0:T(8,128)S(1)} custom-call(s32[1]{0:T(128)S(6)} %sub.56.refs_0_, bf16[2,4,80,5120]{3,2,1,0:T(8,128)(2,1)} %refs_3_.1), custom_call_target="tpu_custom_call" | custom-call | tf_op jit(solution)/shard_map/pallas_call | solution.py:101
  13.9 0.0 copy-start
  13.9 0.0 copy-start.1
  13.9 0.0 copy-start.2
  14.0 0.0 copy-start.3
  14.0 2.5 %shard_map.63 = bf16[2,2,32,5120]{3,2,1,0:T(8,128)(2,1)} custom-call(s32[1]{0:T(128)} %bitcast.flip_ref.refs_0_, bf16[2,4,80,5120]{3,2,1,0:T(8,128)(2,1)} %refs_3_.1), custom_call_target="tpu_custom_call" | custom-call | tf_op jit(solution)/shard_map/pallas_call | solution.py:136
  16.4 2.3 %collective-permute-start.2 = (bf16[2,2,32,5120]{3,2,1,0:T(8,128)(2,1)}, bf16[2,2,32,5120]{3,2,1,0:T(8,128)(2,1)S(1)}, u32[]{:S(2)}, u32[]{:S(2)}) collective-permute-start(bf16[2,2,32,5120]{3,2,1,0:T(8,128)(2,1)} %shard_map.63), channel_id=1, source_target_pairs={{16,32},{48,64},{80,96},{112,128},{144,160},{176,192},{208,224},{3... | collective-permute-start | bytes 3932168 | tf_op jit(solution)/shard_map/ppermute | solution.py:314
  18.7 0.7 and_select_fusion.1
  19.4 0.0 copy-done
  19.4 0.0 copy-done.1
  19.4 0.0 copy-done.2
  19.5 0.0 copy-done.3
  19.5 0.7 fusion.3
  20.1 0.2 select_reduce_fusion
  20.4 0.0 collective-permute-done.refs_2_
  20.4 8.5 %shard_map.61.refs_1_ = f32[16,14,256]{2,1,0:T(8,128)S(1)} custom-call(s32[1]{0:T(128)S(6)} %sub.56.refs_0_, bf16[2,4,80,5120]{3,2,1,0:T(8,128)(2,1)} %refs_3_.1, bf16[2,4,80,5120]{3,2,1,0:T(8,128)(2,1)} %collective-permute-done.refs_2_), custom_call_target="tpu_custom_call" | custom-call | tf_op jit(solution)/shard_map/pallas_call | solution.py:101
  28.9 0.1 collective-permute-done.1.refs_1_
  29.0 5.2 %shard_map.62.refs_2_ = f32[11,14,256]{2,1,0:T(8,128)S(1)} custom-call(s32[1]{0:T(128)} %bitcast.flip_ref.refs_0_, bf16[2,2,48,5120]{3,2,1,0:T(8,128)(2,1)} %collective-permute-done.1.refs_1_, bf16[2,4,80,5120]{3,2,1,0:T(8,128)(2,1)} %refs_3_.1, bf16[2,4,80,5120]{3,2,1,0:T(8,128)(2,1)} %refs_3_.1, bf16[2,4,80,5120]{3,2,1,0:T(8,128)(2,1)} %refs_3_.1), custom_call_target="tpu_custom_call" | custom-call | tf_op jit(solution)/shard_map/pallas_call | solution.py:101
  34.3 4.3 %collective-permute-start.4 = (f32[1,44,256]{2,1,0:T(8,128)S(1)}, f32[1,44,256]{2,1,0:T(8,128)S(1)}, u32[]{:S(2)}, u32[]{:S(2)}) collective-permute-start(f32[1,44,256]{2,1,0:T(8,128)S(1)} %pad_maximum_fusion.1), channel_id=1, source_target_pairs={{1,0},{2,1},{3,2},{4,3},{5,4},{6,5},{7,6},{8,7},{9,8},{10,9},{11,1... | collective-permute-start | bytes 135176 | tf_op jit(solution)/shard_map/ppermute | solution.py:309
  38.6 1.9 %collective-permute-start.3 = (f32[1,44,256]{2,1,0:T(8,128)S(1)}, f32[1,44,256]{2,1,0:T(8,128)S(1)}, u32[]{:S(2)}, u32[]{:S(2)}) collective-permute-start(f32[1,44,256]{2,1,0:T(8,128)S(1)} %pad_maximum_fusion), channel_id=1, source_target_pairs={{0,1},{1,2},{2,3},{3,4},{4,5},{5,6},{6,7},{7,8},{8,9},{9,10},{10,1... | collective-permute-start | bytes 135176 | tf_op jit(solution)/shard_map/ppermute | solution.py:309
  40.5 0.1 select_reduce_fusion.2
  40.6 2.6 %collective-permute-done.2.refs_1_ = bf16[2,2,32,5120]{3,2,1,0:T(8,128)(2,1)S(1)} collective-permute-done((bf16[2,2,32,5120]{3,2,1,0:T(8,128)(2,1)}, bf16[2,2,32,5120]{3,2,1,0:T(8,128)(2,1)S(1)}, u32[]{:S(2)}, u32[]{:S(2)}) %collective-permute-start.2) | collective-permute-done | bytes 1310752 | tf_op jit(solution)/shard_map/ppermute | solution.py:314
  43.2 3.8 %shard_map.64.refs_3_ = f32[7,14,256]{2,1,0:T(8,128)S(1)} custom-call(s32[1]{0:T(128)} %bitcast.flip_ref.refs_0_, bf16[2,2,32,5120]{3,2,1,0:T(8,128)(2,1)S(1)} %collective-permute-done.2.refs_1_, bf16[2,4,80,5120]{3,2,1,0:T(8,128)(2,1)} %refs_3_.1, bf16[2,4,80,5120]{3,2,1,0:T(8,128)(2,1)} %refs_3_.1), custom_call_target="tpu_custom_call" | custom-call | tf_op jit(solution)/shard_map/pallas_call | solution.py:101
  47.0 0.0 collective-permute-done.4.refs_5_
  47.0 0.0 collective-permute-done.3.refs_4_
  47.0 0.6 shard_map.65
  47.7 3.4 %collective-permute-start.5 = (s16[256,128]{1,0:T(8,128)(2,1)S(1)}, s16[256,128]{1,0:T(8,128)(2,1)S(1)}, u32[]{:S(2)}, u32[]{:S(2)}) collective-permute-start(s16[256,128]{1,0:T(8,128)(2,1)S(1)} %get-tuple-element.20), channel_id=1, source_target_pairs={{16,32},{48,64},{80,96},{112,128},{144,160},{176,192},{208,224},{3... | collective-permute-start | bytes 196616 | tf_op jit(solution)/shard_map/ppermute | solution.py:314
  51.1 0.1 collective-permute-start.6
  51.2 0.1 pad_add_fusion.scalar_ref
  51.3 2.0 %collective-permute-done.5.refs_1_ = s16[256,128]{1,0:T(8,128)(2,1)S(1)} collective-permute-done((s16[256,128]{1,0:T(8,128)(2,1)S(1)}, s16[256,128]{1,0:T(8,128)(2,1)S(1)}, u32[]{:S(2)}, u32[]{:S(2)}) %collective-permute-start.5) | collective-permute-done | bytes 65568 | tf_op jit(solution)/shard_map/ppermute | solution.py:314
  53.3 0.0 collective-permute-done.6.refs_2_
  53.3 1.5 %shard_map.66 = (s16[16,64,128]{2,1,0:T(8,128)(2,1)S(1)}, f32[2,4,4096]{2,1,0:T(4,128)}) custom-call(s32[59]{0:T(128)S(1)} %pad_add_fusion.scalar_ref, f32[1152,128]{1,0:T(8,128)S(1)} %get-tuple-element.19.refs_0_, s16[256,128]{1,0:T(8,128)(2,1)S(1)} %collective-permute-done.5.refs_1_, s16[256,128]{1,0:T(8,128)(2,1)S(1)} %collective-permute-done.6.refs_2_), custom_call_target="tpu_custom_call" | custom-call | tf_op jit(solution)/shard_map/pallas_call | solution.py:267
  54.8 22.4 %all_to_all.5.arrived_ref = s16[16,64,128]{2,1,0:T(8,128)(2,1)S(1)} all-to-all(s16[16,64,128]{2,1,0:T(8,128)(2,1)S(1)} %get-tuple-element.22), channel_id=1, replica_groups=mesh['date'=16,'strip'=16] {'date'}, dimensions={0} | all-to-all | bytes 524288 | tf_op jit(solution)/shard_map/all_to_all | solution.py:434
  77.1 1.1 %shard_map.67 = f32[2,16,4096]{2,1,0:T(8,128)} custom-call(s16[16,64,128]{2,1,0:T(8,128)(2,1)S(1)} %all_to_all.5.arrived_ref), custom_call_target="tpu_custom_call" | custom-call | tf_op jit(solution)/shard_map/pallas_call | solution.py:298
  (7 shorter events, 0.0 us)
Async XLA Ops:
  2.2 18.2 %collective-permute-start = (bf16[2,4,80,5120]{3,2,1,0:T(8,128)(2,1)}, bf16[2,4,80,5120]{3,2,1,0:T(8,128)(2,1)}, u32[]{:S(2)}, u32[]{:S(2)}) collective-permute-start(bf16[2,4,80,5120]{3,2,1,0:T(8,128)(2,1)} %refs_3_.1), channel_id=1, source_target_pairs={{0,16},{32,48},{64,80},{96,112},{128,144},{160,176},{192,208},{224... | collective-permute-start | bytes 19660808 | tf_op jit(solution)/shard_map/ppermute | solution.py:319
  2.9 26.0 %collective-permute-start.1 = (bf16[2,2,48,5120]{3,2,1,0:T(8,128)(2,1)S(1)}, bf16[2,2,48,5120]{3,2,1,0:T(8,128)(2,1)}, u32[]{:S(2)}, u32[]{:S(2)}) collective-permute-start(bf16[2,2,48,5120]{3,2,1,0:T(8,128)(2,1)S(1)} %shard_map.60), channel_id=1, source_target_pairs={{16,32},{48,64},{80,96},{112,128},{144,160},{176,192},{208,224},{3... | collective-permute-start | bytes 5898248 | tf_op jit(solution)/shard_map/ppermute | solution.py:314
  13.9 5.5 %copy-start = (s32[128,2]{0,1:T(2,128)S(1)}, s32[128,2]{0,1:T(2,128)}, u32[]{:S(2)}) copy-start(s32[128,2]{0,1:T(2,128)} %param.5) | copy-start | bytes 3076
  13.9 5.5 %copy-start.1 = (pred[26,1]{0,1:T(4,128)(4,1)S(1)}, pred[26,1]{0,1:T(4,128)(4,1)}, u32[]{:S(2)}) copy-start(pred[26,1]{0,1:T(4,128)(4,1)} %constant.62) | copy-start | bytes 82
  13.9 5.5 %copy-start.2 = (s32[26,1]{0,1:T(1,128)S(1)}, s32[26,1]{0,1:T(1,128)}, u32[]{:S(2)}) copy-start(s32[26,1]{0,1:T(1,128)} %constant.69) | copy-start | bytes 316
  14.0 5.5 %copy-start.3 = (s32[26,1]{0,1:T(1,128)S(1)}, s32[26,1]{0,1:T(1,128)}, u32[]{:S(2)}) copy-start(s32[26,1]{0,1:T(1,128)} %constant.70) | copy-start | bytes 316
  16.4 26.8 %collective-permute-start.2 = (bf16[2,2,32,5120]{3,2,1,0:T(8,128)(2,1)}, bf16[2,2,32,5120]{3,2,1,0:T(8,128)(2,1)S(1)}, u32[]{:S(2)}, u32[]{:S(2)}) collective-permute-start(bf16[2,2,32,5120]{3,2,1,0:T(8,128)(2,1)} %shard_map.63), channel_id=1, source_target_pairs={{16,32},{48,64},{80,96},{112,128},{144,160},{176,192},{208,224},{3... | collective-permute-start | bytes 3932168 | tf_op jit(solution)/shard_map/ppermute | solution.py:314
  34.3 12.7 %collective-permute-start.4 = (f32[1,44,256]{2,1,0:T(8,128)S(1)}, f32[1,44,256]{2,1,0:T(8,128)S(1)}, u32[]{:S(2)}, u32[]{:S(2)}) collective-permute-start(f32[1,44,256]{2,1,0:T(8,128)S(1)} %pad_maximum_fusion.1), channel_id=1, source_target_pairs={{1,0},{2,1},{3,2},{4,3},{5,4},{6,5},{7,6},{8,7},{9,8},{10,9},{11,1... | collective-permute-start | bytes 135176 | tf_op jit(solution)/shard_map/ppermute | solution.py:309
  38.6 8.5 %collective-permute-start.3 = (f32[1,44,256]{2,1,0:T(8,128)S(1)}, f32[1,44,256]{2,1,0:T(8,128)S(1)}, u32[]{:S(2)}, u32[]{:S(2)}) collective-permute-start(f32[1,44,256]{2,1,0:T(8,128)S(1)} %pad_maximum_fusion), channel_id=1, source_target_pairs={{0,1},{1,2},{2,3},{3,4},{4,5},{5,6},{6,7},{7,8},{8,9},{9,10},{10,1... | collective-permute-start | bytes 135176 | tf_op jit(solution)/shard_map/ppermute | solution.py:309
  47.7 5.6 %collective-permute-start.5 = (s16[256,128]{1,0:T(8,128)(2,1)S(1)}, s16[256,128]{1,0:T(8,128)(2,1)S(1)}, u32[]{:S(2)}, u32[]{:S(2)}) collective-permute-start(s16[256,128]{1,0:T(8,128)(2,1)S(1)} %get-tuple-element.20), channel_id=1, source_target_pairs={{16,32},{48,64},{80,96},{112,128},{144,160},{176,192},{208,224},{3... | collective-permute-start | bytes 196616 | tf_op jit(solution)/shard_map/ppermute | solution.py:314
  51.1 2.2 %collective-permute-start.6 = (s16[256,128]{1,0:T(8,128)(2,1)S(1)}, s16[256,128]{1,0:T(8,128)(2,1)S(1)}, u32[]{:S(2)}, u32[]{:S(2)}) collective-permute-start(s16[256,128]{1,0:T(8,128)(2,1)S(1)} %get-tuple-element.21), channel_id=1, source_target_pairs={{0,16},{32,48},{64,80},{96,112},{128,144},{160,176},{192,208},{224... | collective-permute-start | bytes 196616 | tf_op jit(solution)/shard_map/ppermute | solution.py:319
